TPU v7x, 32 devices: a whole 2x2x4 slice. The times are simulated.
32 devices in a mesh: items: 8 (over z, x), seq: 4 (over y, core).
Axes of the slice: x: 2, y: 2, z: 4, core: 2. Of those that a mesh axis runs over, the one named last changes fastest.
Arguments:
- media: bfloat16 [8, 2048, 1536], P('items', 'seq'), may hold values from -6 to 6
- latents: bfloat16 [8, 64, 1536], P('items', 'seq'), may hold values from -6 to 6
- frames: int32 [8], P('items'), may hold values from 1 to 8, as said below
- time_embed: float32 [8, 1536], replicated, may hold values from -4 to 4
- media_gain: float32 [1536], replicated, may hold values from 0.5 to 1.5
- media_bias: float32 [1536], replicated, may hold values from -2 to 2
- latent_gain: float32 [1536], replicated, may hold values from 0.5 to 1.5
- latent_bias: float32 [1536], replicated, may hold values from -2 to 2
- ffn_gain: float32 [1536], replicated, may hold values from 0.5 to 1.5
- ffn_bias: float32 [1536], replicated, may hold values from -2 to 2
- w_query: bfloat16 [1536, 1536], P(('items', 'seq')), may hold values from -0.15625 to 0.15625
- w_key: bfloat16 [1536, 1536], P(('items', 'seq')), may hold values from -0.15625 to 0.15625
- w_value: bfloat16 [1536, 1536], P(('items', 'seq')), may hold values from -0.15625 to 0.15625
- w_out: bfloat16 [1536, 1536], P(('items', 'seq')), may hold values from -2.5 to 2.5
- w_up: bfloat16 [1536, 6144], P(('items', 'seq')), may hold values from -0.15625 to 0.15625
- w_down: bfloat16 [6144, 1536], P(('items', 'seq')), may hold values from -0.078125 to 0.078125
- grad_out: bfloat16 [8, 64, 1536], P('items', 'seq'), may hold values from -6 to 6
Outputs:
- latents_out: bfloat16 [8, 64, 1536], P('items', 'seq')
- latents_grad: bfloat16 [8, 64, 1536], P('items', 'seq')
- media_grad: bfloat16 [8, 2048, 1536], P('items', 'seq')
- time_grad: float32 [8, 1536], replicated
- media_gain_grad: float32 [1536], replicated
- media_bias_grad: float32 [1536], replicated
- latent_gain_grad: float32 [1536], replicated
- latent_bias_grad: float32 [1536], replicated
- ffn_gain_grad: float32 [1536], replicated
- ffn_bias_grad: float32 [1536], replicated
- query_grad: float32 [1536, 1536], P(('items', 'seq'))
- key_grad: float32 [1536, 1536], P(('items', 'seq'))
- value_grad: float32 [1536, 1536], P(('items', 'seq'))
- out_grad: float32 [1536, 1536], P(('items', 'seq'))
- up_grad: float32 [1536, 6144], P(('items', 'seq'))
- down_grad: float32 [6144, 1536], P(('items', 'seq'))
Inputs may be any that keep to these rules, and one draw needn't show every extreme that they name: `frames`: each entry is 1 (an image) or 8 (a clip); both values occur in every draw.
All inputs are finite; a program needn't handle non-finite values.
Results may differ from a plain program's by a relative error of at most 0.012.
Values may be sent and summed in bfloat16 or wider, within the bound.
No kernel may reach another device: no remote copies, remote signals or barrier semaphores. Data moves between devices by JAX's collectives and lax.ppermute only.
A program may use at most 448 MiB of HBM per device.

v0:
```python
import jax
import jax.numpy as jnp
from jax import lax
from jax.sharding import PartitionSpec as P

H = 16
FRAMES = 8
PATCH = 256


def layer_norm(values, gain, bias):
    center = jnp.mean(values, axis=-1, keepdims=True)
    spread = jnp.mean(jnp.square(values - center), axis=-1, keepdims=True)
    return (values - center) * lax.rsqrt(spread + 1e-05) * gain + bias


def raw_scores(query_four, key_four, visible):
    scores = jnp.einsum("bqhd,bkhd->bhqk", query_four, key_four, preferred_element_type=jnp.float32)
    return jnp.where(visible[:, None, None, :], scores, -1e30)


def shards(
    media,
    latents,
    frames,
    time_embed,
    media_gain,
    media_bias,
    latent_gain,
    latent_bias,
    ffn_gain,
    ffn_bias,
    w_query,
    w_key,
    w_value,
    w_out,
    w_up,
    w_down,
    grad_out,
):
    seq_count = lax.axis_size("seq")
    seq_index = lax.axis_index("seq")
    batch_items, media_rows, width = media.shape
    head_size = width // H
    local_heads = H // seq_count
    frames_here = FRAMES // seq_count
    scaling = head_size ** (-0.5)
    weights_full = (
        lax.all_gather(w_query, ("items", "seq"), axis=0, tiled=True),
        lax.all_gather(w_key, ("items", "seq"), axis=0, tiled=True),
        lax.all_gather(w_value, ("items", "seq"), axis=0, tiled=True),
        lax.all_gather(w_out, ("items", "seq"), axis=0, tiled=True),
        lax.all_gather(w_up, ("items", "seq"), axis=0, tiled=True),
        lax.all_gather(w_down, ("items", "seq"), axis=0, tiled=True),
    )
    query_full, key_full, value_full, out_full, up_full, down_full = weights_full
    time_rows = lax.dynamic_slice_in_dim(time_embed, seq_index * frames_here, frames_here, 0)
    shifted = (
        media.astype(jnp.float32).reshape(batch_items, frames_here, PATCH, width)
        + time_rows[None, :, None, :]
    ).reshape(batch_items, media_rows, width)
    media_normed = layer_norm(shifted, media_gain, media_bias).astype(jnp.bfloat16)
    latent_in = latents.astype(jnp.float32)
    latent_normed = layer_norm(latent_in, latent_gain, latent_bias).astype(jnp.bfloat16)
    sources = jnp.concatenate([media_normed, latent_normed], axis=1)
    source_rows = sources.shape[1]
    key_local = jnp.dot(sources, key_full, preferred_element_type=jnp.float32).astype(jnp.bfloat16)
    value_local = jnp.dot(sources, value_full, preferred_element_type=jnp.float32).astype(
        jnp.bfloat16
    )
    query_local = (
        jnp.dot(latent_normed, query_full, preferred_element_type=jnp.float32) * scaling
    ).astype(jnp.bfloat16)
    key_heads, value_heads, query_heads = (
        lax.all_to_all(key_local, "seq", split_axis=2, concat_axis=1, tiled=True),
        lax.all_to_all(value_local, "seq", split_axis=2, concat_axis=1, tiled=True),
        lax.all_to_all(query_local, "seq", split_axis=2, concat_axis=1, tiled=True),
    )
    total_keys = key_heads.shape[1]
    query_count = query_heads.shape[1]
    position = jnp.arange(total_keys, dtype=jnp.int32)
    anchor = position // source_rows
    within = position % source_rows
    frame_pos = (anchor * media_rows + within) // PATCH
    visible = (within >= media_rows)[None, :] | (frame_pos[None, :] < frames[:, None])
    key_four = key_heads.reshape(batch_items, total_keys, local_heads, head_size)
    value_four = value_heads.reshape(batch_items, total_keys, local_heads, head_size)
    query_four = query_heads.reshape(batch_items, query_count, local_heads, head_size)
    scores = raw_scores(query_four, key_four, visible)
    row_max = jnp.max(scores, axis=-1, keepdims=True)
    log_total = row_max + jnp.log(jnp.sum(jnp.exp(scores - row_max), axis=-1, keepdims=True))
    probs_low = jnp.exp(scores - log_total).astype(jnp.bfloat16)
    mixture = jnp.einsum(
        "bhqk,bkhd->bqhd", probs_low, value_four, preferred_element_type=jnp.float32
    )
    mixture = mixture.astype(jnp.bfloat16).reshape(
        batch_items, query_count, local_heads * head_size
    )
    mixed_rows = lax.all_to_all(mixture, "seq", split_axis=1, concat_axis=2, tiled=True)
    attended = jnp.dot(mixed_rows, out_full, preferred_element_type=jnp.float32)
    hidden = latent_in + attended
    ffn_in = layer_norm(hidden, ffn_gain, ffn_bias).astype(jnp.bfloat16)
    pre_act = jnp.dot(ffn_in, up_full, preferred_element_type=jnp.float32)
    active = jax.nn.gelu(pre_act).astype(jnp.bfloat16)
    result = hidden + jnp.dot(active, down_full, preferred_element_type=jnp.float32)
    latents_out = result.astype(jnp.bfloat16)
    query_back, key_back, value_back, out_back, up_back, down_back = weights_full
    upstream = grad_out.astype(jnp.float32)
    active_grad = jnp.einsum("bro,io->bri", grad_out, down_back, preferred_element_type=jnp.float32)
    unused_act, gelu_back = jax.vjp(jax.nn.gelu, pre_act)
    pre_grad = gelu_back(active_grad)[0].astype(jnp.bfloat16)
    ffn_in_grad = jnp.einsum("brf,df->brd", pre_grad, up_back, preferred_element_type=jnp.float32)
    unused_norm, ffn_back = jax.vjp(layer_norm, hidden, ffn_gain, ffn_bias)
    hidden_norm_grad, ffn_gain_grad, ffn_bias_grad = ffn_back(ffn_in_grad)
    hidden_grad = upstream + hidden_norm_grad
    attended_low = hidden_grad.astype(jnp.bfloat16)
    mixture_grad = jnp.einsum(
        "bro,io->bri", attended_low, out_back, preferred_element_type=jnp.float32
    ).astype(jnp.bfloat16)
    mixture_heads_grad = lax.all_to_all(
        mixture_grad, "seq", split_axis=2, concat_axis=1, tiled=True
    )
    grad_four = mixture_heads_grad.reshape(batch_items, query_count, local_heads, head_size)
    probs_again = jnp.exp(raw_scores(query_four, key_four, visible) - log_total)
    prob_grad = jnp.einsum(
        "bqhd,bkhd->bhqk", grad_four, value_four, preferred_element_type=jnp.float32
    )
    inner = jnp.sum(probs_again * prob_grad, axis=-1, keepdims=True)
    score_grad = (probs_again * (prob_grad - inner)).astype(jnp.bfloat16)
    query_head_grad = jnp.einsum(
        "bhqk,bkhd->bqhd", score_grad, key_four, preferred_element_type=jnp.float32
    ).astype(jnp.bfloat16)
    key_head_grad = jnp.einsum(
        "bhqk,bqhd->bkhd", score_grad, query_four, preferred_element_type=jnp.float32
    ).astype(jnp.bfloat16)
    value_head_grad = jnp.einsum(
        "bhqk,bqhd->bkhd",
        probs_again.astype(jnp.bfloat16),
        grad_four,
        preferred_element_type=jnp.float32,
    ).astype(jnp.bfloat16)
    query_head_grad = query_head_grad.reshape(batch_items, query_count, local_heads * head_size)
    key_head_grad = key_head_grad.reshape(batch_items, key_four.shape[1], local_heads * head_size)
    value_head_grad = value_head_grad.reshape(
        batch_items, key_four.shape[1], local_heads * head_size
    )
    key_row_grad, value_row_grad, query_row_grad = (
        lax.all_to_all(key_head_grad, "seq", split_axis=1, concat_axis=2, tiled=True),
        lax.all_to_all(value_head_grad, "seq", split_axis=1, concat_axis=2, tiled=True),
        lax.all_to_all(query_head_grad, "seq", split_axis=1, concat_axis=2, tiled=True),
    )
    source_grad = jnp.einsum(
        "bre,de->brd", key_row_grad, key_back, preferred_element_type=jnp.float32
    )
    source_grad = source_grad + jnp.einsum(
        "bre,de->brd", value_row_grad, value_back, preferred_element_type=jnp.float32
    )
    latent_norm_grad = (
        source_grad[:, media_rows:]
        + jnp.einsum("bre,de->brd", query_row_grad, query_back, preferred_element_type=jnp.float32)
        * scaling
    )
    unused_media, media_back = jax.vjp(layer_norm, shifted, media_gain, media_bias)
    shifted_grad, media_gain_grad, media_bias_grad = media_back(source_grad[:, :media_rows])
    media_grad = shifted_grad.astype(jnp.bfloat16)
    frame_sums = jnp.sum(shifted_grad.reshape(batch_items, frames_here, PATCH, width), axis=(0, 2))
    time_local = lax.dynamic_update_slice_in_dim(
        jnp.zeros((FRAMES, width), jnp.float32), frame_sums, seq_index * frames_here, 0
    )
    unused_latent, latent_back = jax.vjp(layer_norm, latent_in, latent_gain, latent_bias)
    latent_in_grad, latent_gain_grad, latent_bias_grad = latent_back(latent_norm_grad)
    latents_grad = (hidden_grad + latent_in_grad).astype(jnp.bfloat16)
    (
        time_grad,
        media_gain_sum,
        media_bias_sum,
        latent_gain_sum,
        latent_bias_sum,
        ffn_gain_sum,
        ffn_bias_sum,
    ) = lax.psum(
        (
            time_local,
            media_gain_grad,
            media_bias_grad,
            latent_gain_grad,
            latent_bias_grad,
            ffn_gain_grad,
            ffn_bias_grad,
        ),
        ("items", "seq"),
    )
    proj_share = lax.psum_scatter(
        jnp.concatenate(
            [
                jnp.einsum(
                    "brd,bre->de", latent_normed, query_row_grad, preferred_element_type=jnp.float32
                )
                * scaling,
                jnp.einsum(
                    "brd,bre->de", sources, key_row_grad, preferred_element_type=jnp.float32
                ),
                jnp.einsum(
                    "brd,bre->de", sources, value_row_grad, preferred_element_type=jnp.float32
                ),
                jnp.einsum(
                    "brd,bre->de", mixed_rows, attended_low, preferred_element_type=jnp.float32
                ),
                jnp.einsum("brd,brf->df", ffn_in, pre_grad, preferred_element_type=jnp.float32),
            ],
            axis=1,
        ),
        ("items", "seq"),
        scatter_dimension=0,
        tiled=True,
    )
    down_share = lax.psum_scatter(
        jnp.einsum("bri,bro->io", active, grad_out, preferred_element_type=jnp.float32),
        ("items", "seq"),
        scatter_dimension=0,
        tiled=True,
    )
    query_part_sum = proj_share[:, 0:width]
    key_part = proj_share[:, width : 2 * width]
    value_part = proj_share[:, 2 * width : 3 * width]
    out_part = proj_share[:, 3 * width : 4 * width]
    up_part = proj_share[:, 4 * width :]
    return (
        latents_out,
        latents_grad,
        media_grad,
        time_grad,
        media_gain_sum,
        media_bias_sum,
        latent_gain_sum,
        latent_bias_sum,
        ffn_gain_sum,
        ffn_bias_sum,
        query_part_sum,
        key_part,
        value_part,
        out_part,
        up_part,
        down_share,
    )


def solution(mesh):
    return jax.shard_map(
        shards,
        mesh=mesh,
        in_specs=(
            P("items", "seq", None),
            P("items", "seq", None),
            P("items"),
            P(),
            P(),
            P(),
            P(),
            P(),
            P(),
            P(),
            P(("items", "seq"), None),
            P(("items", "seq"), None),
            P(("items", "seq"), None),
            P(("items", "seq"), None),
            P(("items", "seq"), None),
            P(("items", "seq"), None),
            P("items", "seq", None),
        ),
        out_specs=(
            P("items", "seq", None),
            P("items", "seq", None),
            P("items", "seq", None),
            P(),
            P(),
            P(),
            P(),
            P(),
            P(),
            P(),
            P(("items", "seq"), None),
            P(("items", "seq"), None),
            P(("items", "seq"), None),
            P(("items", "seq"), None),
            P(("items", "seq"), None),
            P(("items", "seq"), None),
        ),
        check_vma=False,
    )
```

profile of v0, /device:TPU:0, one launch (start us, length us, event | category | flops | bytes accessed | tf_op | source)
XLA Modules:
  0.0 1890.2 jit_solution(14027897879312206144)
XLA Ops:
  16.2 61.1 %all-gather.9.cloned.1.call-done = bf16[1536,1536]{1,0:T(8,128)(2,1)} async-done(((bf16[48,1536]{1,0:T(8,128)(2,1)}), bf16[1536,1536]{1,0:T(8,128)(2,1)}) %all-gather.9.cloned.1.call-update) | async-done | bytes 4718608 | tf_op jit(solution)/shard_map/all_gather | solution.py:49
  81.4 8.8 reduce.32
  94.7 47.9 %all-gather.7.cloned.1.call-done = bf16[1536,1536]{1,0:T(8,128)(2,1)} async-done(((bf16[48,1536]{1,0:T(8,128)(2,1)}), bf16[1536,1536]{1,0:T(8,128)(2,1)}) %all-gather.7.cloned.1.call-update) | async-done | bytes 4718608 | tf_op jit(solution)/shard_map/all_gather | solution.py:51
  142.6 5.0 fusion.5
  147.6 6.0 copy.85
  153.6 12.7 reduce.30
  166.2 4.2 reshape.623
  170.5 4.5 all-to-all-start
  175.0 38.6 %all-gather.11.cloned.1.call-done = bf16[1536,1536]{1,0:T(8,128)(2,1)} async-done(((bf16[48,1536]{1,0:T(8,128)(2,1)}), bf16[1536,1536]{1,0:T(8,128)(2,1)}) %all-gather.11.cloned.1.call-update) | async-done | bytes 4718608 | tf_op jit(solution)/shard_map/all_gather | solution.py:50
  213.6 5.0 fusion.6
  218.6 6.0 copy.91
  224.5 12.7 reduce.31
  237.2 4.2 reshape.625
  241.4 4.6 all-to-all-start.2
  247.9 5.5 reshape.624
  258.7 4.2 copy.87
  265.4 7.2 all-to-all-done.2
  272.6 5.5 reshape.626
  283.5 4.2 copy.93
  294.8 6.9 all_to_all.120
  305.2 104.0 %all-gather.15.cloned.1.call-done = bf16[1536,6144]{1,0:T(8,128)(2,1)} async-done(((bf16[48,6144]{1,0:T(8,128)(2,1)}), bf16[1536,6144]{1,0:T(8,128)(2,1)}) %all-gather.15.cloned.1.call-update) | async-done | bytes 18874384 | tf_op jit(solution)/shard_map/all_gather | solution.py:53
  409.2 7.7 fusion.81
  417.0 117.9 %all-gather.17.cloned.1.call-done = bf16[6144,1536]{1,0:T(8,128)(2,1)} async-done(((bf16[192,1536]{1,0:T(8,128)(2,1)}), bf16[6144,1536]{1,0:T(8,128)(2,1)}) %all-gather.17.cloned.1.call-update) | async-done | bytes 18874384 | tf_op jit(solution)/shard_map/all_gather | solution.py:54
  534.9 11.4 fusion.24
  546.3 9.6 fusion.43
  561.7 9.6 reduce.34
  572.7 6.7 all_to_all.121
  597.6 8.7 copy.103
  606.3 14.4 reduce.36
  624.5 4.4 all-to-all-start.5
  630.7 8.6 copy.106
  639.3 13.4 reduce.37
  657.4 4.4 all-to-all-start.6
  661.9 5.1 convolution_multiply_fusion
  666.9 9.8 copy.111
  676.7 8.1 constant_dynamic-update-slice_fusion
  695.3 6.3 convolution_dynamic-update-slice_fusion.3
  701.7 6.4 convolution_dynamic-update-slice_fusion.2
  708.0 5.0 convolution_dynamic-update-slice_fusion.1
  713.1 14.9 convolution_dynamic-update-slice_fusion
  728.0 5.0 fusion.88
  733.1 4.8 add_bitcast_fusion
  749.3 5.8 fusion.40
  755.1 22.2 %fusion.55 = f32[6144,1536]{1,0:T(8,128)} fusion(bf16[1,16,1536]{2,1,0:T(8,128)(2,1)} %param.33, f32[16,6144]{1,0:T(8,128)} %copy-done.8), kind=kOutput, calls=%fused_computation.98 | convolution fusion | flops 302874624 | bytes 38191104 | tf_op jit(solution)/shard_map/bri,bro->io/dot_general | solution.py:218
  778.4 12.6 fusion.11
  791.9 592.4 %reduce-scatter.3.cloned.1.call-done = f32[48,12288]{1,0:T(8,128)} async-done(((f32[1536,12288]{1,0:T(8,128)}), f32[48,12288]{1,0:T(8,128)}) %reduce-scatter.3.cloned.1.call-update) | async-done | bytes 2359312 | tf_op jit(solution)/shard_map/reduce_scatter | solution.py:193
  1387.9 128.1 %all-reduce.3.cloned.1.call-done = (f32[8,1536]{1,0:T(8,128)}, f32[1536]{0:T(1024)}, f32[1536]{0:T(1024)}, f32[1536]{0:T(1024)}, f32[1536]{0:T(1024)}, /*index=5*/f32[1536]{0:T(1024)}, f32[1536]{0:T(1024)}) async-done(((f32[8,1536]{1,0:T(8,128)}, f32[1536]{0:T(1024)}, f32[1536]{0:T(1024)}, f32[1536]{0:T(1024)}, f32[1536]{0:T(1024)}, /*index=5*/f32[1536]{0:T(1024)}, f32[1536]{0:T(1024)}), ...) | async-done | bytes 86032 | tf_op jit(solution)/shard_map/psum | solution.py:181
  1516.0 358.0 %reduce-scatter.5.cloned.1.call-done = f32[192,1536]{1,0:T(8,128)} async-done(((f32[6144,1536]{1,0:T(8,128)}), f32[192,1536]{1,0:T(8,128)}) %reduce-scatter.5.cloned.1.call-update) | async-done | bytes 1179664 | tf_op jit(solution)/shard_map/reduce_scatter | solution.py:217
  (247 shorter events, 114.6 us)
Async XLA Ops:
  7.2 5.9 copy-start
  7.2 6.4 copy-start.4
  7.2 70.1 %all-gather.9.cloned.1.call-start = ((), (), s32[]{:S(2)}) async-start(), calls=%async_computation.11 | async-start | bytes 4866048 | tf_op jit(solution)/shard_map/all_gather | solution.py:49
  7.9 134.7 %all-gather.7.cloned.1.call-start = ((), (), s32[]{:S(2)}) async-start(), calls=%async_computation.10 | async-start | bytes 4866048 | tf_op jit(solution)/shard_map/all_gather | solution.py:51
  8.7 204.9 %all-gather.11.cloned.1.call-start = ((), (), s32[]{:S(2)}) async-start(), calls=%async_computation.12 | async-start | bytes 4866048 | tf_op jit(solution)/shard_map/all_gather | solution.py:50
  9.4 292.3 %all-gather.13.cloned.1.call-start = ((), (), s32[]{:S(2)}) async-start(), calls=%async_computation.13 | async-start | bytes 4866048 | tf_op jit(solution)/shard_map/all_gather | solution.py:52
  10.0 399.2 %all-gather.15.cloned.1.call-start = ((), (), s32[]{:S(2)}) async-start(), calls=%async_computation.14 | async-start | bytes 19464192 | tf_op jit(solution)/shard_map/all_gather | solution.py:53
  10.6 524.3 %all-gather.17.cloned.1.call-start = ((), (), s32[]{:S(2)}) async-start(), calls=%async_computation.15 | async-start | bytes 19464192 | tf_op jit(solution)/shard_map/all_gather | solution.py:54
  15.4 198.2 %copy-start.25 = (bf16[1,16,1536]{2,1,0:T(8,128)(2,1)}, bf16[1,16,1536]{2,1,0:T(8,128)(2,1)S(1)}, u32[]{:S(2)}) copy-start(bf16[1,16,1536]{2,1,0:T(8,128)(2,1)S(1)} %fusion.39) | copy-start | bytes 147460
  16.2 126.4 %copy-start.19 = (bf16[1,512,1536]{2,1,0:T(8,128)(2,1)}, bf16[1,512,1536]{2,1,0:T(8,128)(2,1)S(1)}, u32[]{:S(2)}) copy-start(bf16[1,512,1536]{2,1,0:T(8,128)(2,1)S(1)} %add_convert_fusion) | copy-start | bytes 4718596
  91.2 79.2 %all-to-all-start.1 = ((bf16[4,2,3072]{2,1,0:T(2,128)(2,1)}), bf16[4,2,3072]{2,1,0:T(2,128)(2,1)S(1)}, u32[]{:S(2)}, u32[]{:S(2)}) async-start(bf16[4,2,3072]{2,1,0:T(2,128)(2,1)} %reshape.627), calls=%async_computation.1 | async-start | bytes 98304 | tf_op jit(solution)/shard_map/all_to_all | solution.py:77
  170.5 43.1 %copy-start.20 = (bf16[1,512,1536]{2,1,0:T(8,128)(2,1)S(1)}, bf16[1,512,1536]{2,1,0:T(8,128)(2,1)}, u32[]{:S(2)}) copy-start(bf16[1,512,1536]{2,1,0:T(8,128)(2,1)} %copy-done.19) | copy-start | bytes 4718596
  170.5 70.9 %all-to-all-start = ((bf16[4,2,101376]{2,1,0:T(2,128)(2,1)}), bf16[4,2,101376]{2,1,0:T(2,128)(2,1)}, u32[]{:S(2)}, u32[]{:S(2)}) async-start(bf16[4,2,101376]{2,1,0:T(2,128)(2,1)} %reshape.623), calls=%async_computation | async-start | bytes 3244032 | tf_op jit(solution)/shard_map/all_to_all | solution.py:76
  241.4 31.2 %all-to-all-start.2 = ((bf16[4,2,101376]{2,1,0:T(2,128)(2,1)}), bf16[4,2,101376]{2,1,0:T(2,128)(2,1)}, u32[]{:S(2)}, u32[]{:S(2)}) async-start(bf16[4,2,101376]{2,1,0:T(2,128)(2,1)} %reshape.625), calls=%async_computation.2 | async-start | bytes 3244032 | tf_op jit(solution)/shard_map/all_to_all | solution.py:75
  247.8 42.3 %copy-start.24 = (bf16[64,4,96]{2,1,0:T(4,128)(2,1)}, bf16[64,4,96]{2,1,0:T(4,128)(2,1)S(1)}, u32[]{:S(2)}) copy-start(bf16[64,4,96]{2,1,0:T(4,128)(2,1)S(1)} %reshape.604) | copy-start | bytes 147460
  292.7 287.8 %copy-start.40 = (f32[4,64]{1,0:T(4,128)}, f32[4,64]{1,0:T(4,128)S(1)}, u32[]{:S(2)}) copy-start(f32[4,64]{1,0:T(4,128)S(1)} %log_add_fusion) | copy-start | bytes 3076
  293.6 115.6 %copy-start.31 = (f32[1536]{0:T(1024)S(1)}, f32[1536]{0:T(1024)}, u32[]{:S(2)}) copy-start(f32[1536]{0:T(1024)} %param.25) | copy-start | bytes 18436
  293.6 115.6 %copy-start.33 = (f32[1536]{0:T(1024)S(1)}, f32[1536]{0:T(1024)}, u32[]{:S(2)}) copy-start(f32[1536]{0:T(1024)} %param.26) | copy-start | bytes 18436
  304.9 251.8 %copy-start.42 = (f32[16]{0:T(128)}, f32[16]{0:T(128)S(1)}, u32[]{:S(2)}) copy-start(f32[16]{0:T(128)S(1)} %broadcast_multiply_fusion.1) | copy-start | bytes 196
  305.2 251.6 %copy-start.44 = (f32[16]{0:T(128)}, f32[16]{0:T(128)S(1)}, u32[]{:S(2)}) copy-start(f32[16]{0:T(128)S(1)} %fusion.79) | copy-start | bytes 196
  305.2 229.7 %copy-start.30 = (bf16[1,16,1536]{2,1,0:T(8,128)(2,1)S(1)}, bf16[1,16,1536]{2,1,0:T(8,128)(2,1)}, u32[]{:S(2)}) copy-start(bf16[1,16,1536]{2,1,0:T(8,128)(2,1)} %param.33) | copy-start | bytes 147460
  417.0 129.3 %copy-start.8 = (f32[16,6144]{1,0:T(8,128)}, f32[16,6144]{1,0:T(8,128)S(1)}, u32[]{:S(2)}) copy-start(f32[16,6144]{1,0:T(8,128)S(1)} %fusion.81) | copy-start | bytes 1179652
  546.2 9.6 copy-start.12
  591.0 33.5 %all-to-all-start.7 = ((bf16[4,2,3072]{2,1,0:T(2,128)(2,1)}), bf16[4,2,3072]{2,1,0:T(2,128)(2,1)}, u32[]{:S(2)}, u32[]{:S(2)}) async-start(bf16[4,2,3072]{2,1,0:T(2,128)(2,1)} %reshape.633), calls=%async_computation.7 | async-start | bytes 98304 | tf_op jit(solution)/shard_map/all_to_all | solution.py:150
  620.7 8.2 copy-start.23
  620.7 8.2 copy-start.41
  624.5 32.9 %all-to-all-start.5 = ((bf16[4,2,101376]{2,1,0:T(2,128)(2,1)}), bf16[4,2,101376]{2,1,0:T(2,128)(2,1)}, u32[]{:S(2)}, u32[]{:S(2)}) async-start(bf16[4,2,101376]{2,1,0:T(2,128)(2,1)} %reshape.635), calls=%async_computation.5 | async-start | bytes 3244032 | tf_op jit(solution)/shard_map/all_to_all | solution.py:148
  652.7 9.2 copy-start.26
  657.4 9.5 copy-start.28
  657.4 32.8 %all-to-all-start.6 = ((bf16[4,2,101376]{2,1,0:T(2,128)(2,1)}), bf16[4,2,101376]{2,1,0:T(2,128)(2,1)}, u32[]{:S(2)}, u32[]{:S(2)}) async-start(bf16[4,2,101376]{2,1,0:T(2,128)(2,1)} %reshape.637), calls=%async_computation.6 | async-start | bytes 3244032 | tf_op jit(solution)/shard_map/all_to_all | solution.py:149
  661.8 722.6 %reduce-scatter.3.cloned.1.call-start = ((), (), s32[]{:S(2)}) async-start(), calls=%async_computation.16 | async-start | bytes 77856768 | tf_op jit(solution)/shard_map/reduce_scatter | solution.py:193
  694.3 7.3 copy-start.15
  695.3 6.3 copy-start.27
  701.6 6.4 copy-start.18
  708.0 5.1 copy-start.13
  708.0 5.1 copy-start.43
  708.0 5.1 copy-start.45
  728.0 788.0 %all-reduce.3.cloned.1.call-start = ((), (), s32[]{:S(2)}) async-start(), calls=%async_computation.18 | async-start | bytes 196608 | tf_op jit(solution)/shard_map/psum | solution.py:181
  744.1 5.2 copy-start.29
  744.1 5.2 copy-start.35
  744.1 5.2 copy-start.51
  744.1 5.2 copy-start.55
  755.1 1118.9 %reduce-scatter.5.cloned.1.call-start = ((), (), s32[]{:S(2)}) async-start(), calls=%async_computation.17 | async-start | bytes 38928384 | tf_op jit(solution)/shard_map/reduce_scatter | solution.py:217
  778.4 12.6 copy-start.57
  778.4 12.6 copy-start.59
  778.4 12.8 copy-start.58
  778.4 12.8 copy-start.32
  778.4 1104.8 %copy-start.1 = (f32[8,1536]{1,0:T(8,128)S(1)}, f32[8,1536]{1,0:T(8,128)}, u32[]{:S(2)}) copy-start(f32[8,1536]{1,0:T(8,128)} %param.20) | copy-start | bytes 147460
  (27 other events, 63.3 us)
Sparse Core Ops, SparseCore 0:
  11.0 66.2 all-gather.8
  80.2 62.3 all-gather.6
  145.5 67.9 all-gather.10
  216.3 66.4 all-gather.12
  285.6 123.5 all-gather.14
  412.0 122.8 all-gather.16
  728.1 656.2 reduce-scatter.2
  1393.1 122.8 all-reduce.2
  1524.1 349.8 reduce-scatter.4
where the time goes:
time: 1900 us; the launch traced here: 1890 us
  waiting for transfers between devices  1460 us (77%)
  matrix products  147 us (8%)
  local copies, waits for them, and re-layouts  137 us (7%)
  other arithmetic  91.9 us (5%)
  starting transfers between devices  25.5 us (1%)
    reduce_scatter x1, waiting for transfers between devices, shards(): lax.psum_scatter(jnp.concatenate([jnp.einsum('brd,bre->de', latent_normed...  592 us
    reduce_scatter x1, waiting for transfers between devices, shards(): lax.psum_scatter(jnp.einsum('bri,bro->io', active, grad_out, preferred_el...  358 us
    psum x1, waiting for transfers between devices, shards(): lax.psum((time_local, media_gain_grad, media_bias_grad, latent_gain_grad,...  128 us
    all_gather x1, waiting for transfers between devices, shards(): lax.all_gather(w_down, ('items', 'seq'), axis=0, tiled=True)  118 us
    all_gather x1, waiting for transfers between devices, shards(): lax.all_gather(w_up, ('items', 'seq'), axis=0, tiled=True)  104 us
    unnamed x8, other arithmetic  74.8 us
    unnamed x155, local copies, waits for them, and re-layouts  67.4 us
    all_gather x1, waiting for transfers between devices, shards(): lax.all_gather(w_query, ('items', 'seq'), axis=0, tiled=True)  61.1 us
  transfers between devices with their start and end apart: 15, of which 9 were waited for; matrix products, arithmetic and copies ran while one was open for 15% of the time, Pallas kernels for 0%

commit v1 on v0

v1 whole, which is shorter than its diff:
```python
import jax
import jax.numpy as jnp
from jax import lax
from jax.experimental import pallas as pl
from jax.experimental.pallas import tpu as pltpu
from jax.sharding import PartitionSpec as P

H = 16
FRAMES = 8
PATCH = 256
AXES = ("items", "seq")
BF = jnp.bfloat16
F32 = jnp.float32


def layer_norm(values, gain, bias):
    center = jnp.mean(values, axis=-1, keepdims=True)
    spread = jnp.mean(jnp.square(values - center), axis=-1, keepdims=True)
    rstd = lax.rsqrt(spread + 1e-05)
    unit = (values - center) * rstd
    return unit * gain + bias, unit, rstd


def layer_norm_back(grad, unit, rstd, gain):
    scaled = grad * gain
    inner = scaled - jnp.mean(scaled, axis=-1, keepdims=True)
    inner = inner - unit * jnp.mean(scaled * unit, axis=-1, keepdims=True)
    return inner * rstd, jnp.sum(grad * unit, axis=0), jnp.sum(grad, axis=0)


def dot(a, b, dims=((1,), (0,))):
    return lax.dot_general(a, b, (dims, ((), ())), preferred_element_type=F32)


def trade(x, mask, count):
    return lax.ppermute(x, AXES, [(i, i ^ mask) for i in range(count)])


def gather_rel(x, order, count):
    x = x[None]
    for mask in order:
        x = jnp.concatenate([x, trade(x, mask, count)], axis=0)
    return x


def scatter_rel(x, order, count):
    for mask in reversed(order):
        half = x.shape[0] // 2
        x = x[:half].astype(F32) + trade(x[half:].astype(BF), mask, count).astype(F32)
    return x[0]


def gather_abs(x, order, count, me):
    done = []
    for mask in order:
        other = trade(x, mask, count)
        axis = sum(m > mask for m in done)
        mine, other = jnp.expand_dims(x, axis), jnp.expand_dims(other, axis)
        x = jnp.where(
            (me & mask) != 0,
            jnp.concatenate([other, mine], axis),
            jnp.concatenate([mine, other], axis),
        )
        done.append(mask)
    return x.reshape(-1, x.shape[-1])


def scatter_abs(x, order, count, me):
    steps = len(order)
    x = x.reshape((2,) * steps + (x.shape[0] // count, x.shape[1]))
    left = sorted(order, reverse=True)
    for mask in order:
        axis = left.index(mask)
        left.remove(mask)
        bit = ((me & mask) != 0).astype(jnp.int32)
        keep = lax.dynamic_index_in_dim(x, bit, axis, keepdims=False)
        send = lax.dynamic_index_in_dim(x, 1 - bit, axis, keepdims=False)
        x = keep.astype(F32) + trade(send.astype(BF), mask, count).astype(F32)
    return x


def sum_all(x, order, count):
    for mask in order:
        x = x + trade(x, mask, count)
    return x


def share_seq(x, seq_count, count):
    return jnp.concatenate([x] + [trade(x, m, count) for m in range(1, seq_count)], axis=0)


def windows(width):
    size = width // H
    for pair in range(H // 2):
        base = (pair // 2) * 4 * size + (pair % 2) * 128
        yield pair, base, (2 * pair * size - base, (2 * pair + 1) * size - base, (2 * pair + 2) * size - base)


def stacked(rows, edges):
    column = lax.broadcasted_iota(jnp.int32, rows.shape, 1)
    first = (column >= edges[0]) & (column < edges[1])
    second = (column >= edges[1]) & (column < edges[2])
    zero = jnp.zeros_like(rows)
    return jnp.concatenate([jnp.where(first, rows, zero), jnp.where(second, rows, zero)], axis=0)


def unstacked(both, edges):
    count = both.shape[0] // 2
    column = lax.broadcasted_iota(jnp.int32, (count, both.shape[1]), 1)
    first = (column >= edges[0]) & (column < edges[1])
    second = (column >= edges[1]) & (column < edges[2])
    return jnp.where(first, both[:count], jnp.where(second, both[count:], 0.0))


def masked_scores(seen, queries, keys, media_rows):
    scores = dot(queries, keys, ((1,), (1,)))
    place = lax.broadcasted_iota(jnp.int32, scores.shape, 1)
    return jnp.where((place < seen) | (place >= media_rows), scores, -1e30)


def attend_kernel(media_rows, seen_ref, q_ref, k_ref, v_ref, out_ref, stat_ref):
    count, width = q_ref.shape
    seen = seen_ref[0]
    lane = lax.broadcasted_iota(jnp.int32, (count, 128), 1)
    stats = jnp.zeros((count, 128), F32)
    carry = None
    for pair, base, edges in windows(width):
        cols = slice(base, base + 256)
        scores = masked_scores(seen, stacked(q_ref[:, cols], edges), k_ref[:, cols], media_rows)
        top = jnp.max(scores, axis=1, keepdims=True)
        probs = jnp.exp(scores - top)
        total = jnp.sum(probs, axis=1, keepdims=True)
        mixed = unstacked(dot(probs.astype(BF), v_ref[:, cols]), edges)
        if pair % 2 == 0:
            out_ref[:, base : base + 128] = mixed[:, :128]
            carry = mixed[:, 128:]
        else:
            out_ref[:, base : base + 128] = carry + mixed[:, :128]
            out_ref[:, base + 128 : base + 256] = mixed[:, 128:]
        for k in range(2):
            rows = slice(k * count, (k + 1) * count)
            stats = jnp.where(lane == 2 * pair + k, top[rows], stats)
            stats = jnp.where(lane == H + 2 * pair + k, total[rows], stats)
    stat_ref[...] = stats


def attend_back_kernel(
    media_rows, seen_ref, q_ref, g_ref, stat_ref, k_ref, v_ref, dq_ref, dk_ref, dv_ref
):
    count, width = q_ref.shape
    seen = seen_ref[0]
    lane = lax.broadcasted_iota(jnp.int32, (count, 128), 1)
    stats = stat_ref[...]

    def column(at):
        parts = [
            jnp.sum(jnp.where(lane == at + k, stats, 0.0), axis=1, keepdims=True) for k in range(2)
        ]
        return jnp.concatenate(parts, axis=0)

    carry = None
    for pair, base, edges in windows(width):
        cols = slice(base, base + 256)
        queries, grads = stacked(q_ref[:, cols], edges), stacked(g_ref[:, cols], edges)
        keys, values = k_ref[:, cols], v_ref[:, cols]
        scores = masked_scores(seen, queries, keys, media_rows)
        probs = jnp.exp(scores - column(2 * pair))
        prob_grad = dot(grads, values, ((1,), (1,)))
        score_grad = (probs * (prob_grad - column(H + 2 * pair))).astype(BF)
        dq = unstacked(dot(score_grad, keys), edges)
        dk = dot(score_grad, queries, ((0,), (0,)))
        dv = dot(probs.astype(BF), grads, ((0,), (0,)))
        if pair % 2 == 0:
            dq_ref[:, base : base + 128] = dq[:, :128]
            dk_ref[:, base : base + 128] = dk[:, :128].astype(BF)
            dv_ref[:, base : base + 128] = dv[:, :128].astype(BF)
            carry = (dq[:, 128:], dk[:, 128:], dv[:, 128:])
        else:
            for ref, full, old in zip((dq_ref, dk_ref, dv_ref), (dq, dk, dv), carry):
                ref[:, base : base + 128] = (old + full[:, :128]).astype(ref.dtype)
                ref[:, base + 128 : base + 256] = full[:, 128:].astype(ref.dtype)


def call(kernel, inputs, outputs, flops):
    smem = pl.BlockSpec(memory_space=pltpu.SMEM)
    vmem = pl.BlockSpec(memory_space=pltpu.VMEM)
    nbytes = sum(x.size * x.dtype.itemsize for x in inputs)
    nbytes += sum(x.size * x.dtype.itemsize for x in outputs)
    return pl.pallas_call(
        kernel,
        out_shape=tuple(outputs),
        in_specs=[smem] + [vmem] * (len(inputs) - 1),
        out_specs=tuple(vmem for _ in outputs),
        compiler_params=pltpu.CompilerParams(vmem_limit_bytes=40 << 20),
        cost_estimate=pl.CostEstimate(flops=flops, bytes_accessed=nbytes, transcendentals=0),
    )(*inputs)


def shards(
    media,
    latents,
    frames,
    time_embed,
    media_gain,
    media_bias,
    latent_gain,
    latent_bias,
    ffn_gain,
    ffn_bias,
    w_query,
    w_key,
    w_value,
    w_out,
    w_up,
    w_down,
    grad_out,
):
    item_count, seq_count = lax.axis_size("items"), lax.axis_size("seq")
    count = item_count * seq_count
    seq_index = lax.axis_index("seq")
    me = lax.axis_index("items") * seq_count + seq_index
    unused_items, media_rows, width = media.shape
    latent_rows = latents.shape[1]
    head_size = width // H
    frames_here = media_rows // PATCH
    scaling = head_size ** (-0.5)

    item_bits = [m for m in (1 << k for k in reversed(range(30))) if seq_count <= m < count]
    seq_bits = [m for m in (1 << k for k in reversed(range(30))) if m < seq_count]
    order_a = item_bits + seq_bits
    order_b = item_bits[:-1] + seq_bits[:-1] + item_bits[-1:] + seq_bits[-1:]
    orders = (order_a, order_b)

    def gather_rows(x):
        half = x.shape[0] // 2
        return jnp.concatenate(
            [
                gather_rel(part, order, count).reshape(-1, x.shape[1])
                for part, order in zip((x[:half], x[half:]), orders)
            ],
            axis=0,
        )

    def scatter_rows(x):
        half = x.shape[0] // 2
        return jnp.concatenate(
            [
                scatter_rel(part.reshape(count, -1, x.shape[1]), order, count)
                for part, order in zip((x[:half], x[half:]), orders)
            ],
            axis=0,
        )

    key_full = gather_abs(w_key, order_a, count, me)
    query_full = gather_abs(w_query, order_b, count, me)
    value_full = gather_abs(w_value, order_a, count, me)
    out_full = gather_abs(w_out, order_b, count, me)

    time_rows = lax.dynamic_slice_in_dim(time_embed, seq_index * frames_here, frames_here, 0)
    shifted = (
        media[0].astype(F32).reshape(frames_here, PATCH, width) + time_rows[:, None, :]
    ).reshape(media_rows, width)
    media_normed, media_unit, media_rstd = layer_norm(shifted, media_gain, media_bias)
    latent_in = latents[0].astype(F32)
    latent_normed, latent_unit, latent_rstd = layer_norm(latent_in, latent_gain, latent_bias)
    latent_normed = latent_normed.astype(BF)
    sources = jnp.concatenate([media_normed.astype(BF), latent_normed], axis=0)

    queries = share_seq(
        (dot(latent_normed, query_full) * scaling).astype(BF), seq_count, count
    )
    keys = dot(sources, key_full).astype(BF)
    values = dot(sources, value_full).astype(BF)
    seen = jnp.clip((frames - seq_index * frames_here) * PATCH, 0, media_rows).astype(jnp.int32)
    all_rows = queries.shape[0]
    pair_flops = 2 * H // 2 * 2 * all_rows * 256 * sources.shape[0]
    mixed, stats = call(
        lambda *refs: attend_kernel(media_rows, *refs),
        (seen, queries, keys, values),
        (jax.ShapeDtypeStruct((all_rows, width), F32), jax.ShapeDtypeStruct((all_rows, 128), F32)),
        2 * pair_flops,
    )

    def own_parts(x):
        blocks = x.reshape(seq_count, latent_rows, x.shape[1])
        return jnp.stack([blocks[0]] + [trade(blocks[m], m, count) for m in range(1, seq_count)])

    mixed_parts, stat_parts = own_parts(mixed), own_parts(stats)
    tops, totals = stat_parts[:, :, :H], stat_parts[:, :, H : 2 * H]
    top = jnp.max(tops, axis=0)
    weights = jnp.exp(tops - top)
    total = jnp.sum(weights * totals, axis=0)
    weights = weights / total
    log_total = top + jnp.log(total)
    mixture_wide = jnp.sum(
        mixed_parts.reshape(seq_count, latent_rows, H, head_size) * weights[..., None], axis=0
    ).reshape(latent_rows, width)
    mixture = mixture_wide.astype(BF)

    hidden = latent_in + dot(mixture, out_full)
    ffn_in, ffn_unit, ffn_rstd = layer_norm(hidden, ffn_gain, ffn_bias)
    ffn_in = ffn_in.astype(BF)

    up_mine = lax.all_to_all(w_up, AXES, split_axis=1, concat_axis=0, tiled=True)
    grad_rows = gather_rows(grad_out[0])
    ffn_rows = gather_rows(ffn_in)
    pre_act = dot(ffn_rows, up_mine)
    active, gelu_back = jax.vjp(jax.nn.gelu, pre_act)
    active = active.astype(BF)
    active_grad = dot(grad_rows, w_down, ((1,), (1,)))
    pre_grad = gelu_back(active_grad)[0].astype(BF)
    ffn_in_grad = scatter_rows(dot(pre_grad, up_mine, ((1,), (1,))))
    latents_out = hidden + scatter_rows(dot(active, w_down))
    down_grad = dot(active, grad_rows, ((0,), (0,)))
    up_grad_mine = dot(ffn_rows, pre_grad, ((0,), (0,))).astype(BF)
    up_grad = lax.all_to_all(up_grad_mine, AXES, split_axis=0, concat_axis=1, tiled=True)

    hidden_norm_grad, ffn_gain_grad, ffn_bias_grad = layer_norm_back(
        ffn_in_grad, ffn_unit, ffn_rstd, ffn_gain
    )
    hidden_grad = grad_out[0].astype(F32) + hidden_norm_grad
    attended_low = hidden_grad.astype(BF)
    mixture_grad = dot(attended_low, out_full, ((1,), (1,))).astype(BF)
    inner = jnp.sum(
        (mixture_wide * mixture_grad.astype(F32)).reshape(latent_rows, H, head_size), axis=-1
    )
    back_stats = jnp.concatenate(
        [log_total, inner, jnp.zeros((latent_rows, 128 - 2 * H), F32)], axis=1
    )
    query_part, key_row_grad, value_row_grad = call(
        lambda *refs: attend_back_kernel(media_rows, *refs),
        (
            seen,
            queries,
            share_seq(mixture_grad, seq_count, count),
            share_seq(back_stats, seq_count, count),
            keys,
            values,
        ),
        (
            jax.ShapeDtypeStruct((all_rows, width), F32),
            jax.ShapeDtypeStruct(keys.shape, BF),
            jax.ShapeDtypeStruct(keys.shape, BF),
        ),
        5 * pair_flops,
    )
    query_row_grad = jnp.sum(own_parts(query_part), axis=0).astype(BF)

    value_grad = scatter_abs(
        dot(sources, value_row_grad, ((0,), (0,))), order_a[::-1], count, me
    )
    key_grad = scatter_abs(dot(sources, key_row_grad, ((0,), (0,))), order_b[::-1], count, me)
    share = width // count

    def my_columns(x):
        return lax.dynamic_slice_in_dim(x, me * share, share, 1)

    out_grad = dot(my_columns(gather_rows(mixture)), gather_rows(attended_low), ((0,), (0,)))
    query_grad = scaling * dot(
        my_columns(gather_rows(latent_normed)), gather_rows(query_row_grad), ((0,), (0,))
    )

    source_grad = dot(key_row_grad, key_full, ((1,), (1,))) + dot(
        value_row_grad, value_full, ((1,), (1,))
    )
    latent_norm_grad = (
        source_grad[media_rows:] + dot(query_row_grad, query_full, ((1,), (1,))) * scaling
    )
    shifted_grad, media_gain_grad, media_bias_grad = layer_norm_back(
        source_grad[:media_rows], media_unit, media_rstd, media_gain
    )
    frame_sums = jnp.sum(shifted_grad.reshape(frames_here, PATCH, width), axis=1)
    time_local = lax.dynamic_update_slice_in_dim(
        jnp.zeros((FRAMES, width), F32), frame_sums, seq_index * frames_here, 0
    )
    latent_in_grad, latent_gain_grad, latent_bias_grad = layer_norm_back(
        latent_norm_grad, latent_unit, latent_rstd, latent_gain
    )
    latents_grad = hidden_grad + latent_in_grad
    sums = jnp.concatenate(
        [
            time_local,
            jnp.stack(
                [
                    media_gain_grad,
                    media_bias_grad,
                    latent_gain_grad,
                    latent_bias_grad,
                    ffn_gain_grad,
                    ffn_bias_grad,
                    jnp.zeros((width,), F32),
                    jnp.zeros((width,), F32),
                ]
            ),
        ],
        axis=0,
    )
    sums = sum_all(sums, order_a, count)
    return (
        latents_out.astype(BF)[None],
        latents_grad.astype(BF)[None],
        shifted_grad.astype(BF)[None],
        sums[:FRAMES],
        sums[FRAMES],
        sums[FRAMES + 1],
        sums[FRAMES + 2],
        sums[FRAMES + 3],
        sums[FRAMES + 4],
        sums[FRAMES + 5],
        query_grad,
        key_grad,
        value_grad,
        out_grad,
        up_grad.astype(F32),
        down_grad,
    )


def solution(mesh):
    rows, split = P("items", "seq", None), P(AXES, None)
    return jax.shard_map(
        shards,
        mesh=mesh,
        in_specs=(rows, rows, P("items")) + (P(),) * 7 + (split,) * 6 + (rows,),
        out_specs=(rows,) * 3 + (P(),) * 7 + (split,) * 6,
        check_vma=False,
    )
```

time: 1900 us -> 544 us (0.29)
  waiting for transfers between devices: 1460 us -> 232 us
  starting transfers between devices: 25.5 us -> 134 us
  matrix products: 147 us -> 50.9 us
  local copies, waits for them, and re-layouts: 137 us -> 62.8 us
  other arithmetic: 91.9 us -> 42.4 us
    reduce_scatter x2 -> x0, waiting for transfers between devices: 950 us -> none  [the longest x1 592 us: shards(): lax.psum_scatter(jnp.concatenate([jnp.einsum('brd,bre->de', latent_normed...]
    all_gather x6 -> x0, waiting for transfers between devices: 369 us -> none  [the longest x1 118 us: shards(): lax.all_gather(w_down, ('items', 'seq'), axis=0, tiled=True)]
    ppermute x0 -> x133, waiting for transfers between devices: none -> 232 us  [trade(): return lax.ppermute(x, AXES, [(i, i ^ mask) for i in range(count)])]
    psum x1 -> x0, waiting for transfers between devices: 128 us -> none  [shards(): lax.psum((time_local, media_gain_grad, media_bias_grad, latent_gain_grad,...]
    ppermute x0 -> x133, starting transfers between devices: none -> 124 us  [trade(): return lax.ppermute(x, AXES, [(i, i ^ mask) for i in range(count)])]
    dot_general x24 -> x18, matrix products: 147 us -> 50.9 us  [dot(): return lax.dot_general(a, b, (dims, ((), ())), preferred_element_type=F32)]
    unnamed x8 -> x4, other arithmetic: 74.8 us -> 0.01 us
    unnamed x155 -> x250, local copies, waits for them, and re-layouts: 67.4 us -> 29.9 us
  transfers between devices with their start and end apart: 15 -> 135, of which waited for: 9 -> 55; matrix products, arithmetic and copies ran while one was open for 15% -> 26% of each run, Pallas kernels for 0% -> 1%
where the time goes in v1:
time: 544 us; the launch traced here: 533 us
  waiting for transfers between devices  232 us (43%)
  starting transfers between devices  134 us (25%)
  local copies, waits for them, and re-layouts  62.8 us (12%)
  matrix products  50.9 us (9%)
  other arithmetic  42.4 us (8%)
  Pallas kernels  6.88 us (1%)
    ppermute x133, waiting for transfers between devices, trade(): return lax.ppermute(x, AXES, [(i, i ^ mask) for i in range(count)])  232 us
    ppermute x133, starting transfers between devices, trade(): return lax.ppermute(x, AXES, [(i, i ^ mask) for i in range(count)])  124 us
    dot_general x18, matrix products, dot(): return lax.dot_general(a, b, (dims, ((), ())), preferred_element_type=F32)  50.9 us
    unnamed x250, local copies, waits for them, and re-layouts  29.9 us
    select_n x36, other arithmetic, gather_abs(): jnp.where(me & mask != 0, jnp.concatenate([other, mine], axis), jnp.conca...  12.2 us
  transfers between devices with their start and end apart: 135, of which 55 were waited for; matrix products, arithmetic and copies ran while one was open for 26% of the time, Pallas kernels for 1%

profile of v1, /device:TPU:0, one launch (start us, length us, event | category | flops | bytes accessed | tf_op | source)
XLA Modules:
  0.0 533.5 jit_solution(10284601074517591342)
XLA Ops:
  0.7 4.1 collective-permute-start
  4.9 2.8 collective-permute-start.13
  11.1 6.2 %all-to-all-start = ((bf16[48,32,192]{2,0,1:T(8,128)(2,1)}), bf16[48,32,192]{2,0,1:T(8,128)(2,1)}, u32[]{:S(2)}, u32[]{:S(2)}) async-start(bf16[48,32,192]{2,0,1:T(8,128)(2,1)} %copy.128), calls=%async_computation | async-start | bytes 1572864 | tf_op jit(solution)/shard_map/all_to_all | solution.py:304
  18.0 2.6 collective-permute-start.54
  27.1 21.9 %collective-permute-done.54 = bf16[1,8,1536]{2,1,0:T(8,128)(2,1)S(1)} collective-permute-done((bf16[1,8,1536]{2,1,0:T(8,128)(2,1)S(1)}, bf16[1,8,1536]{2,1,0:T(8,128)(2,1)S(1)}, u32[]{:S(2)}, u32[]{:S(2)}) %collective-permute-start.54) | collective-permute-done | bytes 24608 | tf_op jit(solution)/shard_map/ppermute | solution.py:36
  49.0 4.9 collective-permute-done.49
  53.9 4.7 collective-permute-done.83
  58.7 4.7 collective-permute-done.88
  68.5 3.1 collective-permute-done.50
  72.5 3.1 collective-permute-done.84
  94.4 3.9 collective-permute-done.57
  99.6 4.4 collective-permute-done.52
  105.3 4.4 collective-permute-done.86
  111.3 4.1 collective-permute-done.91
  122.1 11.5 %collective-permute-done.2 = bf16[2,2,48,1536]{3,2,1,0:T(8,128)(2,1)S(1)} collective-permute-done((bf16[2,2,48,1536]{3,2,1,0:T(8,128)(2,1)S(1)}, bf16[2,2,48,1536]{3,2,1,0:T(8,128)(2,1)S(1)}, u32[]{:S(2)}, u32[]{:S(2)}) %collective-permute-start.2) | collective-permute-done | bytes 589856 | tf_op jit(solution)/shard_map/ppermute | solution.py:36
  137.0 9.3 %collective-permute-done.26 = bf16[2,2,48,1536]{3,2,0,1:T(8,128)(2,1)S(1)} collective-permute-done((bf16[2,2,48,1536]{3,2,0,1:T(8,128)(2,1)S(1)}, bf16[2,2,48,1536]{3,2,0,1:T(8,128)(2,1)S(1)}, u32[]{:S(2)}, u32[]{:S(2)}) %collective-permute-start.26) | collective-permute-done | bytes 589856 | tf_op jit(solution)/shard_map/ppermute | solution.py:36
  151.3 21.8 %collective-permute-done.3 = bf16[2,2,2,48,1536]{4,3,2,1,0:T(8,128)(2,1)S(1)} collective-permute-done((bf16[2,2,2,48,1536]{4,3,2,1,0:T(8,128)(2,1)S(1)}, bf16[2,2,2,48,1536]{4,3,2,1,0:T(8,128)(2,1)S(1)}, u32[]{:S(2)}, u32[]{:S(2)}) %collective-permute-start.3) | collective-permute-done | bytes 1179680 | tf_op jit(solution)/shard_map/ppermute | solution.py:36
  174.8 21.1 %collective-permute-done.16 = bf16[2,2,2,48,1536]{4,3,0,1,2:T(8,128)(2,1)S(1)} collective-permute-done((bf16[2,2,2,48,1536]{4,3,0,1,2:T(8,128)(2,1)S(1)}, bf16[2,2,2,48,1536]{4,3,0,1,2:T(8,128)(2,1)S(1)}, u32[]{:S(2)}, u32[]{:S(2)}) %collective-permute-start.16) | collective-permute-done | bytes 1179680 | tf_op jit(solution)/shard_map/ppermute | solution.py:36
  205.8 4.4 maximum_select_fusion.2
  211.6 2.7 convolution_convert_fusion.1.refs_2_.refs_4_
  214.3 2.7 convolution_convert_fusion.refs_3_.refs_5_
  217.8 2.6 copy.127
  220.4 2.9 shard_map.288
  230.2 2.7 collective-permute-done.19
  234.3 3.2 fusion.119
  272.1 3.5 fusion.120
  280.2 3.2 all-to-all-start.1
  283.3 3.2 fusion.31
  293.9 4.8 collective-permute-done.65
  301.1 2.9 collective-permute-done.45
  337.8 2.5 collective-permute-start.118
  350.9 4.0 shard_map.289
  354.9 7.0 %fusion.122 = f32[528,1536]{1,0:T(8,128)} fusion(bf16[528,1536]{1,0:T(8,128)(2,1)S(1)} %get-tuple-element.24, bf16[1536,1536]{1,0:T(8,128)(2,1)} %bitcast.456), kind=kOutput, calls=%fused_computation.475 | convolution fusion | flops 2491416576 | bytes 9584640 | tf_op jit(solution)/shard_map/dot_general | solution.py:32
  361.8 4.1 fusion.111
  366.7 3.9 fusion.112
  370.6 7.2 %convolution_add_fusion = f32[528,1536]{1,0:T(8,128)S(1)} fusion(f32[528,1536]{1,0:T(8,128)} %fusion.122, bf16[528,1536]{1,0:T(8,128)(2,1)S(1)} %get-tuple-element.23, bf16[1536,1536]{1,0:T(8,128)(2,1)S(1)} %bitcast.454), kind=kOutput, calls=%fused_computation.10 | convolution fusion | flops 2492227584 | bytes 12828672 | tf_op jit(solution)/shard_map/dot_general | solution.py:32
  401.8 4.5 collective-permute-done.98
  406.6 4.6 collective-permute-done.93
  424.8 2.5 collective-permute-done.95
  447.1 3.2 collective-permute-done.81
  455.6 2.7 fusion.25
  458.3 3.8 bitcast_add_fusion.1
  468.9 21.7 %collective-permute-done.104 = bf16[2,2,2,48,1536]{4,3,0,1,2:T(8,128)(2,1)S(1)} collective-permute-done((bf16[2,2,2,48,1536]{4,3,0,1,2:T(8,128)(2,1)S(1)}, bf16[2,2,2,48,1536]{4,3,0,1,2:T(8,128)(2,1)S(1)}, u32[]{:S(2)}, u32[]{:S(2)}) %collective-permute-start.104) | collective-permute-done | bytes 1179680 | tf_op jit(solution)/shard_map/ppermute | solution.py:36
  496.4 10.4 %collective-permute-done.105 = bf16[2,2,48,1536]{3,2,0,1:T(8,128)(2,1)S(1)} collective-permute-done((bf16[2,2,48,1536]{3,2,0,1:T(8,128)(2,1)S(1)}, bf16[2,2,48,1536]{3,2,0,1:T(8,128)(2,1)S(1)}, u32[]{:S(2)}, u32[]{:S(2)}) %collective-permute-start.105) | collective-permute-done | bytes 589856 | tf_op jit(solution)/shard_map/ppermute | solution.py:36
  509.9 7.0 %collective-permute-done.106 = bf16[2,48,1536]{2,1,0:T(8,128)(2,1)S(1)} collective-permute-done((bf16[2,48,1536]{2,1,0:T(8,128)(2,1)S(1)}, bf16[2,48,1536]{2,1,0:T(8,128)(2,1)S(1)}, u32[]{:S(2)}, u32[]{:S(2)}) %collective-permute-start.106) | collective-permute-done | bytes 294944 | tf_op jit(solution)/shard_map/ppermute | solution.py:36
  518.6 6.0 %collective-permute-done.111 = bf16[2,48,1536]{2,1,0:T(8,128)(2,1)S(1)} collective-permute-done((bf16[2,48,1536]{2,1,0:T(8,128)(2,1)S(1)}, bf16[2,48,1536]{2,1,0:T(8,128)(2,1)S(1)}, u32[]{:S(2)}, u32[]{:S(2)}) %collective-permute-start.111) | collective-permute-done | bytes 294944 | tf_op jit(solution)/shard_map/ppermute | solution.py:36
  524.9 2.8 collective-permute-done.107
  528.4 3.9 collective-permute-done.112
  (740 shorter events, 250.3 us)
Async XLA Ops:
  0.7 83.9 %collective-permute-start = (bf16[48,1536]{1,0:T(8,128)(2,1)}, bf16[48,1536]{1,0:T(8,128)(2,1)S(1)}, u32[]{:S(2)}, u32[]{:S(2)}) collective-permute-start(bf16[48,1536]{1,0:T(8,128)(2,1)} %param.27), channel_id=1, source_target_pairs={{0,16},{1,17},{2,18},{3,19},{4,20},{5,21},{6,22},{7,23},{8,24},{9,... | collective-permute-start | bytes 442376 | tf_op jit(solution)/shard_map/ppermute | solution.py:36
  4.8 81.5 %collective-permute-start.8 = (bf16[48,1536]{1,0:T(8,128)(2,1)}, bf16[48,1536]{1,0:T(8,128)(2,1)S(1)}, u32[]{:S(2)}, u32[]{:S(2)}) collective-permute-start(bf16[48,1536]{1,0:T(8,128)(2,1)} %param.28), channel_id=1, source_target_pairs={{0,16},{1,17},{2,18},{3,19},{4,20},{5,21},{6,22},{7,23},{8,24},{9,... | collective-permute-start | bytes 442376 | tf_op jit(solution)/shard_map/ppermute | solution.py:36
  4.9 82.0 %collective-permute-start.13 = (bf16[48,1536]{1,0:T(8,128)(2,1)}, bf16[48,1536]{1,0:T(8,128)(2,1)S(1)}, u32[]{:S(2)}, u32[]{:S(2)}) collective-permute-start(bf16[48,1536]{1,0:T(8,128)(2,1)} %param.29), channel_id=1, source_target_pairs={{0,16},{1,17},{2,18},{3,19},{4,20},{5,21},{6,22},{7,23},{8,24},{9,... | collective-permute-start | bytes 442376 | tf_op jit(solution)/shard_map/ppermute | solution.py:36
  7.7 79.7 %collective-permute-start.24 = (bf16[48,1536]{1,0:T(8,128)(2,1)}, bf16[48,1536]{1,0:T(8,128)(2,1)S(1)}, u32[]{:S(2)}, u32[]{:S(2)}) collective-permute-start(bf16[48,1536]{1,0:T(8,128)(2,1)} %param.30), channel_id=1, source_target_pairs={{0,16},{1,17},{2,18},{3,19},{4,20},{5,21},{6,22},{7,23},{8,24},{9,... | collective-permute-start | bytes 442376 | tf_op jit(solution)/shard_map/ppermute | solution.py:36
  11.1 255.5 %all-to-all-start = ((bf16[48,32,192]{2,0,1:T(8,128)(2,1)}), bf16[48,32,192]{2,0,1:T(8,128)(2,1)}, u32[]{:S(2)}, u32[]{:S(2)}) async-start(bf16[48,32,192]{2,0,1:T(8,128)(2,1)} %copy.128), calls=%async_computation | async-start | bytes 1572864 | tf_op jit(solution)/shard_map/all_to_all | solution.py:304
  18.0 31.1 %collective-permute-start.54 = (bf16[1,8,1536]{2,1,0:T(8,128)(2,1)S(1)}, bf16[1,8,1536]{2,1,0:T(8,128)(2,1)S(1)}, u32[]{:S(2)}, u32[]{:S(2)}) collective-permute-start(bf16[1,8,1536]{2,1,0:T(8,128)(2,1)S(1)} %get-tuple-element.175), channel_id=1, source_target_pairs={{0,16},{1,17},{2,18},{3,19},{4,20},{5,21},{6,22},{7,23},{8,24},{9,... | collective-permute-start | bytes 73736 | tf_op jit(solution)/shard_map/ppermute | solution.py:36
  87.6 28.5 %collective-permute-start.1 = (bf16[2,48,1536]{2,1,0:T(8,128)(2,1)S(1)}, bf16[2,48,1536]{2,1,0:T(8,128)(2,1)S(1)}, u32[]{:S(2)}, u32[]{:S(2)}) collective-permute-start(bf16[2,48,1536]{2,1,0:T(8,128)(2,1)S(1)} %maximum_select_fusion.24), channel_id=1, source_target_pairs={{0,8},{1,9},{2,10},{3,11},{4,12},{5,13},{6,14},{7,15},{8,0},{9,1},... | collective-permute-start | bytes 884744 | tf_op jit(solution)/shard_map/ppermute | solution.py:36
  88.8 26.6 %collective-permute-start.9 = (bf16[2,48,1536]{2,1,0:T(8,128)(2,1)S(1)}, bf16[2,48,1536]{2,1,0:T(8,128)(2,1)S(1)}, u32[]{:S(2)}, u32[]{:S(2)}) collective-permute-start(bf16[2,48,1536]{2,1,0:T(8,128)(2,1)S(1)} %maximum_select_fusion.25), channel_id=1, source_target_pairs={{0,8},{1,9},{2,10},{3,11},{4,12},{5,13},{6,14},{7,15},{8,0},{9,1},... | collective-permute-start | bytes 884744 | tf_op jit(solution)/shard_map/ppermute | solution.py:36
  89.9 26.6 %collective-permute-start.14 = (bf16[2,48,1536]{2,1,0:T(8,128)(2,1)S(1)}, bf16[2,48,1536]{2,1,0:T(8,128)(2,1)S(1)}, u32[]{:S(2)}, u32[]{:S(2)}) collective-permute-start(bf16[2,48,1536]{2,1,0:T(8,128)(2,1)S(1)} %maximum_select_fusion.26), channel_id=1, source_target_pairs={{0,8},{1,9},{2,10},{3,11},{4,12},{5,13},{6,14},{7,15},{8,0},{9,1},... | collective-permute-start | bytes 884744 | tf_op jit(solution)/shard_map/ppermute | solution.py:36
  91.0 26.3 %collective-permute-start.25 = (bf16[2,48,1536]{2,1,0:T(8,128)(2,1)S(1)}, bf16[2,48,1536]{2,1,0:T(8,128)(2,1)S(1)}, u32[]{:S(2)}, u32[]{:S(2)}) collective-permute-start(bf16[2,48,1536]{2,1,0:T(8,128)(2,1)S(1)} %maximum_select_fusion.27), channel_id=1, source_target_pairs={{0,8},{1,9},{2,10},{3,11},{4,12},{5,13},{6,14},{7,15},{8,0},{9,1},... | collective-permute-start | bytes 884744 | tf_op jit(solution)/shard_map/ppermute | solution.py:36
  117.4 16.3 %collective-permute-start.2 = (bf16[2,2,48,1536]{3,2,1,0:T(8,128)(2,1)S(1)}, bf16[2,2,48,1536]{3,2,1,0:T(8,128)(2,1)S(1)}, u32[]{:S(2)}, u32[]{:S(2)}) collective-permute-start(bf16[2,2,48,1536]{3,2,1,0:T(8,128)(2,1)S(1)} %maximum_select_fusion.19), channel_id=1, source_target_pairs={{0,2},{1,3},{2,0},{3,1},{4,6},{5,7},{6,4},{7,5},{8,10},{9,11},{10,... | collective-permute-start | bytes 1769480 | tf_op jit(solution)/shard_map/ppermute | solution.py:36
  118.9 16.5 %collective-permute-start.10 = (bf16[2,2,48,1536]{3,2,0,1:T(8,128)(2,1)S(1)}, bf16[2,2,48,1536]{3,2,0,1:T(8,128)(2,1)S(1)}, u32[]{:S(2)}, u32[]{:S(2)}) collective-permute-start(bf16[2,2,48,1536]{3,2,0,1:T(8,128)(2,1)S(1)} %maximum_select_fusion.20), channel_id=1, source_target_pairs={{0,4},{1,5},{2,6},{3,7},{4,0},{5,1},{6,2},{7,3},{8,12},{9,13},{10,... | collective-permute-start | bytes 1769480 | tf_op jit(solution)/shard_map/ppermute | solution.py:36
  120.6 27.2 %collective-permute-start.15 = (bf16[2,2,48,1536]{3,2,0,1:T(8,128)(2,1)S(1)}, bf16[2,2,48,1536]{3,2,0,1:T(8,128)(2,1)S(1)}, u32[]{:S(2)}, u32[]{:S(2)}) collective-permute-start(bf16[2,2,48,1536]{3,2,0,1:T(8,128)(2,1)S(1)} %maximum_select_fusion.22), channel_id=1, source_target_pairs={{0,4},{1,5},{2,6},{3,7},{4,0},{5,1},{6,2},{7,3},{8,12},{9,13},{10,... | collective-permute-start | bytes 1769480 | tf_op jit(solution)/shard_map/ppermute | solution.py:36
  121.2 25.1 %collective-permute-start.26 = (bf16[2,2,48,1536]{3,2,0,1:T(8,128)(2,1)S(1)}, bf16[2,2,48,1536]{3,2,0,1:T(8,128)(2,1)S(1)}, u32[]{:S(2)}, u32[]{:S(2)}) collective-permute-start(bf16[2,2,48,1536]{3,2,0,1:T(8,128)(2,1)S(1)} %maximum_select_fusion.23), channel_id=1, source_target_pairs={{0,2},{1,3},{2,0},{3,1},{4,6},{5,7},{6,4},{7,5},{8,10},{9,11},{10,... | collective-permute-start | bytes 1769480 | tf_op jit(solution)/shard_map/ppermute | solution.py:36
  133.7 39.4 %collective-permute-start.3 = (bf16[2,2,2,48,1536]{4,3,2,1,0:T(8,128)(2,1)S(1)}, bf16[2,2,2,48,1536]{4,3,2,1,0:T(8,128)(2,1)S(1)}, u32[]{:S(2)}, u32[]{:S(2)}) collective-permute-start(bf16[2,2,2,48,1536]{4,3,2,1,0:T(8,128)(2,1)S(1)} %maximum_select_fusion.12), channel_id=1, source_target_pairs={{0,4},{1,5},{2,6},{3,7},{4,0},{5,1},{6,2},{7,3},{8,12},{9,13},{10,... | collective-permute-start | bytes 3538952 | tf_op jit(solution)/shard_map/ppermute | solution.py:36
  135.6 38.2 %collective-permute-start.11 = (bf16[2,2,2,48,1536]{4,3,0,1,2:T(8,128)(2,1)S(1)}, bf16[2,2,2,48,1536]{4,3,0,1,2:T(8,128)(2,1)S(1)}, u32[]{:S(2)}, u32[]{:S(2)}) collective-permute-start(bf16[2,2,2,48,1536]{4,3,0,1,2:T(8,128)(2,1)S(1)} %maximum_select_fusion.13), channel_id=1, source_target_pairs={{0,2},{1,3},{2,0},{3,1},{4,6},{5,7},{6,4},{7,5},{8,10},{9,11},{10,... | collective-permute-start | bytes 3538952 | tf_op jit(solution)/shard_map/ppermute | solution.py:36
  148.1 47.8 %collective-permute-start.16 = (bf16[2,2,2,48,1536]{4,3,0,1,2:T(8,128)(2,1)S(1)}, bf16[2,2,2,48,1536]{4,3,0,1,2:T(8,128)(2,1)S(1)}, u32[]{:S(2)}, u32[]{:S(2)}) collective-permute-start(bf16[2,2,2,48,1536]{4,3,0,1,2:T(8,128)(2,1)S(1)} %maximum_select_fusion.15), channel_id=1, source_target_pairs={{0,2},{1,3},{2,0},{3,1},{4,6},{5,7},{6,4},{7,5},{8,10},{9,11},{10,... | collective-permute-start | bytes 3538952 | tf_op jit(solution)/shard_map/ppermute | solution.py:36
  149.1 48.1 %collective-permute-start.27 = (bf16[2,2,2,48,1536]{4,3,0,1,2:T(8,128)(2,1)S(1)}, bf16[2,2,2,48,1536]{4,3,0,1,2:T(8,128)(2,1)S(1)}, u32[]{:S(2)}, u32[]{:S(2)}) collective-permute-start(bf16[2,2,2,48,1536]{4,3,0,1,2:T(8,128)(2,1)S(1)} %maximum_select_fusion.17), channel_id=1, source_target_pairs={{0,4},{1,5},{2,6},{3,7},{4,0},{5,1},{6,2},{7,3},{8,12},{9,13},{10,... | collective-permute-start | bytes 3538952 | tf_op jit(solution)/shard_map/ppermute | solution.py:36
  173.5 26.0 %collective-permute-start.4 = (bf16[2,2,2,2,48,1536]{5,4,3,1,0,2:T(8,128)(2,1)S(1)}, bf16[2,2,2,2,48,1536]{5,4,3,1,0,2:T(8,128)(2,1)S(1)}, u32[]{:S(2)}, u32[]{:S(2)}) collective-permute-start(bf16[2,2,2,2,48,1536]{5,4,3,1,0,2:T(8,128)(2,1)S(1)} %maximum_select_fusion.4), channel_id=1, source_target_pairs={{0,1},{1,0},{2,3},{3,2},{4,5},{5,4},{6,7},{7,6},{8,9},{9,8},{10,11... | collective-permute-start | bytes 7077896 | tf_op jit(solution)/shard_map/ppermute | solution.py:36
  174.2 30.3 %collective-permute-start.12 = (bf16[2,2,2,2,48,1536]{5,4,0,1,2,3:T(8,128)(2,1)S(1)}, bf16[2,2,2,2,48,1536]{5,4,0,1,2,3:T(8,128)(2,1)S(1)}, u32[]{:S(2)}, u32[]{:S(2)}) collective-permute-start(bf16[2,2,2,2,48,1536]{5,4,0,1,2,3:T(8,128)(2,1)S(1)} %maximum_select_fusion.6), channel_id=1, source_target_pairs={{0,1},{1,0},{2,3},{3,2},{4,5},{5,4},{6,7},{7,6},{8,9},{9,8},{10,11... | collective-permute-start | bytes 7077896 | tf_op jit(solution)/shard_map/ppermute | solution.py:36
  197.5 19.5 %collective-permute-start.28 = (bf16[2,2,2,2,48,1536]{5,4,0,1,3,2:T(8,128)(2,1)S(1)}, bf16[2,2,2,2,48,1536]{5,4,0,1,3,2:T(8,128)(2,1)S(1)}, u32[]{:S(2)}, u32[]{:S(2)}) collective-permute-start(bf16[2,2,2,2,48,1536]{5,4,0,1,3,2:T(8,128)(2,1)S(1)} %maximum_select_fusion.10), channel_id=1, source_target_pairs={{0,1},{1,0},{2,3},{3,2},{4,5},{5,4},{6,7},{7,6},{8,9},{9,8},{10,11... | collective-permute-start | bytes 7077896 | tf_op jit(solution)/shard_map/ppermute | solution.py:36
  202.4 17.9 %collective-permute-start.7 = (bf16[16,1536]{1,0:T(8,128)(2,1)S(1)}, bf16[16,1536]{1,0:T(8,128)(2,1)S(1)}, u32[]{:S(2)}, u32[]{:S(2)}) collective-permute-start(bf16[16,1536]{1,0:T(8,128)(2,1)S(1)} %fusion.21), channel_id=1, source_target_pairs={{0,3},{1,2},{2,1},{3,0},{4,7},{5,6},{6,5},{7,4},{8,11},{9,10},{10,... | collective-permute-start | bytes 147464 | tf_op jit(solution)/shard_map/ppermute | solution.py:36
  203.3 17.1 %collective-permute-start.6 = (bf16[16,1536]{1,0:T(8,128)(2,1)S(1)}, bf16[16,1536]{1,0:T(8,128)(2,1)S(1)}, u32[]{:S(2)}, u32[]{:S(2)}) collective-permute-start(bf16[16,1536]{1,0:T(8,128)(2,1)S(1)} %fusion.21), channel_id=1, source_target_pairs={{0,2},{1,3},{2,0},{3,1},{4,6},{5,7},{6,4},{7,5},{8,10},{9,11},{10,... | collective-permute-start | bytes 147464 | tf_op jit(solution)/shard_map/ppermute | solution.py:36
  204.6 15.8 %collective-permute-start.5 = (bf16[16,1536]{1,0:T(8,128)(2,1)S(1)}, bf16[16,1536]{1,0:T(8,128)(2,1)S(1)}, u32[]{:S(2)}, u32[]{:S(2)}) collective-permute-start(bf16[16,1536]{1,0:T(8,128)(2,1)S(1)} %fusion.21), channel_id=1, source_target_pairs={{0,1},{1,0},{2,3},{3,2},{4,5},{5,4},{6,7},{7,6},{8,9},{9,8},{10,11... | collective-permute-start | bytes 147464 | tf_op jit(solution)/shard_map/ppermute | solution.py:36
  278.0 13.4 %collective-permute-start.39 = (bf16[16,8,1536]{2,1,0:T(8,128)(2,1)}, bf16[16,8,1536]{2,1,0:T(8,128)(2,1)}, u32[]{:S(2)}, u32[]{:S(2)}) collective-permute-start(bf16[16,8,1536]{2,1,0:T(8,128)(2,1)} %get-tuple-element.53), channel_id=1, source_target_pairs={{0,1},{1,0},{2,3},{3,2},{4,5},{5,4},{6,7},{7,6},{8,9},{9,8},{10,11... | collective-permute-start | bytes 1179656 | tf_op jit(solution)/shard_map/ppermute | solution.py:36
  278.5 12.9 %collective-permute-start.44 = (bf16[16,8,1536]{2,1,0:T(8,128)(2,1)}, bf16[16,8,1536]{2,1,0:T(8,128)(2,1)}, u32[]{:S(2)}, u32[]{:S(2)}) collective-permute-start(bf16[16,8,1536]{2,1,0:T(8,128)(2,1)} %get-tuple-element.54), channel_id=1, source_target_pairs={{0,1},{1,0},{2,3},{3,2},{4,5},{5,4},{6,7},{7,6},{8,9},{9,8},{10,11... | collective-permute-start | bytes 1179656 | tf_op jit(solution)/shard_map/ppermute | solution.py:36
  280.2 162.0 %all-to-all-start.1 = ((bf16[32,48,192]{2,1,0:T(8,128)(2,1)}), bf16[32,48,192]{2,1,0:T(8,128)(2,1)S(1)}, u32[]{:S(2)}, u32[]{:S(2)}) async-start(bf16[32,48,192]{2,1,0:T(8,128)(2,1)} %bitcast.457), calls=%async_computation.1 | async-start | bytes 1572864 | tf_op jit(solution)/shard_map/all_to_all | solution.py:316
  324.5 22.9 %collective-permute-start.71 = (bf16[16,1536]{1,0:T(8,128)(2,1)S(1)}, bf16[16,1536]{1,0:T(8,128)(2,1)S(1)}, u32[]{:S(2)}, u32[]{:S(2)}) collective-permute-start(bf16[16,1536]{1,0:T(8,128)(2,1)S(1)} %convolution_convert_fusion.3), channel_id=1, source_target_pairs={{0,3},{1,2},{2,1},{3,0},{4,7},{5,6},{6,5},{7,4},{8,11},{9,10},{10,... | collective-permute-start | bytes 147464 | tf_op jit(solution)/shard_map/ppermute | solution.py:36
  324.5 23.2 %collective-permute-start.70 = (bf16[16,1536]{1,0:T(8,128)(2,1)S(1)}, bf16[16,1536]{1,0:T(8,128)(2,1)S(1)}, u32[]{:S(2)}, u32[]{:S(2)}) collective-permute-start(bf16[16,1536]{1,0:T(8,128)(2,1)S(1)} %convolution_convert_fusion.3), channel_id=1, source_target_pairs={{0,2},{1,3},{2,0},{3,1},{4,6},{5,7},{6,4},{7,5},{8,10},{9,11},{10,... | collective-permute-start | bytes 147464 | tf_op jit(solution)/shard_map/ppermute | solution.py:36
  330.8 18.6 %collective-permute-start.69 = (bf16[16,1536]{1,0:T(8,128)(2,1)S(1)}, bf16[16,1536]{1,0:T(8,128)(2,1)S(1)}, u32[]{:S(2)}, u32[]{:S(2)}) collective-permute-start(bf16[16,1536]{1,0:T(8,128)(2,1)S(1)} %convolution_convert_fusion.3), channel_id=1, source_target_pairs={{0,1},{1,0},{2,3},{3,2},{4,5},{5,4},{6,7},{7,6},{8,9},{9,8},{10,11... | collective-permute-start | bytes 147464 | tf_op jit(solution)/shard_map/ppermute | solution.py:36
  341.6 44.0 %collective-permute-start.129 = (bf16[2,8,1536]{2,1,0:T(8,128)(2,1)}, bf16[2,8,1536]{2,1,0:T(8,128)(2,1)S(1)}, u32[]{:S(2)}, u32[]{:S(2)}) collective-permute-start(bf16[2,8,1536]{2,1,0:T(8,128)(2,1)} %pad_maximum_fusion.51), channel_id=1, source_target_pairs={{0,8},{1,9},{2,10},{3,11},{4,12},{5,13},{6,14},{7,15},{8,0},{9,1},... | collective-permute-start | bytes 147464 | tf_op jit(solution)/shard_map/ppermute | solution.py:36
  342.6 43.7 %collective-permute-start.124 = (bf16[2,8,1536]{2,1,0:T(8,128)(2,1)}, bf16[2,8,1536]{2,1,0:T(8,128)(2,1)S(1)}, u32[]{:S(2)}, u32[]{:S(2)}) collective-permute-start(bf16[2,8,1536]{2,1,0:T(8,128)(2,1)} %pad_maximum_fusion.50), channel_id=1, source_target_pairs={{0,8},{1,9},{2,10},{3,11},{4,12},{5,13},{6,14},{7,15},{8,0},{9,1},... | collective-permute-start | bytes 147464 | tf_op jit(solution)/shard_map/ppermute | solution.py:36
  347.4 40.8 %collective-permute-start.114 = (bf16[2,8,1536]{2,1,0:T(8,128)(2,1)}, bf16[2,8,1536]{2,1,0:T(8,128)(2,1)S(1)}, u32[]{:S(2)}, u32[]{:S(2)}) collective-permute-start(bf16[2,8,1536]{2,1,0:T(8,128)(2,1)} %pad_maximum_fusion.48), channel_id=1, source_target_pairs={{0,8},{1,9},{2,10},{3,11},{4,12},{5,13},{6,14},{7,15},{8,0},{9,1},... | collective-permute-start | bytes 147464 | tf_op jit(solution)/shard_map/ppermute | solution.py:36
  347.7 40.5 %collective-permute-start.119 = (bf16[2,8,1536]{2,1,0:T(8,128)(2,1)}, bf16[2,8,1536]{2,1,0:T(8,128)(2,1)S(1)}, u32[]{:S(2)}, u32[]{:S(2)}) collective-permute-start(bf16[2,8,1536]{2,1,0:T(8,128)(2,1)} %pad_maximum_fusion.49), channel_id=1, source_target_pairs={{0,8},{1,9},{2,10},{3,11},{4,12},{5,13},{6,14},{7,15},{8,0},{9,1},... | collective-permute-start | bytes 147464 | tf_op jit(solution)/shard_map/ppermute | solution.py:36
  366.7 24.8 %collective-permute-start.77 = (f32[16,1536]{1,0:T(8,128)S(1)}, f32[16,1536]{1,0:T(8,128)S(1)}, u32[]{:S(2)}, u32[]{:S(2)}) collective-permute-start(f32[16,1536]{1,0:T(8,128)S(1)} %get-tuple-element.68), channel_id=1, source_target_pairs={{0,3},{1,2},{2,1},{3,0},{4,7},{5,6},{6,5},{7,4},{8,11},{9,10},{10,... | collective-permute-start | bytes 294920 | tf_op jit(solution)/shard_map/ppermute | solution.py:36
  388.2 70.1 %collective-permute-start.103 = (bf16[2,2,2,2,48,1536]{5,4,0,1,3,2:T(8,128)(2,1)}, bf16[2,2,2,2,48,1536]{5,4,0,1,3,2:T(8,128)(2,1)}, u32[]{:S(2)}, u32[]{:S(2)}) collective-permute-start(bf16[2,2,2,2,48,1536]{5,4,0,1,3,2:T(8,128)(2,1)} %fusion.18), channel_id=1, source_target_pairs={{0,1},{1,0},{2,3},{3,2},{4,5},{5,4},{6,7},{7,6},{8,9},{9,8},{10,11... | collective-permute-start | bytes 7077896 | tf_op jit(solution)/shard_map/ppermute | solution.py:36
  388.3 75.1 %collective-permute-start.108 = (bf16[2,2,2,2,48,1536]{5,4,0,1,2,3:T(8,128)(2,1)}, bf16[2,2,2,2,48,1536]{5,4,0,1,2,3:T(8,128)(2,1)}, u32[]{:S(2)}, u32[]{:S(2)}) collective-permute-start(bf16[2,2,2,2,48,1536]{5,4,0,1,2,3:T(8,128)(2,1)} %fusion.19), channel_id=1, source_target_pairs={{0,1},{1,0},{2,3},{3,2},{4,5},{5,4},{6,7},{7,6},{8,9},{9,8},{10,11... | collective-permute-start | bytes 7077896 | tf_op jit(solution)/shard_map/ppermute | solution.py:36
  397.3 14.3 %collective-permute-start.120 = (bf16[4,8,1536]{2,1,0:T(8,128)(2,1)S(1)}, bf16[4,8,1536]{2,1,0:T(8,128)(2,1)S(1)}, u32[]{:S(2)}, u32[]{:S(2)}) collective-permute-start(bf16[4,8,1536]{2,1,0:T(8,128)(2,1)S(1)} %pad_maximum_fusion.37), channel_id=1, source_target_pairs={{0,2},{1,3},{2,0},{3,1},{4,6},{5,7},{6,4},{7,5},{8,10},{9,11},{10,... | collective-permute-start | bytes 294920 | tf_op jit(solution)/shard_map/ppermute | solution.py:36
  398.7 21.5 %collective-permute-start.78 = (f32[16,1536]{1,0:T(8,128)S(1)}, f32[16,1536]{1,0:T(8,128)S(1)}, u32[]{:S(2)}, u32[]{:S(2)}) collective-permute-start(f32[16,1536]{1,0:T(8,128)S(1)} %concatenate.1096), channel_id=1, source_target_pairs={{0,16},{1,17},{2,18},{3,19},{4,20},{5,21},{6,22},{7,23},{8,24},{9,... | collective-permute-start | bytes 294920 | tf_op jit(solution)/shard_map/ppermute | solution.py:36
  417.3 15.4 %collective-permute-start.131 = (bf16[8,8,1536]{2,1,0:T(8,128)(2,1)S(1)}, bf16[8,8,1536]{2,1,0:T(8,128)(2,1)S(1)}, u32[]{:S(2)}, u32[]{:S(2)}) collective-permute-start(bf16[8,8,1536]{2,1,0:T(8,128)(2,1)S(1)} %pad_maximum_fusion.26), channel_id=1, source_target_pairs={{0,4},{1,5},{2,6},{3,7},{4,0},{5,1},{6,2},{7,3},{8,12},{9,13},{10,... | collective-permute-start | bytes 589832 | tf_op jit(solution)/shard_map/ppermute | solution.py:36
  420.2 15.0 %collective-permute-start.126 = (bf16[8,8,1536]{2,1,0:T(8,128)(2,1)S(1)}, bf16[8,8,1536]{2,1,0:T(8,128)(2,1)S(1)}, u32[]{:S(2)}, u32[]{:S(2)}) collective-permute-start(bf16[8,8,1536]{2,1,0:T(8,128)(2,1)S(1)} %pad_maximum_fusion.25), channel_id=1, source_target_pairs={{0,2},{1,3},{2,0},{3,1},{4,6},{5,7},{6,4},{7,5},{8,10},{9,11},{10,... | collective-permute-start | bytes 589832 | tf_op jit(solution)/shard_map/ppermute | solution.py:36
  454.8 12.6 %collective-permute-start.102 = (bf16[16,8,1536]{2,1,0:T(8,128)(2,1)}, bf16[16,8,1536]{2,1,0:T(8,128)(2,1)S(1)}, u32[]{:S(2)}, u32[]{:S(2)}) collective-permute-start(bf16[16,8,1536]{2,1,0:T(8,128)(2,1)} %get-tuple-element.88), channel_id=1, source_target_pairs={{0,1},{1,0},{2,3},{3,2},{4,5},{5,4},{6,7},{7,6},{8,9},{9,8},{10,11... | collective-permute-start | bytes 1179656 | tf_op jit(solution)/shard_map/ppermute | solution.py:36
  455.0 12.5 %collective-permute-start.97 = (bf16[16,8,1536]{2,1,0:T(8,128)(2,1)}, bf16[16,8,1536]{2,1,0:T(8,128)(2,1)S(1)}, u32[]{:S(2)}, u32[]{:S(2)}) collective-permute-start(bf16[16,8,1536]{2,1,0:T(8,128)(2,1)} %get-tuple-element.86), channel_id=1, source_target_pairs={{0,1},{1,0},{2,3},{3,2},{4,5},{5,4},{6,7},{7,6},{8,9},{9,8},{10,11... | collective-permute-start | bytes 1179656 | tf_op jit(solution)/shard_map/ppermute | solution.py:36
  462.3 28.3 %collective-permute-start.104 = (bf16[2,2,2,48,1536]{4,3,0,1,2:T(8,128)(2,1)S(1)}, bf16[2,2,2,48,1536]{4,3,0,1,2:T(8,128)(2,1)S(1)}, u32[]{:S(2)}, u32[]{:S(2)}) collective-permute-start(bf16[2,2,2,48,1536]{4,3,0,1,2:T(8,128)(2,1)S(1)} %fusion.29), channel_id=1, source_target_pairs={{0,4},{1,5},{2,6},{3,7},{4,0},{5,1},{6,2},{7,3},{8,12},{9,13},{10,... | collective-permute-start | bytes 3538952 | tf_op jit(solution)/shard_map/ppermute | solution.py:36
  466.1 28.8 %collective-permute-start.109 = (bf16[2,2,2,48,1536]{4,3,0,1,2:T(8,128)(2,1)S(1)}, bf16[2,2,2,48,1536]{4,3,0,1,2:T(8,128)(2,1)S(1)}, u32[]{:S(2)}, u32[]{:S(2)}) collective-permute-start(bf16[2,2,2,48,1536]{4,3,0,1,2:T(8,128)(2,1)S(1)} %fusion.30), channel_id=1, source_target_pairs={{0,2},{1,3},{2,0},{3,1},{4,6},{5,7},{6,4},{7,5},{8,10},{9,11},{10,... | collective-permute-start | bytes 3538952 | tf_op jit(solution)/shard_map/ppermute | solution.py:36
  491.1 15.7 %collective-permute-start.105 = (bf16[2,2,48,1536]{3,2,0,1:T(8,128)(2,1)S(1)}, bf16[2,2,48,1536]{3,2,0,1:T(8,128)(2,1)S(1)}, u32[]{:S(2)}, u32[]{:S(2)}) collective-permute-start(bf16[2,2,48,1536]{3,2,0,1:T(8,128)(2,1)S(1)} %fusion.38), channel_id=1, source_target_pairs={{0,2},{1,3},{2,0},{3,1},{4,6},{5,7},{6,4},{7,5},{8,10},{9,11},{10,... | collective-permute-start | bytes 1769480 | tf_op jit(solution)/shard_map/ppermute | solution.py:36
  495.3 13.8 %collective-permute-start.110 = (bf16[2,2,48,1536]{3,2,0,1:T(8,128)(2,1)S(1)}, bf16[2,2,48,1536]{3,2,0,1:T(8,128)(2,1)S(1)}, u32[]{:S(2)}, u32[]{:S(2)}) collective-permute-start(bf16[2,2,48,1536]{3,2,0,1:T(8,128)(2,1)S(1)} %fusion.39), channel_id=1, source_target_pairs={{0,4},{1,5},{2,6},{3,7},{4,0},{5,1},{6,2},{7,3},{8,12},{9,13},{10,... | collective-permute-start | bytes 1769480 | tf_op jit(solution)/shard_map/ppermute | solution.py:36
  509.3 15.3 %collective-permute-start.111 = (bf16[2,48,1536]{2,1,0:T(8,128)(2,1)S(1)}, bf16[2,48,1536]{2,1,0:T(8,128)(2,1)S(1)}, u32[]{:S(2)}, u32[]{:S(2)}) collective-permute-start(bf16[2,48,1536]{2,1,0:T(8,128)(2,1)S(1)} %fusion.49), channel_id=1, source_target_pairs={{0,8},{1,9},{2,10},{3,11},{4,12},{5,13},{6,14},{7,15},{8,0},{9,1},... | collective-permute-start | bytes 884744 | tf_op jit(solution)/shard_map/ppermute | solution.py:36
  (191 other events, 2208.9 us)

commit v2 on v1

v2 whole, which is shorter than its diff:
```python
import jax
import jax.numpy as jnp
from jax import lax
from jax.experimental import pallas as pl
from jax.experimental.pallas import tpu as pltpu
from jax.sharding import PartitionSpec as P

H = 16
FRAMES = 8
PATCH = 256
AXES = ("items", "seq")
BF = jnp.bfloat16
F32 = jnp.float32


def layer_norm(values, gain, bias):
    center = jnp.mean(values, axis=-1, keepdims=True)
    spread = jnp.mean(jnp.square(values - center), axis=-1, keepdims=True)
    rstd = lax.rsqrt(spread + 1e-05)
    unit = (values - center) * rstd
    return unit * gain + bias, unit, rstd


def layer_norm_back(grad, unit, rstd, gain):
    scaled = grad * gain
    inner = scaled - jnp.mean(scaled, axis=-1, keepdims=True)
    inner = inner - unit * jnp.mean(scaled * unit, axis=-1, keepdims=True)
    return inner * rstd, jnp.sum(grad * unit, axis=0), jnp.sum(grad, axis=0)


def dot(a, b, dims=((1,), (0,))):
    return lax.dot_general(a, b, (dims, ((), ())), preferred_element_type=F32)


def trade(x, mask, count):
    return lax.ppermute(x, AXES, [(i, i ^ mask) for i in range(count)])


def after(x, *others):
    return lax.optimization_barrier((x,) + others)[0]


class Gather:
    def __init__(self, x, order, me):
        self.x, self.order, self.me, self.done = x, list(order), me, []

    def send(self):
        return self.x, self.order[0]

    def take(self, sent, other):
        mask = self.order.pop(0)
        axis = sum(m > mask for m in self.done)
        mine, other = jnp.expand_dims(sent, axis), jnp.expand_dims(other, axis)
        self.x = jnp.where(
            (self.me & mask) != 0,
            jnp.concatenate([other, mine], axis),
            jnp.concatenate([mine, other], axis),
        )
        self.done.append(mask)


class GatherRel:
    def __init__(self, x, order):
        self.order, self.x = list(order), x

    def send(self):
        return self.x, self.order[0]

    def take(self, sent, other):
        self.order.pop(0)
        self.x = jnp.concatenate([sent, other], axis=0)


class GatherApart(GatherRel):
    def take(self, sent, other):
        if len(self.order) > 2:
            GatherRel.take(self, sent, other)
        else:
            self.order.pop(0)
            self.x = (sent, other)

    def last(self, count, token):
        mask = self.order.pop(0)
        pieces = lax.optimization_barrier(tuple(self.x) + (token,))[:2]
        self.x = [*pieces, *[trade(x, mask, count) for x in pieces]]
        return pieces[0]


class Halves:
    def __init__(self, keep, send, orders):
        self.orders, self.keep, self.sends = [list(order) for order in orders], keep, send

    def step(self, count, wait=()):
        sent = lax.optimization_barrier(tuple(self.sends) + tuple(wait))
        masks = [order.pop() for order in self.orders]
        self.others = [trade(x, mask, count) for x, mask in zip(sent, masks)]
        self.token = sent[0]

    def split(self, parts=1):
        self.keep, self.sends = add_split(self.keep, self.others, parts)

    def total(self):
        return [k.astype(F32) + o.astype(F32) for k, o in zip(self.keep, self.others)]


def add_split_kernel(pairs, *refs):
    ins, outs = refs[: 4 * pairs], refs[4 * pairs :]
    for k in range(pairs):
        keep, keep2, other, other2 = ins[4 * k : 4 * k + 4]
        out, send = outs[2 * k : 2 * k + 2]
        out[...] = (keep[...].astype(F32) + other[...].astype(F32)).reshape(out.shape)
        send[...] = (keep2[...].astype(F32) + other2[...].astype(F32)).astype(BF).reshape(send.shape)


def add_split(keeps, others, parts=1):
    shape = keeps[0].shape[-3:]
    half = shape[0] // 2
    some = min(half, 2)
    ins, specs, outs = [], [], []
    for keep, other in zip(keeps, others):
        for part in range(parts):

            def spec(at, part=part):
                if parts == 1:
                    return pl.BlockSpec((some,) + shape[1:], lambda i: (i + at, 0, 0))
                return pl.BlockSpec((1, some) + shape[1:], lambda i: (part, i + at, 0, 0))

            ins += [keep, keep, other, other]
            specs += [spec(0), spec(half // some), spec(0), spec(half // some)]
            outs += [
                jax.ShapeDtypeStruct((half,) + shape[1:], F32),
                jax.ShapeDtypeStruct((half,) + shape[1:], BF),
            ]
    out = pl.pallas_call(
        lambda *refs: add_split_kernel(len(ins) // 4, *refs),
        grid=(half // some,),
        out_shape=tuple(outs),
        in_specs=specs,
        out_specs=tuple(pl.BlockSpec((some,) + shape[1:], lambda i: (i, 0, 0)) for x in outs),
        compiler_params=pltpu.CompilerParams(vmem_limit_bytes=56 << 20),
        cost_estimate=pl.CostEstimate(
            flops=1, bytes_accessed=sum(6 * x.size for x in outs), transcendentals=0
        ),
    )(*ins)
    return list(out[::2]), list(out[1::2])


class Sum:
    def __init__(self, x, order):
        self.order, self.x = list(order), x

    def send(self):
        return self.x, self.order[0]

    def take(self, sent, other):
        self.order.pop(0)
        self.x = self.x + other


def exchange(count, *jobs, wait=()):
    sends = [job.send() for job in jobs]
    sent = lax.optimization_barrier(tuple(x for x, unused in sends) + tuple(wait))
    for job, x, (unused, mask) in zip(jobs, sent, sends):
        job.take(x, trade(x, mask, count))
    return sent[0]


def share_seq(x, seq_count, count):
    return jnp.concatenate([x] + [trade(x, m, count) for m in range(1, seq_count)], axis=0)


def windows(width):
    size = width // H
    for pair in range(H // 2):
        base = (pair // 2) * 4 * size + (pair % 2) * 128
        yield pair, base, (2 * pair * size - base, (2 * pair + 1) * size - base, (2 * pair + 2) * size - base)


def stacked(rows, edges):
    column = lax.broadcasted_iota(jnp.int32, rows.shape, 1)
    first = (column >= edges[0]) & (column < edges[1])
    second = (column >= edges[1]) & (column < edges[2])
    zero = jnp.zeros_like(rows)
    return jnp.concatenate([jnp.where(first, rows, zero), jnp.where(second, rows, zero)], axis=0)


def unstacked(both, edges):
    count = both.shape[0] // 2
    column = lax.broadcasted_iota(jnp.int32, (count, both.shape[1]), 1)
    first = (column >= edges[0]) & (column < edges[1])
    second = (column >= edges[1]) & (column < edges[2])
    return jnp.where(first, both[:count], jnp.where(second, both[count:], 0.0))


def masked_scores(seen, queries, keys, media_rows):
    scores = dot(queries, keys, ((1,), (1,)))
    place = lax.broadcasted_iota(jnp.int32, scores.shape, 1)
    return jnp.where((place < seen) | (place >= media_rows), scores, -1e30)


def attend_kernel(media_rows, seen_ref, q_ref, kv_ref, out_ref):
    count, width = q_ref.shape
    seen = seen_ref[0]
    lane = lax.broadcasted_iota(jnp.int32, (count, 128), 1)
    stats = jnp.zeros((count, 128), F32)
    carry = None
    for pair, base, edges in windows(width):
        cols, value_cols = slice(base, base + 256), slice(width + base, width + base + 256)
        scores = masked_scores(seen, stacked(q_ref[:, cols], edges), kv_ref[:, cols], media_rows)
        top = jnp.max(scores, axis=1, keepdims=True)
        probs = jnp.exp(scores - top)
        total = jnp.sum(probs, axis=1, keepdims=True)
        mixed = unstacked(dot(probs.astype(BF), kv_ref[:, value_cols]) / total, edges)
        if pair % 2 == 0:
            out_ref[:, base : base + 128] = mixed[:, :128].astype(BF)
            carry = mixed[:, 128:]
        else:
            out_ref[:, base : base + 128] = (carry + mixed[:, :128]).astype(BF)
            out_ref[:, base + 128 : base + 256] = mixed[:, 128:].astype(BF)
        for k in range(2):
            rows = slice(k * count, (k + 1) * count)
            for n, value in enumerate((top, total)):
                value = value[rows]
                for term in range(3):
                    low = value.astype(BF).astype(F32)
                    stats = jnp.where(lane == (3 * n + term) * H + 2 * pair + k, low, stats)
                    value = value - low
    out_ref[:, width:] = stats.astype(BF)


def attend_back_kernel(media_rows, pieces, seen_ref, q_ref, kv_ref, *refs):
    dq_ref, dkv_ref = refs[pieces:]
    count, width = q_ref.shape
    seen = seen_ref[0]
    lane = lax.broadcasted_iota(jnp.int32, (count, 128), 1)
    packed = jnp.concatenate([ref[...] for ref in refs[:pieces]], axis=0)
    stats = packed[:, width:].astype(F32)

    def column(at):
        parts = []
        for k in range(2):
            here = (lane == at + k) | (lane == at + H + k) | (lane == at + 2 * H + k)
            parts.append(jnp.sum(jnp.where(here, stats, 0.0), axis=1, keepdims=True))
        return jnp.concatenate(parts, axis=0)

    carry = None
    for pair, base, edges in windows(width):
        cols = slice(base, base + 256)
        queries, grads = stacked(q_ref[:, cols], edges), stacked(packed[:, cols], edges)
        keys, values = kv_ref[:, cols], kv_ref[:, width + base : width + base + 256]
        scores = masked_scores(seen, queries, keys, media_rows)
        probs = jnp.exp(scores - column(2 * pair))
        prob_grad = dot(grads, values, ((1,), (1,)))
        score_grad = (probs * (prob_grad - column(3 * H + 2 * pair))).astype(BF)
        new = (
            (dq_ref, 0, dot(score_grad, keys)),
            (dkv_ref, 0, dot(score_grad, queries, ((0,), (0,)))),
            (dkv_ref, width, dot(probs.astype(BF), grads, ((0,), (0,)))),
        )
        new = [(ref, at + base, unstacked(x, edges) if ref is dq_ref else x) for ref, at, x in new]
        if pair % 2 == 0:
            for ref, at, x in new:
                ref[:, at : at + 128] = x[:, :128].astype(BF)
            carry = [x[:, 128:] for unused_ref, unused_at, x in new]
        else:
            for (ref, at, x), old in zip(new, carry):
                ref[:, at : at + 128] = (old + x[:, :128]).astype(BF)
                ref[:, at + 128 : at + 256] = x[:, 128:].astype(BF)


def lane_heads(shape, width, dim):
    lane = lax.broadcasted_iota(jnp.int32, shape, dim)
    column = lax.broadcasted_iota(jnp.int32, shape, 1 - dim)
    size = width // H
    first = (lane % H) * size
    return lane // H, column - first, (column >= first) & (column < first + size)


def three_terms(x):
    terms = []
    for unused in range(3):
        terms.append(x.astype(BF))
        x = x - terms[-1].astype(F32)
    return terms


def combine_kernel(pieces, whole, me_ref, *refs):
    parts, refs = refs[:pieces], refs[pieces:]
    latent_ref, gain_ref, bias_ref, *refs = refs
    *refs, wide_ref, low_ref, stat_ref, hidden_ref, ffn_ref, w_ref, sems = refs
    waits = whole.fetch(me_ref[0], refs, w_ref, sems)
    rows, width = latent_ref.shape
    group, unused, inside = lane_heads((128, width), width, 0)
    spread_top = jnp.where(inside & (group < 3), 1.0, 0.0).astype(BF)
    spread_total = jnp.where(inside & (group >= 3) & (group < 6), 1.0, 0.0).astype(BF)
    tops = [dot(ref[:, width:], spread_top) for ref in parts]
    top = tops[0]
    for other in tops[1:]:
        top = jnp.maximum(top, other)
    total = jnp.zeros((rows, width), F32)
    mixed = jnp.zeros((rows, width), F32)
    for ref, mine in zip(parts, tops):
        weight = jnp.exp(mine - top) * dot(ref[:, width:], spread_total)
        total += weight
        mixed += weight * ref[:, :width].astype(F32)
    mixed = mixed / total
    wide_ref[...] = mixed
    low = mixed.astype(BF)
    low_ref[...] = low
    group, offset, unused = lane_heads((width, 128), width, 1)
    stats = jnp.zeros((rows, 128), F32)
    for k, term in enumerate(three_terms(top + jnp.log(total))):
        pick = jnp.where((group == k) & (offset == 0), 1.0, 0.0).astype(BF)
        stats += dot(term, pick)
    stat_ref[...] = stats
    for wait in waits:
        wait.wait()
    hidden = latent_ref[...].astype(F32) + dot(low, w_ref[...])
    hidden_ref[...] = hidden
    ffn_ref[...] = layer_norm(hidden, gain_ref[...], bias_ref[...])[0].astype(BF)


def hidden_back_kernel(whole, me_ref, *refs):
    keep_ref, other_ref, hidden_ref, upstream_ref, wide_ref, stat_ref, gain_ref, *refs = refs
    *refs, hidden_grad_ref, low_ref, packed_ref, sums_ref, w_ref, sems = refs
    waits = whole.fetch(me_ref[0], refs, w_ref, sems)
    rows, width = hidden_ref.shape
    grad = keep_ref[0].astype(F32) + other_ref[0].astype(F32)
    gain = gain_ref[...]
    unused, unit, rstd = layer_norm(hidden_ref[...], gain, gain)
    norm_grad, gain_grad, bias_grad = layer_norm_back(grad, unit, rstd, gain)
    row = lax.broadcasted_iota(jnp.int32, (8, width), 0)
    sums_ref[...] = jnp.where(row == 0, gain_grad[None], jnp.where(row == 1, bias_grad[None], 0.0))
    hidden_grad = upstream_ref[...].astype(F32) + norm_grad
    hidden_grad_ref[...] = hidden_grad
    low = hidden_grad.astype(BF)
    low_ref[...] = low
    for wait in waits:
        wait.wait()
    mixture_grad = dot(low, w_ref[...], ((1,), (1,))).astype(BF)
    packed_ref[:, :width] = mixture_grad
    group, unused, inside = lane_heads((width, 128), width, 1)
    heads = jnp.where(inside & (group >= 3) & (group < 6), 1.0, 0.0).astype(BF)
    inner = jnp.zeros((rows, 128), F32)
    for term in three_terms(wide_ref[...] * mixture_grad.astype(F32)):
        inner += dot(term, heads)
    lane = lax.broadcasted_iota(jnp.int32, (rows, 128), 1) // H
    stats = stat_ref[...]
    for k, term in enumerate(three_terms(inner)):
        stats = jnp.where(lane == 3 + k, term.astype(F32), stats)
    packed_ref[:, width:] = stats.astype(BF)


def owner_of(place, order):
    return sum(mask for k, mask in enumerate(order) if (place >> k) % 2)


def place_of(owner, order):
    return sum(((owner // mask) % 2) << k for k, mask in enumerate(order))


class Stacks:
    def __init__(self, parts, orders):
        self.each = len(parts[0])
        self.arrays = [x for pieces in parts for x in pieces]
        self.orders = orders
        self.cols = sum(pieces[0].shape[2] for pieces in parts)
        self.ends = [parts[0][0].shape[2] * (k + 1) for k in range(len(parts))]

    def fetch(self, me, refs, into, sems):
        at, waits = 0, []
        for k, order in enumerate(self.orders):
            pieces = refs[self.each * k : self.each * (k + 1)]
            some, block, cols = pieces[0].shape
            for place in range(self.each * some):
                owner = me ^ owner_of(place, order)
                to = into.at[pl.ds(pl.multiple_of(owner * block, 16), block), at : at + cols]
                source = pieces[place // some].at[place % some]
                pltpu.make_async_copy(source, to, sems.at[k]).start()
            part = into.at[:, at : at + cols]
            waits.append(pltpu.make_async_copy(part, part, sems.at[k]))
            at += cols
        return waits


class Plain:
    def __init__(self, x):
        self.arrays, self.orders = [x], (None,)
        self.cols = x.shape[1]
        self.ends = [self.cols]

    def fetch(self, me, refs, into, sems):
        copy = pltpu.make_async_copy(refs[0], into, sems.at[0])
        copy.start()
        return [copy]


def halves_kernel(me_ref, s_ref, mine_ref, other_ref):
    block = 48
    for parity in range(2):

        @pl.when(me_ref[0] % 2 == parity)
        def _():
            for out_ref, which in ((mine_ref, parity), (other_ref, 1 - parity)):
                for n in range(out_ref.shape[1] // block):
                    at = (2 * n + which) * block
                    out_ref[:, n * block : (n + 1) * block] = s_ref[:, at : at + block]


def order_kernel(whole, me_ref, *refs):
    *refs, out_ref, sems = refs
    for wait in whole.fetch(me_ref[0], refs, out_ref, sems):
        wait.wait()


def project_kernel(whole, me_ref, s_ref, *refs):
    *refs, out_ref, w_ref, sems = refs
    at = 0
    for wait, end in zip(whole.fetch(me_ref[0], refs, w_ref, sems), whole.ends):
        wait.wait()
        out_ref[:, at:end] = dot(s_ref[...], w_ref[:, at:end]).astype(BF)
        at = end


def gelu_parts(x):
    c = 0.7978845608028654
    t = jnp.tanh(c * (x + 0.044715 * (x * x * x)))
    slope = 0.5 * (1.0 + t) + 0.5 * x * (1.0 - t * t) * (c * (1.0 + 3 * 0.044715 * (x * x)))
    return 0.5 * x * (1.0 + t), slope


def ffn_kernel(
    order,
    me_ref,
    mine_ref,
    other_ref,
    up_ref,
    down_ref,
    all_ref,
    keep_ref,
    send_ref,
    active_ref,
    pre_ref,
    rows_ref,
    grad_rows_ref,
    sem,
):
    some, each, width = mine_ref.shape
    for place in range(2 * some):
        owner = me_ref[0] ^ owner_of(place, order)
        pltpu.make_async_copy(
            all_ref.at[owner, :, width : 2 * width],
            grad_rows_ref.at[place * each : (place + 1) * each],
            sem,
        ).start()
    rows_ref[: some * each, :] = mine_ref[...].reshape(some * each, width)
    rows_ref[some * each :, :] = other_ref[...].reshape(some * each, width)
    active, slope = gelu_parts(dot(rows_ref[...], up_ref[...]))
    active_ref[...] = active.astype(BF)
    pltpu.make_async_copy(grad_rows_ref, grad_rows_ref, sem).wait()
    pre_grad = (dot(grad_rows_ref[...], down_ref[...], ((1,), (1,))) * slope).astype(BF)
    pre_ref[...] = pre_grad
    total = dot(pre_grad, up_ref[...], ((1,), (1,)))
    keep_ref[...] = total[: some * each].reshape(keep_ref.shape)
    send_ref[...] = total[some * each :].astype(BF).reshape(send_ref.shape)


def ffn_sums_kernel(
    rows_ref,
    grad_rows_ref,
    active_ref,
    pre_ref,
    down_ref,
    down_keep_ref,
    down_send_ref,
    up_ref,
    keep_ref,
    send_ref,
):
    first = ((0,), (0,))
    units = down_keep_ref.shape[0]
    down = dot(active_ref[...], grad_rows_ref[...], first)
    down_keep_ref[...] = down[:units]
    down_send_ref[...] = down[units:].astype(BF)
    up_ref[...] = dot(rows_ref[...], pre_ref[...], first).astype(BF)
    out = dot(active_ref[...], down_ref[...])
    half = out.shape[0] // 2
    keep_ref[...] = out[:half].reshape(keep_ref.shape)
    send_ref[...] = out[half:].astype(BF).reshape(send_ref.shape)


def source_kernel(whole, me_ref, g_ref, media_ref, time_ref, gain_ref, *refs):
    *refs, media_grad_ref, latent_ref, sums_ref, acc_ref, w_ref, sems = refs
    at = 0
    for wait, end in zip(whole.fetch(me_ref[0], refs, w_ref, sems), whole.ends):
        wait.wait()
        new = dot(g_ref[:, at:end], w_ref[:, at:end], ((1,), (1,)))
        acc_ref[...] = acc_ref[...] + new if at else new
        at = end
    media_rows, width = media_ref.shape
    gain = gain_ref[...]
    rows = [jnp.zeros((1, width), F32), jnp.zeros((1, width), F32)]
    for frame in range(media_rows // PATCH):
        here = slice(frame * PATCH, (frame + 1) * PATCH)
        shifted = media_ref[here, :].astype(F32) + time_ref[frame : frame + 1, :]
        unused, unit, rstd = layer_norm(shifted, gain, gain)
        grad = acc_ref[here, :]
        shifted_grad, gain_grad, bias_grad = layer_norm_back(grad, unit, rstd, gain)
        media_grad_ref[here, :] = shifted_grad.astype(BF)
        rows[0] += gain_grad[None]
        rows[1] += bias_grad[None]
        rows.append(jnp.sum(shifted_grad, axis=0, keepdims=True))
    at = lax.broadcasted_iota(jnp.int32, sums_ref.shape, 0)
    sums = jnp.zeros(sums_ref.shape, F32)
    for k, row in enumerate(rows):
        sums = jnp.where(at == k, row, sums)
    sums_ref[...] = sums
    latent_ref[...] = acc_ref[media_rows:, :]


def latent_kernel(pieces, scaling, *refs):
    parts, refs = refs[:pieces], refs[pieces:]
    source_ref, latent_ref, gain_ref, hidden_grad_ref, out_ref, sums_ref = refs
    gain = gain_ref[...]
    width = gain.shape[1]
    query_side = sum(ref[:, :width].astype(F32) for ref in parts)
    grad = source_ref[...] + query_side * scaling
    unused, unit, rstd = layer_norm(latent_ref[...].astype(F32), gain, gain)
    latent_grad, gain_grad, bias_grad = layer_norm_back(grad, unit, rstd, gain)
    out_ref[...] = (hidden_grad_ref[...] + latent_grad).astype(BF)
    at = lax.broadcasted_iota(jnp.int32, sums_ref.shape, 0)
    sums_ref[...] = jnp.where(
        at == 0, gain_grad[None], jnp.where(at == 1, bias_grad[None], 0.0)
    )


def sums_kernel(orders, me_ref, s_ref, s2_ref, g_ref, g2_ref, *refs):
    *out_refs, s_held, g_held, held, sems = refs
    me = me_ref[0] - me_ref[0] % 2
    half, block, cols = out_refs[0].shape
    rows = s_ref.shape[0]
    for k, ref in enumerate((s_ref, s2_ref)):
        pltpu.make_async_copy(ref, s_held.at[k * rows : (k + 1) * rows], sems.at[0]).start()
    for part in range(len(orders)):
        columns = slice(part * cols, (part + 1) * cols)
        for k, ref in enumerate((g_ref, g2_ref)):
            to = g_held.at[k * rows : (k + 1) * rows, columns]
            pltpu.make_async_copy(ref.at[:, columns], to, sems.at[1 + part]).start()
    pltpu.make_async_copy(s_held, s_held, sems.at[0]).wait()
    some = held.shape[0]
    for part, order in enumerate(orders):
        columns = slice(part * cols, (part + 1) * cols)
        here = g_held.at[:, columns]
        pltpu.make_async_copy(here, here, sems.at[1 + part]).wait()
        first = (me // order[-1]) % 2
        for start in range(0, 2 * half, some):
            full = dot(s_held[:, start * block : (start + some) * block], here[...], ((0,), (0,)))
            held[...] = full.astype(BF).reshape(held.shape)
            for bit in range(2):

                @pl.when(first == bit)
                def _(bit=bit, start=start, part=part, order=order):
                    for n in range(some):
                        owner = 2 * (start + n)
                        place = place_of(owner ^ me, order) % half
                        send = (owner // order[-1]) % 2 != bit
                        out_refs[2 * part + send][place] = held[n]


SCALAR = pl.BlockSpec(memory_space=pltpu.SMEM)
FAR = pl.BlockSpec(memory_space=pl.ANY)


def call(kernel, inputs, outputs, flops, specs=(), far_outputs=False, scratch=()):
    specs = dict(specs)

    def whole(x):
        return pl.BlockSpec(x.shape, lambda i, nd=len(x.shape): (0,) * nd)

    nbytes = sum(x.size * x.dtype.itemsize for x in inputs)
    nbytes += sum(x.size * x.dtype.itemsize for x in outputs)
    return pl.pallas_call(
        kernel,
        grid=(1,),
        out_shape=tuple(outputs),
        in_specs=[specs.get(n, whole(x)) for n, x in enumerate(inputs)],
        out_specs=tuple(FAR if far_outputs else whole(x) for x in outputs),
        scratch_shapes=list(scratch),
        compiler_params=pltpu.CompilerParams(vmem_limit_bytes=56 << 20),
        cost_estimate=pl.CostEstimate(flops=flops, bytes_accessed=nbytes, transcendentals=0),
    )(*inputs)


def shards(
    media,
    latents,
    frames,
    time_embed,
    media_gain,
    media_bias,
    latent_gain,
    latent_bias,
    ffn_gain,
    ffn_bias,
    w_query,
    w_key,
    w_value,
    w_out,
    w_up,
    w_down,
    grad_out,
):
    item_count, seq_count = lax.axis_size("items"), lax.axis_size("seq")
    count = item_count * seq_count
    seq_index = lax.axis_index("seq")
    me = lax.axis_index("items") * seq_count + seq_index
    unused_items, media_rows, width = media.shape
    latent_rows = latents.shape[1]
    head_size = width // H
    frames_here = media_rows // PATCH
    scaling = head_size ** (-0.5)

    bits = [1 << k for k in reversed(range(30))]
    item_bits = [m for m in bits if seq_count <= m < count]
    seq_bits = [m for m in bits if m < seq_count]
    head, (fold, near), side, tail = item_bits[:-2], item_bits[-2:], seq_bits[0], seq_bits[1:]
    orders = (
        head + [fold, near, side] + tail,
        head + [side, fold, near] + tail,
        head + [near, side, fold] + tail,
    )
    ffn_order = head + [near, side] + tail
    block = width // count
    regular = block % 16 == 0

    def share(x):
        return jax.ShapeDtypeStruct(x, BF)

    latent_in = latents[0].astype(F32)
    latent_normed, latent_unit, latent_rstd = layer_norm(latent_in, latent_gain, latent_bias)
    latent_normed = latent_normed.astype(BF)
    time_rows = lax.dynamic_slice_in_dim(time_embed, seq_index * frames_here, frames_here, 0)
    shifted = (
        media[0].astype(F32).reshape(frames_here, PATCH, width) + time_rows[:, None, :]
    ).reshape(media_rows, width)
    media_normed, media_unit, media_rstd = layer_norm(shifted, media_gain, media_bias)
    sources = jnp.concatenate([media_normed.astype(BF), latent_normed], axis=0)

    def spread(x):
        x = x.reshape(x.shape[0], count, -1).transpose(1, 0, 2)
        pairs = x.reshape(-1, 2, fold, *x.shape[1:])
        pairs = jnp.concatenate([pairs[:, 1:], pairs[:, :1]], axis=1).reshape(x.shape)
        x = jnp.concatenate([x, pairs], axis=2)
        x = lax.all_to_all(x, AXES, split_axis=0, concat_axis=0, tiled=True)
        return x.reshape(-1, x.shape[2])

    cols_here = width // seq_count

    def seq_blocks(x, axis):
        return jnp.concatenate(
            [
                lax.dynamic_index_in_dim(x, seq_index ^ t, 0, keepdims=False)
                for t in range(seq_count)
            ],
            axis=axis,
        )

    def columns_of(x, m):
        return lax.dynamic_slice_in_dim(x, (seq_index ^ m) * cols_here, cols_here, 1)

    def reordered(x, m):
        blocks = x.reshape(seq_count, latent_rows, x.shape[1])
        return jnp.concatenate([blocks[t ^ m] for t in range(seq_count)], axis=0)

    parts = len(orders)
    units = w_down.shape[0]
    out_orders = (orders[0], head + [fold, side, near] + tail)
    if regular:
        first = GatherRel(jnp.concatenate([w_key, w_value], axis=1)[None], head)
        second = GatherRel(w_out[None], head + [fold])

        def split(x, orders, done):
            cols = x.shape[2] // len(orders)
            return [
                GatherApart(x[..., k * cols : (k + 1) * cols], order[done:])
                for k, order in enumerate(orders)
            ]

        down_job = GatherRel(w_down[None], [fold])
        started = exchange(count, first, down_job)
        while first.order:
            exchange(count, first)
        latent_item = share_seq(latent_normed, seq_count, count)
        pieces = [columns_of(w_query, m) for m in range(seq_count)]
        pieces = [pieces[0]] + [trade(pieces[m], m, count) for m in range(1, seq_count)]
        query_cols = Gather(
            seq_blocks(jnp.stack(pieces), 0), head + [near, fold], me
        )
        first = split(first.x, orders, len(head))
        started = exchange(count, *first, second, query_cols, wait=(down_job.x,))
        rows_all = lax.all_gather(
            jnp.concatenate([after(latent_normed, started), grad_out[0]], axis=1), AXES, axis=0
        )
        exchange(count, *first, second, query_cols)
        second = split(second.x, out_orders, len(head) + 1)
        started = exchange(count, *first)
        half_mine, half_other = call(
            halves_kernel,
            (me[None], after(sources, started)),
            (share((sources.shape[0], width // 2)),) * 2,
            0,
            specs={0: SCALAR},
        )
        half_other = trade(half_other, 1, count)
        for job in first:
            job.last(count, half_other)
        ready = [piece for job in first for piece in job.x]
        exchange(count, *second, query_cols, wait=ready)
        started = exchange(count, *second)
        up_pair = spread(after(w_up, *ready))
        key_value = Stacks([job.x for job in first], orders)
    else:
        started = w_key
        up_pair = spread(w_up)
        rows_all = lax.all_gather(
            jnp.concatenate([latent_normed, grad_out[0]], axis=1), AXES, axis=0
        )
        latent_item = share_seq(latent_normed, seq_count, count)
        pieces = [columns_of(w_query, m) for m in range(seq_count)]
        pieces = [pieces[0]] + [trade(pieces[m], m, count) for m in range(1, seq_count)]
        query_cols = Gather(seq_blocks(jnp.stack(pieces), 0), item_bits, me)
        down_job = GatherRel(w_down[None], [fold])
        exchange(count, down_job)
        both = lax.all_gather(jnp.concatenate([w_key, w_value], 1), AXES, axis=0, tiled=True)
        key_value = Plain(both)
        out_full = Plain(lax.all_gather(w_out, AXES, axis=0, tiled=True))

    def with_weights(kernel, inputs, whole, outputs, flops, keep=True, scratch=()):
        inputs = [me[None]] + list(inputs)
        specs = {0: SCALAR}
        for n in range(len(whole.arrays)):
            specs[len(inputs) + n] = FAR
        scratch = list(scratch) + ([pltpu.VMEM((width, whole.cols), BF)] if keep else [])
        return call(
            lambda *refs: kernel(whole, *refs),
            (*inputs, *whole.arrays),
            outputs,
            flops,
            specs=specs,
            scratch=scratch + [pltpu.SemaphoreType.DMA((len(whole.orders),))],
        )

    source_count = sources.shape[0]
    keys = with_weights(
        project_kernel,
        (sources,),
        key_value,
        (share((source_count, 2 * width)),),
        4 * source_count * width * width,
    )[0]
    while query_cols.order:
        exchange(count, query_cols)
    query_slice = query_cols.x.reshape(width, cols_here)
    query_mine = (dot(latent_item, query_slice) * scaling).astype(BF)
    sends = [reordered(query_mine, m) for m in range(1, seq_count)]
    *sends, keys = lax.optimization_barrier((*sends, keys))
    pieces = [query_mine] + [trade(x, m + 1, count) for m, x in enumerate(sends)]
    queries = seq_blocks(jnp.stack(pieces), 1)
    down_pair = down_job.x.reshape(-1, width)
    if regular:
        for job in second:
            job.last(count, keys)
        out_full = Stacks([job.x for job in second], out_orders)

    seen = jnp.clip((frames - seq_index * frames_here) * PATCH, 0, media_rows).astype(jnp.int32)
    all_rows = queries.shape[0]
    pair_flops = 2 * H // 2 * 2 * all_rows * 256 * sources.shape[0]
    mixed = call(
        lambda *refs: attend_kernel(media_rows, *refs),
        (seen, queries, keys),
        (share((all_rows, width + 128)),),
        2 * pair_flops,
        specs={0: SCALAR},
    )[0]

    def own_parts(x):
        blocks = x.reshape(seq_count, latent_rows, x.shape[1])
        return [blocks[0]] + [trade(blocks[m], m, count) for m in range(1, seq_count)]


    rows_wide = jax.ShapeDtypeStruct((latent_rows, width), F32)
    rows_low = jax.ShapeDtypeStruct((latent_rows, width), BF)
    mixture_wide, mixture, log_total, hidden, ffn_in = with_weights(
        lambda *refs: combine_kernel(seq_count, *refs),
        (*own_parts(mixed), latents[0], ffn_gain[None], ffn_bias[None]),
        out_full,
        (
            rows_wide,
            rows_low,
            jax.ShapeDtypeStruct((latent_rows, 128), F32),
            rows_wide,
            rows_low,
        ),
        2 * latent_rows * width * width,
    )
    mixture_all = lax.all_gather(mixture, AXES, axis=0, tiled=True)

    ffn_rows = GatherRel(ffn_in[None], ffn_order)
    while len(ffn_rows.order) > 1:
        exchange(count, ffn_rows)
    mine = ffn_rows.x
    other = trade(mine, ffn_order[-1], count)
    some = mine.shape[0]
    all_ffn = 2 * some * latent_rows
    units_low = share((all_ffn, 2 * units))
    halves = (jax.ShapeDtypeStruct(mine.shape, F32), share(mine.shape))
    ffn_flops = 2 * all_ffn * 2 * units * width
    keep, send, active, pre, ffn_all, grad_all = call(
        lambda *refs: ffn_kernel(ffn_order, *refs),
        (me[None], mine, other, up_pair, down_pair, rows_all),
        (*halves, units_low, units_low, *(share((all_ffn, width)),) * 2),
        3 * ffn_flops,
        specs={0: SCALAR, 5: FAR},
        scratch=(pltpu.SemaphoreType.DMA(()),),
    )
    back = Halves([keep], [send], [ffn_order])
    back.step(count)
    back.split()
    back.step(count)
    down_keep, down_send, up_sums, keep, send = call(
        ffn_sums_kernel,
        (ffn_all, after(grad_all, back.token), active, pre, down_pair),
        (
            jax.ShapeDtypeStruct((units, width), F32),
            share((units, width)),
            share((width, 2 * units)),
            *halves,
        ),
        3 * ffn_flops,
    )
    result = Halves([keep], [send], [ffn_order])
    back.split()
    back.step(count, (down_send,))
    while back.orders[0]:
        back.split()
        back.step(count)

    hidden_grad, attended_low, packed, ffn_sums = with_weights(
        hidden_back_kernel,
        (
            back.keep[0],
            back.others[0],
            hidden,
            grad_out[0],
            mixture_wide,
            log_total,
            ffn_gain[None],
        ),
        out_full,
        (
            rows_wide,
            rows_low,
            share((latent_rows, width + 128)),
            jax.ShapeDtypeStruct((8, width), F32),
        ),
        2 * latent_rows * width * width,
    )
    down_other = trade(after(down_send, packed), fold, count)
    up_blocks = after(up_sums, packed).reshape(count, -1, 2 * units)
    up_blocks = lax.all_to_all(up_blocks, AXES, split_axis=0, concat_axis=0, tiled=True)
    pieces = [packed] + [trade(packed, m, count) for m in range(1, seq_count)]
    query_part, row_grad = call(
        lambda *refs: attend_back_kernel(media_rows, seq_count, *refs),
        (seen, queries, keys, *pieces),
        (share((all_rows, width)), share(keys.shape)),
        5 * pair_flops,
        specs={0: SCALAR},
    )
    sends = [reordered(columns_of(query_part, m), m) for m in range(seq_count)]
    row_send, mixture_all, *sends = lax.optimization_barrier((row_grad, mixture_all, *sends))
    row_other = trade(row_send, 1, count)
    pieces = [sends[0]] + [trade(sends[m], m, count) for m in range(1, seq_count)]
    row_other, *pieces = lax.optimization_barrier((row_other, *pieces))
    query_cols_grad = sum(x.astype(F32) for x in pieces).astype(BF)
    query_side = dot(query_cols_grad, query_slice, ((1,), (1,))).astype(BF)
    query_side = own_parts(jnp.concatenate([query_side, query_cols_grad], axis=1))
    query_rows = seq_blocks(jnp.stack([x[:, width:] for x in query_side]), 1)
    rows = lax.all_gather(
        jnp.concatenate([attended_low, query_rows], axis=1), AXES, axis=0, tiled=True
    )

    cols = 2 * width // parts
    result.step(count, (query_side[1],))
    if regular:
        place = share((count // 4, block, cols))
        outs = call(
            lambda *refs: sums_kernel([order[:-1] for order in orders], *refs),
            (me[None], half_mine, half_other, row_grad, row_other),
            (place,) * (2 * parts),
            4 * width * width * source_count,
            specs={0: SCALAR, 1: FAR, 2: FAR, 3: FAR, 4: FAR},
            scratch=(
                pltpu.VMEM((2 * source_count, width // 2), BF),
                pltpu.VMEM((2 * source_count, 2 * width), BF),
                pltpu.VMEM((8, block, cols), BF),
                pltpu.SemaphoreType.DMA((1 + parts,)),
            ),
        )
        weights = Halves(outs[::2], outs[1::2], [order[:-1] for order in orders])
        weights.step(count, query_side[1:])
        started = weights.token
    else:
        full = dot(sources, row_grad, ((0,), (0,))).astype(BF)
        full = lax.psum_scatter(full, AXES, scatter_dimension=0, tiled=True).astype(F32)
        started = query_rows
    result.split()
    result.step(count, (started,))

    media_grad, latent_source, media_sums = with_weights(
        source_kernel,
        (after(row_grad, started), media[0], time_rows, media_gain[None]),
        key_value,
        (
            share((media_rows, width)),
            jax.ShapeDtypeStruct((latent_rows, width), F32),
            jax.ShapeDtypeStruct((8, width), F32),
        ),
        4 * source_count * width * width,
        scratch=[pltpu.VMEM((source_count, width), F32)],
    )
    latents_grad, latent_sums = call(
        lambda *refs: latent_kernel(seq_count, scaling, *refs),
        (*query_side, latent_source, latents[0], latent_gain[None], hidden_grad),
        (rows_low, jax.ShapeDtypeStruct((8, width), F32)),
        2 * latent_rows * width * width,
    )
    time_local = lax.dynamic_update_slice_in_dim(
        jnp.zeros((FRAMES, width), F32),
        media_sums[2 : 2 + frames_here],
        seq_index * frames_here,
        0,
    )
    sums = Sum(
        jnp.concatenate(
            [
                time_local,
                media_sums[:2],
                latent_sums[:2],
                ffn_sums[:2],
                jnp.zeros((2, width), F32),
            ],
            axis=0,
        ),
        [near, fold] + head + seq_bits,
    )
    if regular:
        while weights.orders[0]:
            weights.split()
            weights.step(count)
            if result.orders[0]:
                result.split()
                result.step(count, (weights.token,))
            if sums.order:
                exchange(count, sums, wait=(weights.token,))
        full = jnp.concatenate([x[0] for x in weights.total()], axis=1)
    while result.orders[0]:
        result.split()
        result.step(count)
    down_grad = down_keep + down_other.astype(F32)
    up_blocks = up_blocks.reshape(-1, 2, fold, width // count, 2 * units).astype(F32)
    swapped = jnp.concatenate([up_blocks[:, 1:], up_blocks[:, :1]], axis=1)
    up_grad = up_blocks[..., :units] + swapped[..., units:]
    up_grad = up_grad.reshape(count, -1, units).transpose(1, 0, 2).reshape(-1, count * units)
    while sums.order:
        exchange(count, sums)
    sums = sums.x
    latents_out = hidden + result.total()[0][0]

    def my_columns(x):
        return lax.dynamic_slice_in_dim(x, me * block, block, 1)

    out_grad = dot(my_columns(mixture_all), rows[:, :width], ((0,), (0,)))
    latent_all = my_columns(rows_all.reshape(-1, 2 * width))
    query_grad = dot(latent_all, rows[:, width : 2 * width], ((0,), (0,))) * scaling
    return (
        latents_out.astype(BF)[None],
        latents_grad[None],
        media_grad[None],
        sums[:FRAMES],
        sums[FRAMES],
        sums[FRAMES + 1],
        sums[FRAMES + 2],
        sums[FRAMES + 3],
        sums[FRAMES + 4],
        sums[FRAMES + 5],
        query_grad,
        full[:, :width],
        full[:, width:],
        out_grad,
        up_grad,
        down_grad,
    )


def solution(mesh):
    rows, split = P("items", "seq", None), P(AXES, None)
    return jax.shard_map(
        shards,
        mesh=mesh,
        in_specs=(rows, rows, P("items")) + (P(),) * 7 + (split,) * 6 + (rows,),
        out_specs=(rows,) * 3 + (P(),) * 7 + (split,) * 6,
        check_vma=False,
    )
```

time: 544 us -> 425 us (0.78)
  Pallas kernels: 6.88 us -> 98.5 us
  waiting for transfers between devices: 232 us -> 159 us
  starting transfers between devices: 134 us -> 78.3 us
  matrix products: 50.9 us -> 7.05 us
  local copies, waits for them, and re-layouts: 62.8 us -> 34.1 us
  other arithmetic: 42.4 us -> 24.2 us
  between operations: 4.31 us -> 15.9 us
    pallas_call x2 -> x20, Pallas kernels: 6.88 us -> 98.5 us  [the longest x11 77.6 us: call(): pl.pallas_call(kernel, grid=(1,), out_shape=tuple(outputs), in_specs=[spe...]
    ppermute x133 -> x83, waiting for transfers between devices: 232 us -> 159 us  [trade(): return lax.ppermute(x, AXES, [(i, i ^ mask) for i in range(count)])]
    ppermute x133 -> x83, starting transfers between devices: 124 us -> 72 us  [trade(): return lax.ppermute(x, AXES, [(i, i ^ mask) for i in range(count)])]
    dot_general x18 -> x4, matrix products: 50.9 us -> 7.05 us  [dot(): return lax.dot_general(a, b, (dims, ((), ())), preferred_element_type=F32)]
    unnamed x250 -> x153, local copies, waits for them, and re-layouts: 29.9 us -> 16.5 us
    select_n x36 -> x3, other arithmetic: 12.2 us -> 0.35 us  [take(): jnp.where(self.me & mask != 0, jnp.concatenate([other, mine], axis), jnp....]
    add x30 -> x7, other arithmetic: 12.7 us -> 1.68 us  [the longest x1 1.14 us: shards(): down_grad = down_keep + down_other.astype(F32)]
    convert_element_type x16 -> x0, local copies, waits for them, and re-layouts: 9.7 us -> none  [the longest x10 4.02 us: scatter_abs(): x = keep.astype(F32) + trade(send.astype(BF), mask, count).astype(F32)]
  transfers between devices with their start and end apart: 135 -> 88, of which waited for: 55 -> 41; matrix products, arithmetic and copies ran while one was open for 26% -> 10% of each run, Pallas kernels for 1% -> 24%
where the time goes in v2:
time: 425 us; the launch traced here: 417 us
  waiting for transfers between devices  159 us (37%)
  Pallas kernels  98.5 us (23%)
  starting transfers between devices  78.3 us (18%)
  local copies, waits for them, and re-layouts  34.1 us (8%)
  other arithmetic  24.2 us (6%)
  between operations  15.9 us (4%)
  matrix products  7.05 us (2%)
    ppermute x83, waiting for transfers between devices, trade(): return lax.ppermute(x, AXES, [(i, i ^ mask) for i in range(count)])  159 us
    pallas_call x11, Pallas kernels, call(): pl.pallas_call(kernel, grid=(1,), out_shape=tuple(outputs), in_specs=[spe...  77.6 us
    ppermute x83, starting transfers between devices, trade(): return lax.ppermute(x, AXES, [(i, i ^ mask) for i in range(count)])  72 us
    pallas_call x9, Pallas kernels, add_split(): pl.pallas_call(lambda *refs: add_split_kernel(len(ins) // 4, *refs), grid...  20.8 us
    unnamed x153, local copies, waits for them, and re-layouts  16.5 us
  transfers between devices with their start and end apart: 88, of which 41 were waited for; matrix products, arithmetic and copies ran while one was open for 10% of the time, Pallas kernels for 24%

profile of v2, /device:TPU:0, one launch (start us, length us, event | category | flops | bytes accessed | tf_op | source)
XLA Modules:
  0.0 416.8 jit_solution(14894586446940180042)
XLA Ops:
  9.0 4.0 collective-permute-start.3
  24.4 2.4 collective-permute-done.3
  27.8 9.4 %collective-permute-done.7 = bf16[1,192,1536]{2,1,0:T(8,128)(2,1)} collective-permute-done((bf16[1,192,1536]{2,1,0:T(8,128)(2,1)}, bf16[1,192,1536]{2,1,0:T(8,128)(2,1)}, u32[]{:S(2)}, u32[]{:S(2)}) %collective-permute-start.7) | collective-permute-done | bytes 589856 | tf_op jit(solution)/shard_map/ppermute | solution.py:36
  39.7 2.5 collective-permute-start.8
  45.1 2.4 collective-permute-done.11
  47.6 6.1 %collective-permute-done.12 = bf16[192,384]{1,0:T(8,128)(2,1)S(1)} collective-permute-done((bf16[192,384]{1,0:T(8,128)(2,1)S(1)}, bf16[192,384]{1,0:T(8,128)(2,1)S(1)}, u32[]{:S(2)}, u32[]{:S(2)}) %collective-permute-start.12) | collective-permute-done | bytes 147488 | tf_op jit(solution)/shard_map/ppermute | solution.py:36
  55.5 2.1 pad_maximum_fusion.s_ref.refs_1_
  60.2 4.1 collective-permute-done.15
  64.4 3.6 collective-permute-done.16
  70.0 5.1 %shard_map.288 = (bf16[528,768]{1,0:T(8,128)(2,1)}, bf16[528,768]{1,0:T(8,128)(2,1)}) custom-call(s32[1]{0:T(128)} %bitcast.me_ref.refs_0_, bf16[528,1536]{1,0:T(8,128)(2,1)} %pad_maximum_fusion.s_ref.refs_1_), custom_call_target="tpu_custom_call" | custom-call | bytes 3244036 | tf_op jit(solution)/shard_map/pallas_call | solution.py:582
  77.1 19.4 %collective-permute-done.18.refs_3_.refs_6_ = bf16[8,48,1024]{2,1,0:T(8,128)(2,1)S(1)} collective-permute-done((bf16[8,48,1024]{2,1,0:T(8,128)(2,1)S(1)}, bf16[8,48,1024]{2,1,0:T(8,128)(2,1)S(1)}, u32[]{:S(2)}, u32[]{:S(2)}) %collective-permute-start.18) | collective-permute-done | bytes 786464 | tf_op jit(solution)/shard_map/ppermute | solution.py:36
  101.0 8.9 %collective-permute-done.13 = bf16[2,48,1536]{2,1,0:T(8,128)(2,1)S(1)} collective-permute-done((bf16[2,48,1536]{2,1,0:T(8,128)(2,1)S(1)}, bf16[2,48,1536]{2,1,0:T(8,128)(2,1)S(1)}, u32[]{:S(2)}, u32[]{:S(2)}) %collective-permute-start.13) | collective-permute-done | bytes 294944 | tf_op jit(solution)/shard_map/ppermute | solution.py:36
  114.7 2.5 collective-permute-start.35
  118.7 10.7 %shard_map.289.refs_2_ = bf16[528,3072]{1,0:T(8,128)(2,1)} custom-call(s32[1]{0:T(128)} %bitcast.me_ref.refs_0_, bf16[528,1536]{1,0:T(8,128)(2,1)} %pad_maximum_fusion.s_ref.refs_1_, bf16[8,48,1024]{2,1,0:T(8,128)(2,1)} %copy-done.27, bf16[8,48,1024]{2,1,0:T(8,128)(2,1)} %copy-done.61, bf16[8,48,1024]{2,1,0:T(8,128)(2,1)} %collective-permute-done.20.refs_4_.refs_7_, ...), custom_call_target="tpu_custom_call" | custom-call | flops 4982833152 | bytes 14303236 | tf_op jit(solution)/shard_map/pallas_call | solution.py:582
  139.7 3.1 all-to-all-start
  142.9 4.9 %collective-permute-done.31 = bf16[64,384]{1,0:T(8,128)(2,1)} collective-permute-done((bf16[64,384]{1,0:T(8,128)(2,1)}, bf16[64,384]{1,0:T(8,128)(2,1)}, u32[]{:S(2)}, u32[]{:S(2)}) %collective-permute-start.31) | collective-permute-done | bytes 49184 | tf_op jit(solution)/shard_map/ppermute | solution.py:36
  147.8 7.1 %collective-permute-done.30 = bf16[64,384]{1,0:T(8,128)(2,1)} collective-permute-done((bf16[64,384]{1,0:T(8,128)(2,1)}, bf16[64,384]{1,0:T(8,128)(2,1)}, u32[]{:S(2)}, u32[]{:S(2)}) %collective-permute-start.30) | collective-permute-done | bytes 49184 | tf_op jit(solution)/shard_map/ppermute | solution.py:36
  156.6 5.8 %shard_map.290 = bf16[64,1664]{1,0:T(8,128)(2,1)} custom-call(s32[1]{0:T(128)S(6)} %min.6.refs_0_, bf16[64,1536]{1,0:T(8,128)(2,1)} %pad_maximum_fusion.17.refs_1_, bf16[528,3072]{1,0:T(8,128)(2,1)} %shard_map.289.refs_2_), custom_call_target="tpu_custom_call" | custom-call | flops 553648128 | bytes 3653636 | tf_op jit(solution)/shard_map/pallas_call | solution.py:582
  166.6 3.8 collective-permute-start.33
  170.4 2.4 collective-permute-done.33.refs_3_
  177.9 4.9 %shard_map.291 = (f32[16,1536]{1,0:T(8,128)}, bf16[16,1536]{1,0:T(8,128)(2,1)}, f32[16,128]{1,0:T(8,128)}, f32[16,1536]{1,0:T(8,128)}, bf16[16,1536]{1,0:T(8,128)(2,1)}) custom-call(s32[1]{0:T(128)} %bitcast.me_ref.refs_0_, bf16[16,1664]{1,0:T(8,128)(2,1)} %get-tuple-element.314.refs_1_, bf16[16,1664]{1,0:T(8,128)(2,1)} %copy-done.45, ...), custom_call_target="tpu_custom_call" | custom-call | flops 75497472 | bytes 5296132 | tf_op jit(solution)/shard_map/pallas_call | solution.py:582
  184.8 4.1 collective-permute-done.43
  189.8 4.6 %collective-permute-done.44 = bf16[2,16,1536]{2,1,0:T(8,128)(2,1)S(1)} collective-permute-done((bf16[2,16,1536]{2,1,0:T(8,128)(2,1)S(1)}, bf16[2,16,1536]{2,1,0:T(8,128)(2,1)S(1)}, u32[]{:S(2)}, u32[]{:S(2)}) %collective-permute-start.44) | collective-permute-done | bytes 98336 | tf_op jit(solution)/shard_map/ppermute | solution.py:36
  195.7 4.5 %collective-permute-done.45 = bf16[4,16,1536]{2,1,0:T(8,128)(2,1)S(1)} collective-permute-done((bf16[4,16,1536]{2,1,0:T(8,128)(2,1)S(1)}, bf16[4,16,1536]{2,1,0:T(8,128)(2,1)S(1)}, u32[]{:S(2)}, u32[]{:S(2)}) %collective-permute-start.45) | collective-permute-done | bytes 196640 | tf_op jit(solution)/shard_map/ppermute | solution.py:36
  203.2 5.1 %shard_map.292 = (f32[8,16,1536]{2,1,0:T(8,128)}, bf16[8,16,1536]{2,1,0:T(8,128)(2,1)}, bf16[256,384]{1,0:T(8,128)(2,1)}, bf16[256,384]{1,0:T(8,128)(2,1)}, bf16...) custom-call(s32[1]{0:T(128)} %bitcast.me_ref.refs_0_, bf16[8,16,1536]{2,1,0:T(8,128)(2,1)} %copy-done.19, ...), custom_call_target="tpu_custom_call" | custom-call | flops 905969664 | bytes 9437188 | tf_op jit(solution)/shard_map/pallas_call | solution.py:582
  214.3 4.4 %shard_map.294 = (f32[192,1536]{1,0:T(8,128)}, bf16[192,1536]{1,0:T(8,128)(2,1)}, bf16[1536,384]{1,0:T(8,128)(2,1)}, f32[8,16,1536]{2,1,0:T(8,128)}, bf16[8,16,1536]{2,1,0:T(8,128)(2,1)}) custom-call(bf16[256,1536]{1,0:T(8,128)(2,1)} %get-tuple-element.193.rows_ref, bf16[256,1536]{1,0:T(8,128)(2,1)} %get-tuple-element.198.grad_rows_ref, ...), custom_call_target="tpu_custom_call" | custom-call | flops 905969664 | bytes 7274496 | tf_op jit(solution)/shard_map/pallas_call | solution.py:582
  223.5 5.9 %collective-permute-done.49.refs_2_.refs_3_ = bf16[2,16,1536]{2,1,0:T(8,128)(2,1)S(1)} collective-permute-done((bf16[2,16,1536]{2,1,0:T(8,128)(2,1)}, bf16[2,16,1536]{2,1,0:T(8,128)(2,1)S(1)}, u32[]{:S(2)}, u32[]{:S(2)}) %collective-permute-start.49) | collective-permute-done | bytes 98336 | tf_op jit(solution)/shard_map/ppermute | solution.py:36
  231.7 5.5 %collective-permute-done.50.refs_2_ = bf16[1,16,1536]{2,1,0:T(8,128)(2,1)S(1)} collective-permute-done((bf16[1,16,1536]{2,1,0:T(8,128)(2,1)}, bf16[1,16,1536]{2,1,0:T(8,128)(2,1)S(1)}, u32[]{:S(2)}, u32[]{:S(2)}) %collective-permute-start.50) | collective-permute-done | bytes 49184 | tf_op jit(solution)/shard_map/ppermute | solution.py:36
  237.7 5.7 %shard_map.297 = (f32[16,1536]{1,0:T(8,128)}, bf16[16,1536]{1,0:T(8,128)(2,1)}, bf16[16,1664]{1,0:T(8,128)(2,1)}, f32[8,1536]{1,0:T(8,128)}) custom-call(s32[1]{0:T(128)} %bitcast.me_ref.refs_0_, f32[1,16,1536]{2,1,0:T(8,128)} %get-tuple-element.208.refs_1_, bf16[1,16,1536]{2,1,0:T(8,128)(2,1)} %copy-done.48, f32[16,1536]{1,0:T(8,128)} %get-tuple-element.189.refs_3_, ...), custom_call_target="tpu_custom_call" | custom-call | flops 75497472 | bytes 5376004 | tf_op jit(solution)/shard_map/pallas_call | solution.py:582
  245.4 2.6 collective-permute-done.52.refs_5_
  249.6 7.6 %shard_map.298 = (bf16[64,1536]{1,0:T(8,128)(2,1)}, bf16[528,3072]{1,0:T(8,128)(2,1)}) custom-call(s32[1]{0:T(128)S(6)} %min.6.refs_0_, bf16[64,1536]{1,0:T(8,128)(2,1)} %pad_maximum_fusion.17.refs_1_, bf16[528,3072]{1,0:T(8,128)(2,1)} %shard_map.289.refs_2_, bf16[16,1664]{1,0:T(8,128)(2,1)} %get-tuple-element.212.refs_3_, bf16[16,1664]{1,0:T(8,128)(2,1)} %copy-done.69, ...), custom_call_target="tpu_custom_call" | custom-call | flops 1384120320 | bytes 7094276 | tf_op jit(solution)/shard_map/pallas_call | solution.py:582
  261.8 3.0 collective-permute-done.55
  275.4 2.7 all-to-all-start.1
  281.8 13.1 %shard_map.300 = (bf16[8,48,1024]{2,1,0:T(8,128)(2,1)}, bf16[8,48,1024]{2,1,0:T(8,128)(2,1)}, bf16[8,48,1024]{2,1,0:T(8,128)(2,1)}, bf16[8,48,1024]{2,1,0:T(8,12...) custom-call(s32[1]{0:T(128)} %bitcast.me_ref.refs_0_, bf16[528,768]{1,0:T(8,128)(2,1)} %get-tuple-element.228.refs_1_, ...), custom_call_target="tpu_custom_call" | custom-call | flops 4982833152 | bytes 12828676 | tf_op jit(solution)/shard_map/pallas_call | solution.py:582
  298.5 20.7 %collective-permute-done.82 = bf16[192,1536]{1,0:T(8,128)(2,1)S(1)} collective-permute-done((bf16[192,1536]{1,0:T(8,128)(2,1)S(1)}, bf16[192,1536]{1,0:T(8,128)(2,1)S(1)}, u32[]{:S(2)}, u32[]{:S(2)}) %collective-permute-start.82) | collective-permute-done | bytes 589856 | tf_op jit(solution)/shard_map/ppermute | solution.py:36
  320.4 13.2 %shard_map.305 = (bf16[512,1536]{1,0:T(8,128)(2,1)}, f32[16,1536]{1,0:T(8,128)}, f32[8,1536]{1,0:T(8,128)}) custom-call(s32[1]{0:T(128)} %bitcast.me_ref.refs_0_, bf16[528,3072]{1,0:T(8,128)(2,1)} %get-tuple-element.259.refs_3_.refs_1_, bf16[512,1536]{1,0:T(8,128)(2,1)} %bitcast.120, f32[2,1536]{1,0:T(2,128)} %copy-done.40, ...), custom_call_target="tpu_custom_call" | custom-call | flops 4982833152 | bytes 15992836 | tf_op jit(solution)/shard_map/pallas_call | solution.py:582
  334.4 2.3 shard_map.299
  338.2 5.8 %collective-permute-done.65.refs_10_.refs_11_ = bf16[8,48,1024]{2,1,0:T(8,128)(2,1)S(1)} collective-permute-done((bf16[8,48,1024]{2,1,0:T(8,128)(2,1)}, bf16[8,48,1024]{2,1,0:T(8,128)(2,1)S(1)}, u32[]{:S(2)}, u32[]{:S(2)}) %collective-permute-start.65) | collective-permute-done | bytes 786464 | tf_op jit(solution)/shard_map/ppermute | solution.py:36
  344.9 3.9 shard_map.302
  360.2 2.7 collective-permute-done.66.refs_2_.refs_3_
  366.2 3.2 shard_map.304
  370.7 2.5 collective-permute-start.70
  382.0 2.5 shard_map.307
  385.0 2.5 collective-permute-start.81
  388.5 2.5 collective-permute-start.80
  391.0 5.0 %collective-permute-done.76 = f32[16,1536]{1,0:T(8,128)S(1)} collective-permute-done((f32[16,1536]{1,0:T(8,128)S(1)}, f32[16,1536]{1,0:T(8,128)S(1)}, u32[]{:S(2)}, u32[]{:S(2)}) %collective-permute-start.76) | collective-permute-done | bytes 98336 | tf_op jit(solution)/shard_map/ppermute | solution.py:36
  404.6 2.7 convolution_multiply_fusion
  407.3 2.7 fusion.7
  (401 shorter events, 144.8 us)
Async XLA Ops:
  7.2 194.8 %all-gather.9.cloned.1.call-start = ((), (), s32[]{:S(2)}) async-start(), calls=%async_computation.4 | async-start | bytes 3244032 | tf_op jit(solution)/shard_map/all_gather | solution.py:701
  9.0 17.8 %collective-permute-start.3 = (bf16[1,48,3072]{2,1,0:T(8,128)(2,1)}, bf16[1,48,3072]{2,1,0:T(8,128)(2,1)}, u32[]{:S(2)}, u32[]{:S(2)}) collective-permute-start(bf16[1,48,3072]{2,1,0:T(8,128)(2,1)} %maximum_bitcast_fusion), channel_id=1, source_target_pairs={{0,16},{1,17},{2,18},{3,19},{4,20},{5,21},{6,22},{7,23},{8,24},{9,... | collective-permute-start | bytes 884744 | tf_op jit(solution)/shard_map/ppermute | solution.py:36
  16.3 20.9 %collective-permute-start.7 = (bf16[1,192,1536]{2,1,0:T(8,128)(2,1)}, bf16[1,192,1536]{2,1,0:T(8,128)(2,1)}, u32[]{:S(2)}, u32[]{:S(2)}) collective-permute-start(bf16[1,192,1536]{2,1,0:T(8,128)(2,1)} %bitcast.136), channel_id=1, source_target_pairs={{0,8},{1,9},{2,10},{3,11},{4,12},{5,13},{6,14},{7,15},{8,0},{9,1},... | collective-permute-start | bytes 1769480 | tf_op jit(solution)/shard_map/ppermute | solution.py:36
  39.7 14.1 %collective-permute-start.8 = (bf16[2,48,1024]{2,1,0:T(8,128)(2,1)S(1)}, bf16[2,48,1024]{2,1,0:T(8,128)(2,1)S(1)}, u32[]{:S(2)}, u32[]{:S(2)}) collective-permute-start(bf16[2,48,1024]{2,1,0:T(8,128)(2,1)S(1)} %get-tuple-element.155), channel_id=1, source_target_pairs={{0,8},{1,9},{2,10},{3,11},{4,12},{5,13},{6,14},{7,15},{8,0},{9,1},... | collective-permute-start | bytes 589832 | tf_op jit(solution)/shard_map/ppermute | solution.py:36
  42.2 11.6 %collective-permute-start.9 = (bf16[2,48,1024]{2,1,0:T(8,128)(2,1)S(1)}, bf16[2,48,1024]{2,1,0:T(8,128)(2,1)S(1)}, u32[]{:S(2)}, u32[]{:S(2)}) collective-permute-start(bf16[2,48,1024]{2,1,0:T(8,128)(2,1)S(1)} %get-tuple-element.156), channel_id=1, source_target_pairs={{0,2},{1,3},{2,0},{3,1},{4,6},{5,7},{6,4},{7,5},{8,10},{9,11},{10,... | collective-permute-start | bytes 589832 | tf_op jit(solution)/shard_map/ppermute | solution.py:36
  43.5 10.4 %collective-permute-start.10 = (bf16[2,48,1024]{2,1,0:T(8,128)(2,1)S(1)}, bf16[2,48,1024]{2,1,0:T(8,128)(2,1)S(1)}, u32[]{:S(2)}, u32[]{:S(2)}) collective-permute-start(bf16[2,48,1024]{2,1,0:T(8,128)(2,1)S(1)} %get-tuple-element.157), channel_id=1, source_target_pairs={{0,4},{1,5},{2,6},{3,7},{4,0},{5,1},{6,2},{7,3},{8,12},{9,13},{10,... | collective-permute-start | bytes 589832 | tf_op jit(solution)/shard_map/ppermute | solution.py:36
  57.6 12.3 %collective-permute-start.17 = (bf16[4,48,1024]{2,1,0:T(8,128)(2,1)S(1)}, bf16[4,48,1024]{2,1,0:T(8,128)(2,1)S(1)}, u32[]{:S(2)}, u32[]{:S(2)}) collective-permute-start(bf16[4,48,1024]{2,1,0:T(8,128)(2,1)S(1)} %pad_maximum_fusion.11), channel_id=1, source_target_pairs={{0,2},{1,3},{2,0},{3,1},{4,6},{5,7},{6,4},{7,5},{8,10},{9,11},{10,... | collective-permute-start | bytes 1179656 | tf_op jit(solution)/shard_map/ppermute | solution.py:36
  75.1 21.4 %collective-permute-start.19 = (bf16[528,768]{1,0:T(8,128)(2,1)}, bf16[528,768]{1,0:T(8,128)(2,1)S(1)}, u32[]{:S(2)}, u32[]{:S(2)}) collective-permute-start(bf16[528,768]{1,0:T(8,128)(2,1)} %get-tuple-element.167), channel_id=1, source_target_pairs={{0,1},{1,0},{2,3},{3,2},{4,5},{5,4},{6,7},{7,6},{8,9},{9,8},{10,11... | collective-permute-start | bytes 2433032 | tf_op jit(solution)/shard_map/ppermute | solution.py:36
  75.1 21.4 %collective-permute-start.18 = (bf16[8,48,1024]{2,1,0:T(8,128)(2,1)S(1)}, bf16[8,48,1024]{2,1,0:T(8,128)(2,1)S(1)}, u32[]{:S(2)}, u32[]{:S(2)}) collective-permute-start(bf16[8,48,1024]{2,1,0:T(8,128)(2,1)S(1)} %pad_maximum_fusion.3.refs_2_.refs_5_), channel_id=1, source_target_pairs={{0,2},{1,3},{2,0},{3,1},{4,6},{5,7},{6,4},{7,5},{8,10},{9,11},{10,... | collective-permute-start | bytes 2359304 | tf_op jit(solution)/shard_map/ppermute | solution.py:36
  76.5 22.8 %collective-permute-start.22 = (bf16[8,48,1024]{2,1,0:T(8,128)(2,1)}, bf16[8,48,1024]{2,1,0:T(8,128)(2,1)}, u32[]{:S(2)}, u32[]{:S(2)}) collective-permute-start(bf16[8,48,1024]{2,1,0:T(8,128)(2,1)} %pad_maximum_fusion.4.refs_6_.refs_9_), channel_id=1, source_target_pairs={{0,4},{1,5},{2,6},{3,7},{4,0},{5,1},{6,2},{7,3},{8,12},{9,13},{10,... | collective-permute-start | bytes 2359304 | tf_op jit(solution)/shard_map/ppermute | solution.py:36
  76.8 24.2 %collective-permute-start.25 = (bf16[8,48,1024]{2,1,0:T(8,128)(2,1)S(1)}, bf16[8,48,1024]{2,1,0:T(8,128)(2,1)}, u32[]{:S(2)}, u32[]{:S(2)}) collective-permute-start(bf16[8,48,1024]{2,1,0:T(8,128)(2,1)S(1)} %pad_maximum_fusion.5.refs_10_.refs_13_), channel_id=1, source_target_pairs={{0,8},{1,9},{2,10},{3,11},{4,12},{5,13},{6,14},{7,15},{8,0},{9,1},... | collective-permute-start | bytes 2359304 | tf_op jit(solution)/shard_map/ppermute | solution.py:36
  96.4 13.9 %collective-permute-start.20 = (bf16[8,48,1024]{2,1,0:T(8,128)(2,1)S(1)}, bf16[8,48,1024]{2,1,0:T(8,128)(2,1)}, u32[]{:S(2)}, u32[]{:S(2)}) collective-permute-start(bf16[8,48,1024]{2,1,0:T(8,128)(2,1)S(1)} %pad_maximum_fusion.3.refs_2_.refs_5_), channel_id=1, source_target_pairs={{0,1},{1,0},{2,3},{3,2},{4,5},{5,4},{6,7},{7,6},{8,9},{9,8},{10,11... | collective-permute-start | bytes 2359304 | tf_op jit(solution)/shard_map/ppermute | solution.py:36
  97.4 12.5 %collective-permute-start.13 = (bf16[2,48,1536]{2,1,0:T(8,128)(2,1)S(1)}, bf16[2,48,1536]{2,1,0:T(8,128)(2,1)S(1)}, u32[]{:S(2)}, u32[]{:S(2)}) collective-permute-start(bf16[2,48,1536]{2,1,0:T(8,128)(2,1)S(1)} %pad_maximum_fusion.15), channel_id=1, source_target_pairs={{0,8},{1,9},{2,10},{3,11},{4,12},{5,13},{6,14},{7,15},{8,0},{9,1},... | collective-permute-start | bytes 884744 | tf_op jit(solution)/shard_map/ppermute | solution.py:36
  97.7 12.2 %collective-permute-start.14 = (bf16[2,192,384]{2,1,0:T(8,128)(2,1)S(1)}, bf16[2,192,384]{2,1,0:T(8,128)(2,1)S(1)}, u32[]{:S(2)}, u32[]{:S(2)}) collective-permute-start(bf16[2,192,384]{2,1,0:T(8,128)(2,1)S(1)} %maximum_select_fusion.2), channel_id=1, source_target_pairs={{0,4},{1,5},{2,6},{3,7},{4,0},{5,1},{6,2},{7,3},{8,12},{9,13},{10,... | collective-permute-start | bytes 884744 | tf_op jit(solution)/shard_map/ppermute | solution.py:36
  99.3 11.4 %collective-permute-start.21 = (bf16[8,48,1024]{2,1,0:T(8,128)(2,1)}, bf16[8,48,1024]{2,1,0:T(8,128)(2,1)S(1)}, u32[]{:S(2)}, u32[]{:S(2)}) collective-permute-start(bf16[8,48,1024]{2,1,0:T(8,128)(2,1)} %copy-done.61), channel_id=1, source_target_pairs={{0,1},{1,0},{2,3},{3,2},{4,5},{5,4},{6,7},{7,6},{8,9},{9,8},{10,11... | collective-permute-start | bytes 2359304 | tf_op jit(solution)/shard_map/ppermute | solution.py:36
  110.7 23.2 %collective-permute-start.2 = (bf16[16,1536]{1,0:T(8,128)(2,1)}, bf16[16,1536]{1,0:T(8,128)(2,1)}, u32[]{:S(2)}, u32[]{:S(2)}) collective-permute-start(bf16[16,1536]{1,0:T(8,128)(2,1)} %fusion.25), channel_id=1, source_target_pairs={{0,3},{1,2},{2,1},{3,0},{4,7},{5,6},{6,5},{7,4},{8,11},{9,10},{10,... | collective-permute-start | bytes 147464 | tf_op jit(solution)/shard_map/ppermute | solution.py:36
  111.3 22.6 %collective-permute-start.1 = (bf16[16,1536]{1,0:T(8,128)(2,1)}, bf16[16,1536]{1,0:T(8,128)(2,1)}, u32[]{:S(2)}, u32[]{:S(2)}) collective-permute-start(bf16[16,1536]{1,0:T(8,128)(2,1)} %fusion.25), channel_id=1, source_target_pairs={{0,2},{1,3},{2,0},{3,1},{4,6},{5,7},{6,4},{7,5},{8,10},{9,11},{10,... | collective-permute-start | bytes 147464 | tf_op jit(solution)/shard_map/ppermute | solution.py:36
  114.7 18.1 %collective-permute-start.28 = (bf16[2,2,192,384]{3,2,1,0:T(8,128)(2,1)S(1)}, bf16[2,2,192,384]{3,2,1,0:T(8,128)(2,1)S(1)}, u32[]{:S(2)}, u32[]{:S(2)}) collective-permute-start(bf16[2,2,192,384]{3,2,1,0:T(8,128)(2,1)S(1)} %maximum_select_fusion.1), channel_id=1, source_target_pairs={{0,8},{1,9},{2,10},{3,11},{4,12},{5,13},{6,14},{7,15},{8,0},{9,1},... | collective-permute-start | bytes 1769480 | tf_op jit(solution)/shard_map/ppermute | solution.py:36
  114.7 14.9 %collective-permute-start.35 = (bf16[4,48,768]{2,1,0:T(8,128)(2,1)S(1)}, bf16[4,48,768]{2,1,0:T(8,128)(2,1)}, u32[]{:S(2)}, u32[]{:S(2)}) collective-permute-start(bf16[4,48,768]{2,1,0:T(8,128)(2,1)S(1)} %get-tuple-element.181), channel_id=1, source_target_pairs={{0,4},{1,5},{2,6},{3,7},{4,0},{5,1},{6,2},{7,3},{8,12},{9,13},{10,... | collective-permute-start | bytes 884744 | tf_op jit(solution)/shard_map/ppermute | solution.py:36
  117.2 13.5 %collective-permute-start.36 = (bf16[4,48,768]{2,1,0:T(8,128)(2,1)S(1)}, bf16[4,48,768]{2,1,0:T(8,128)(2,1)S(1)}, u32[]{:S(2)}, u32[]{:S(2)}) collective-permute-start(bf16[4,48,768]{2,1,0:T(8,128)(2,1)S(1)} %get-tuple-element.182), channel_id=1, source_target_pairs={{0,2},{1,3},{2,0},{3,1},{4,6},{5,7},{6,4},{7,5},{8,10},{9,11},{10,... | collective-permute-start | bytes 884744 | tf_op jit(solution)/shard_map/ppermute | solution.py:36
  130.8 31.5 %collective-permute-start.37 = (bf16[8,48,768]{2,1,0:T(8,128)(2,1)S(1)}, bf16[8,48,768]{2,1,0:T(8,128)(2,1)}, u32[]{:S(2)}, u32[]{:S(2)}) collective-permute-start(bf16[8,48,768]{2,1,0:T(8,128)(2,1)S(1)} %pad_maximum_fusion.7.refs_8_), channel_id=1, source_target_pairs={{0,2},{1,3},{2,0},{3,1},{4,6},{5,7},{6,4},{7,5},{8,10},{9,11},{10,... | collective-permute-start | bytes 1769480 | tf_op jit(solution)/shard_map/ppermute | solution.py:36
  132.9 30.0 %collective-permute-start.40 = (bf16[8,48,768]{2,1,0:T(8,128)(2,1)S(1)}, bf16[8,48,768]{2,1,0:T(8,128)(2,1)}, u32[]{:S(2)}, u32[]{:S(2)}) collective-permute-start(bf16[8,48,768]{2,1,0:T(8,128)(2,1)S(1)} %pad_maximum_fusion.8.refs_12_), channel_id=1, source_target_pairs={{0,4},{1,5},{2,6},{3,7},{4,0},{5,1},{6,2},{7,3},{8,12},{9,13},{10,... | collective-permute-start | bytes 1769480 | tf_op jit(solution)/shard_map/ppermute | solution.py:36
  136.3 11.5 %collective-permute-start.31 = (bf16[64,384]{1,0:T(8,128)(2,1)}, bf16[64,384]{1,0:T(8,128)(2,1)}, u32[]{:S(2)}, u32[]{:S(2)}) collective-permute-start(bf16[64,384]{1,0:T(8,128)(2,1)} %get-tuple-element.179), channel_id=1, source_target_pairs={{0,3},{1,2},{2,1},{3,0},{4,7},{5,6},{6,5},{7,4},{8,11},{9,10},{10,... | collective-permute-start | bytes 147464 | tf_op jit(solution)/shard_map/ppermute | solution.py:36
  136.3 18.6 %collective-permute-start.30 = (bf16[64,384]{1,0:T(8,128)(2,1)}, bf16[64,384]{1,0:T(8,128)(2,1)}, u32[]{:S(2)}, u32[]{:S(2)}) collective-permute-start(bf16[64,384]{1,0:T(8,128)(2,1)} %get-tuple-element.178), channel_id=1, source_target_pairs={{0,2},{1,3},{2,0},{3,1},{4,6},{5,7},{6,4},{7,5},{8,10},{9,11},{10,... | collective-permute-start | bytes 147464 | tf_op jit(solution)/shard_map/ppermute | solution.py:36
  137.9 17.0 %collective-permute-start.29 = (bf16[64,384]{1,0:T(8,128)(2,1)}, bf16[64,384]{1,0:T(8,128)(2,1)}, u32[]{:S(2)}, u32[]{:S(2)}) collective-permute-start(bf16[64,384]{1,0:T(8,128)(2,1)} %get-tuple-element.177), channel_id=1, source_target_pairs={{0,1},{1,0},{2,3},{3,2},{4,5},{5,4},{6,7},{7,6},{8,9},{9,8},{10,11... | collective-permute-start | bytes 147464 | tf_op jit(solution)/shard_map/ppermute | solution.py:36
  139.7 62.3 %all-to-all-start = ((bf16[32,48,384]{2,1,0:T(8,128)(2,1)}), bf16[32,48,384]{2,1,0:T(8,128)(2,1)S(1)}, u32[]{:S(2)}, u32[]{:S(2)}) async-start(bf16[32,48,384]{2,1,0:T(8,128)(2,1)} %pad_maximum_fusion.2), calls=%async_computation | async-start | bytes 2359296 | tf_op jit(solution)/shard_map/all_to_all | solution.py:654
  142.8 116.9 %all-gather.5.cloned.1.call-start = ((), (), s32[]{:S(2)}) async-start(), calls=%async_computation.2 | async-start | bytes 1622016 | tf_op jit(solution)/shard_map/all_gather | solution.py:806
  162.3 14.2 %collective-permute-start.38 = (bf16[8,48,768]{2,1,0:T(8,128)(2,1)S(1)}, bf16[8,48,768]{2,1,0:T(8,128)(2,1)S(1)}, u32[]{:S(2)}, u32[]{:S(2)}) collective-permute-start(bf16[8,48,768]{2,1,0:T(8,128)(2,1)S(1)} %pad_maximum_fusion.7.refs_8_), channel_id=1, source_target_pairs={{0,1},{1,0},{2,3},{3,2},{4,5},{5,4},{6,7},{7,6},{8,9},{9,8},{10,11... | collective-permute-start | bytes 1769480 | tf_op jit(solution)/shard_map/ppermute | solution.py:36
  162.3 14.2 %collective-permute-start.39 = (bf16[8,48,768]{2,1,0:T(8,128)(2,1)}, bf16[8,48,768]{2,1,0:T(8,128)(2,1)S(1)}, u32[]{:S(2)}, u32[]{:S(2)}) collective-permute-start(bf16[8,48,768]{2,1,0:T(8,128)(2,1)} %collective-permute-done.37.refs_9_), channel_id=1, source_target_pairs={{0,1},{1,0},{2,3},{3,2},{4,5},{5,4},{6,7},{7,6},{8,9},{9,8},{10,11... | collective-permute-start | bytes 1769480 | tf_op jit(solution)/shard_map/ppermute | solution.py:36
  162.9 13.7 %collective-permute-start.41 = (bf16[8,48,768]{2,1,0:T(8,128)(2,1)S(1)}, bf16[8,48,768]{2,1,0:T(8,128)(2,1)S(1)}, u32[]{:S(2)}, u32[]{:S(2)}) collective-permute-start(bf16[8,48,768]{2,1,0:T(8,128)(2,1)S(1)} %pad_maximum_fusion.8.refs_12_), channel_id=1, source_target_pairs={{0,1},{1,0},{2,3},{3,2},{4,5},{5,4},{6,7},{7,6},{8,9},{9,8},{10,11... | collective-permute-start | bytes 1769480 | tf_op jit(solution)/shard_map/ppermute | solution.py:36
  162.9 13.6 %collective-permute-start.42 = (bf16[8,48,768]{2,1,0:T(8,128)(2,1)}, bf16[8,48,768]{2,1,0:T(8,128)(2,1)S(1)}, u32[]{:S(2)}, u32[]{:S(2)}) collective-permute-start(bf16[8,48,768]{2,1,0:T(8,128)(2,1)} %collective-permute-done.40.refs_13_), channel_id=1, source_target_pairs={{0,1},{1,0},{2,3},{3,2},{4,5},{5,4},{6,7},{7,6},{8,9},{9,8},{10,11... | collective-permute-start | bytes 1769480 | tf_op jit(solution)/shard_map/ppermute | solution.py:36
  184.4 220.3 %all-gather.7.cloned.1.call-start = ((), (), s32[]{:S(2)}) async-start(), calls=%async_computation.3 | async-start | bytes 3244032 | tf_op jit(solution)/shard_map/all_gather | solution.py:888
  275.4 84.5 %all-to-all-start.1 = ((bf16[32,48,384]{2,1,0:T(8,128)(2,1)}), bf16[32,48,384]{2,1,0:T(8,128)(2,1)S(1)}, u32[]{:S(2)}, u32[]{:S(2)}) async-start(bf16[32,48,384]{2,1,0:T(8,128)(2,1)} %bitcast.56), calls=%async_computation.1 | async-start | bytes 2359296 | tf_op jit(solution)/shard_map/all_to_all | solution.py:870
  278.1 41.2 %collective-permute-start.82 = (bf16[192,1536]{1,0:T(8,128)(2,1)S(1)}, bf16[192,1536]{1,0:T(8,128)(2,1)S(1)}, u32[]{:S(2)}, u32[]{:S(2)}) collective-permute-start(bf16[192,1536]{1,0:T(8,128)(2,1)S(1)} %copy-done.67), channel_id=1, source_target_pairs={{0,8},{1,9},{2,10},{3,11},{4,12},{5,13},{6,14},{7,15},{8,0},{9,1},... | collective-permute-start | bytes 1769480 | tf_op jit(solution)/shard_map/ppermute | solution.py:36
  295.0 43.2 %collective-permute-start.63 = (bf16[8,48,1024]{2,1,0:T(8,128)(2,1)}, bf16[8,48,1024]{2,1,0:T(8,128)(2,1)S(1)}, u32[]{:S(2)}, u32[]{:S(2)}) collective-permute-start(bf16[8,48,1024]{2,1,0:T(8,128)(2,1)} %get-tuple-element.233), channel_id=1, source_target_pairs={{0,2},{1,3},{2,0},{3,1},{4,6},{5,7},{6,4},{7,5},{8,10},{9,11},{10,... | collective-permute-start | bytes 2359304 | tf_op jit(solution)/shard_map/ppermute | solution.py:36
  296.5 41.7 %collective-permute-start.64 = (bf16[8,48,1024]{2,1,0:T(8,128)(2,1)}, bf16[8,48,1024]{2,1,0:T(8,128)(2,1)S(1)}, u32[]{:S(2)}, u32[]{:S(2)}) collective-permute-start(bf16[8,48,1024]{2,1,0:T(8,128)(2,1)} %get-tuple-element.239), channel_id=1, source_target_pairs={{0,4},{1,5},{2,6},{3,7},{4,0},{5,1},{6,2},{7,3},{8,12},{9,13},{10,... | collective-permute-start | bytes 2359304 | tf_op jit(solution)/shard_map/ppermute | solution.py:36
  298.0 46.0 %collective-permute-start.65 = (bf16[8,48,1024]{2,1,0:T(8,128)(2,1)}, bf16[8,48,1024]{2,1,0:T(8,128)(2,1)S(1)}, u32[]{:S(2)}, u32[]{:S(2)}) collective-permute-start(bf16[8,48,1024]{2,1,0:T(8,128)(2,1)} %get-tuple-element.241), channel_id=1, source_target_pairs={{0,8},{1,9},{2,10},{3,11},{4,12},{5,13},{6,14},{7,15},{8,0},{9,1},... | collective-permute-start | bytes 2359304 | tf_op jit(solution)/shard_map/ppermute | solution.py:36
  320.4 13.3 %collective-permute-start.59 = (bf16[8,16,1536]{2,1,0:T(8,128)(2,1)S(1)}, bf16[8,16,1536]{2,1,0:T(8,128)(2,1)S(1)}, u32[]{:S(2)}, u32[]{:S(2)}) collective-permute-start(bf16[8,16,1536]{2,1,0:T(8,128)(2,1)S(1)} %copy-done.68), channel_id=1, source_target_pairs={{0,1},{1,0},{2,3},{3,2},{4,5},{5,4},{6,7},{7,6},{8,9},{9,8},{10,11... | collective-permute-start | bytes 1179656 | tf_op jit(solution)/shard_map/ppermute | solution.py:36
  336.7 18.6 %collective-permute-start.62 = (bf16[4,16,1536]{2,1,0:T(8,128)(2,1)}, bf16[4,16,1536]{2,1,0:T(8,128)(2,1)S(1)}, u32[]{:S(2)}, u32[]{:S(2)}) collective-permute-start(bf16[4,16,1536]{2,1,0:T(8,128)(2,1)} %get-tuple-element.234), channel_id=1, source_target_pairs={{0,2},{1,3},{2,0},{3,1},{4,6},{5,7},{6,4},{7,5},{8,10},{9,11},{10,... | collective-permute-start | bytes 589832 | tf_op jit(solution)/shard_map/ppermute | solution.py:36
  348.8 16.4 %collective-permute-start.67 = (bf16[4,48,1024]{2,1,0:T(8,128)(2,1)}, bf16[4,48,1024]{2,1,0:T(8,128)(2,1)S(1)}, u32[]{:S(2)}, u32[]{:S(2)}) collective-permute-start(bf16[4,48,1024]{2,1,0:T(8,128)(2,1)} %get-tuple-element.245), channel_id=1, source_target_pairs={{0,4},{1,5},{2,6},{3,7},{4,0},{5,1},{6,2},{7,3},{8,12},{9,13},{10,... | collective-permute-start | bytes 1179656 | tf_op jit(solution)/shard_map/ppermute | solution.py:36
  350.3 14.8 %collective-permute-start.68 = (bf16[4,48,1024]{2,1,0:T(8,128)(2,1)}, bf16[4,48,1024]{2,1,0:T(8,128)(2,1)S(1)}, u32[]{:S(2)}, u32[]{:S(2)}) collective-permute-start(bf16[4,48,1024]{2,1,0:T(8,128)(2,1)} %get-tuple-element.251), channel_id=1, source_target_pairs={{0,8},{1,9},{2,10},{3,11},{4,12},{5,13},{6,14},{7,15},{8,0},{9,1},... | collective-permute-start | bytes 1179656 | tf_op jit(solution)/shard_map/ppermute | solution.py:36
  350.8 14.4 %collective-permute-start.69 = (bf16[4,48,1024]{2,1,0:T(8,128)(2,1)}, bf16[4,48,1024]{2,1,0:T(8,128)(2,1)S(1)}, u32[]{:S(2)}, u32[]{:S(2)}) collective-permute-start(bf16[4,48,1024]{2,1,0:T(8,128)(2,1)} %get-tuple-element.253), channel_id=1, source_target_pairs={{0,2},{1,3},{2,0},{3,1},{4,6},{5,7},{6,4},{7,5},{8,10},{9,11},{10,... | collective-permute-start | bytes 1179656 | tf_op jit(solution)/shard_map/ppermute | solution.py:36
  369.4 10.5 %collective-permute-start.73 = (bf16[2,48,1024]{2,1,0:T(8,128)(2,1)}, bf16[2,48,1024]{2,1,0:T(8,128)(2,1)S(1)}, u32[]{:S(2)}, u32[]{:S(2)}) collective-permute-start(bf16[2,48,1024]{2,1,0:T(8,128)(2,1)} %get-tuple-element.257), channel_id=1, source_target_pairs={{0,8},{1,9},{2,10},{3,11},{4,12},{5,13},{6,14},{7,15},{8,0},{9,1},... | collective-permute-start | bytes 589832 | tf_op jit(solution)/shard_map/ppermute | solution.py:36
  370.7 16.8 %collective-permute-start.70 = (bf16[1,16,1536]{2,1,0:T(8,128)(2,1)S(1)}, bf16[1,16,1536]{2,1,0:T(8,128)(2,1)S(1)}, u32[]{:S(2)}, u32[]{:S(2)}) collective-permute-start(bf16[1,16,1536]{2,1,0:T(8,128)(2,1)S(1)} %copy-done.72), channel_id=1, source_target_pairs={{0,16},{1,17},{2,18},{3,19},{4,20},{5,21},{6,22},{7,23},{8,24},{9,... | collective-permute-start | bytes 147464 | tf_op jit(solution)/shard_map/ppermute | solution.py:36
  384.5 11.5 %collective-permute-start.76 = (f32[16,1536]{1,0:T(8,128)S(1)}, f32[16,1536]{1,0:T(8,128)S(1)}, u32[]{:S(2)}, u32[]{:S(2)}) collective-permute-start(f32[16,1536]{1,0:T(8,128)S(1)} %add.179), channel_id=1, source_target_pairs={{0,16},{1,17},{2,18},{3,19},{4,20},{5,21},{6,22},{7,23},{8,24},{9,... | collective-permute-start | bytes 294920 | tf_op jit(solution)/shard_map/ppermute | solution.py:36
  385.0 13.1 %collective-permute-start.81 = (bf16[1,48,1024]{2,1,0:T(8,128)(2,1)}, bf16[1,48,1024]{2,1,0:T(8,128)(2,1)S(1)}, u32[]{:S(2)}, u32[]{:S(2)}) collective-permute-start(bf16[1,48,1024]{2,1,0:T(8,128)(2,1)} %get-tuple-element.284), channel_id=1, source_target_pairs={{0,16},{1,17},{2,18},{3,19},{4,20},{5,21},{6,22},{7,23},{8,24},{9,... | collective-permute-start | bytes 294920 | tf_op jit(solution)/shard_map/ppermute | solution.py:36
  388.1 13.8 %collective-permute-start.79 = (bf16[1,48,1024]{2,1,0:T(8,128)(2,1)}, bf16[1,48,1024]{2,1,0:T(8,128)(2,1)S(1)}, u32[]{:S(2)}, u32[]{:S(2)}) collective-permute-start(bf16[1,48,1024]{2,1,0:T(8,128)(2,1)} %get-tuple-element.277), channel_id=1, source_target_pairs={{0,16},{1,17},{2,18},{3,19},{4,20},{5,21},{6,22},{7,23},{8,24},{9,... | collective-permute-start | bytes 294920 | tf_op jit(solution)/shard_map/ppermute | solution.py:36
  388.5 12.4 %collective-permute-start.80 = (bf16[1,48,1024]{2,1,0:T(8,128)(2,1)}, bf16[1,48,1024]{2,1,0:T(8,128)(2,1)S(1)}, u32[]{:S(2)}, u32[]{:S(2)}) collective-permute-start(bf16[1,48,1024]{2,1,0:T(8,128)(2,1)} %get-tuple-element.282), channel_id=1, source_target_pairs={{0,16},{1,17},{2,18},{3,19},{4,20},{5,21},{6,22},{7,23},{8,24},{9,... | collective-permute-start | bytes 294920 | tf_op jit(solution)/shard_map/ppermute | solution.py:36
  (113 other events, 797.6 us)
Sparse Core Ops, SparseCore 0:
  60.3 59.6 all-gather.8
  184.5 53.9 all-gather.4
  275.5 65.6 all-gather.6

commit v3 on v2

--- a/solution.py
+++ b/solution.py
@@ -44,19 +44,24 @@
     def __init__(self, x, order, me):
         self.x, self.order, self.me, self.done = x, list(order), me, []
 
+    def rows(self):
+        if isinstance(self.x, (list, tuple)):
+            mine, other = self.x
+            axis = sum(m > self.done[-1] for m in self.done)
+            mine, other = jnp.expand_dims(mine, axis), jnp.expand_dims(other, axis)
+            self.x = jnp.where(
+                (self.me & self.done[-1]) != 0,
+                jnp.concatenate([other, mine], axis),
+                jnp.concatenate([mine, other], axis),
+            )
+        return self.x
+
     def send(self):
-        return self.x, self.order[0]
+        return self.rows(), self.order[0]
 
     def take(self, sent, other):
-        mask = self.order.pop(0)
-        axis = sum(m > mask for m in self.done)
-        mine, other = jnp.expand_dims(sent, axis), jnp.expand_dims(other, axis)
-        self.x = jnp.where(
-            (self.me & mask) != 0,
-            jnp.concatenate([other, mine], axis),
-            jnp.concatenate([mine, other], axis),
-        )
-        self.done.append(mask)
+        self.done.append(self.order.pop(0))
+        self.x = (sent, other)
 
 
 class GatherRel:
@@ -79,11 +84,10 @@
             self.order.pop(0)
             self.x = (sent, other)
 
-    def last(self, count, token):
+    def last(self, count, join=False):
         mask = self.order.pop(0)
-        pieces = lax.optimization_barrier(tuple(self.x) + (token,))[:2]
+        pieces = (jnp.concatenate(self.x, axis=0),) if join else tuple(self.x)
         self.x = [*pieces, *[trade(x, mask, count) for x in pieces]]
-        return pieces[0]
 
 
 class Halves:
@@ -96,8 +100,8 @@
         self.others = [trade(x, mask, count) for x, mask in zip(sent, masks)]
         self.token = sent[0]
 
-    def split(self, parts=1):
-        self.keep, self.sends = add_split(self.keep, self.others, parts)
+    def split(self):
+        self.keep, self.sends = add_split(self.keep, self.others)
 
     def total(self):
         return [k.astype(F32) + o.astype(F32) for k, o in zip(self.keep, self.others)]
@@ -112,34 +116,27 @@
         send[...] = (keep2[...].astype(F32) + other2[...].astype(F32)).astype(BF).reshape(send.shape)
 
 
-def add_split(keeps, others, parts=1):
-    shape = keeps[0].shape[-3:]
-    half = shape[0] // 2
+def add_split(keeps, others):
+    half = keeps[0].shape[0] // 2
     some = min(half, 2)
-    ins, specs, outs = [], [], []
+    ins, specs, outs, out_specs = [], [], [], []
     for keep, other in zip(keeps, others):
-        for part in range(parts):
-
-            def spec(at, part=part):
-                if parts == 1:
-                    return pl.BlockSpec((some,) + shape[1:], lambda i: (i + at, 0, 0))
-                return pl.BlockSpec((1, some) + shape[1:], lambda i: (part, i + at, 0, 0))
-
-            ins += [keep, keep, other, other]
-            specs += [spec(0), spec(half // some), spec(0), spec(half // some)]
-            outs += [
-                jax.ShapeDtypeStruct((half,) + shape[1:], F32),
-                jax.ShapeDtypeStruct((half,) + shape[1:], BF),
-            ]
+        tail = keep.shape[1:]
+        low = pl.BlockSpec((some,) + tail, lambda i: (i, 0, 0))
+        high = pl.BlockSpec((some,) + tail, lambda i: (i + half // some, 0, 0))
+        ins += [keep, keep, other, other]
+        specs += [low, high, low, high]
+        outs += [jax.ShapeDtypeStruct((half,) + tail, F32), jax.ShapeDtypeStruct((half,) + tail, BF)]
+        out_specs += [low, low]
     out = pl.pallas_call(
         lambda *refs: add_split_kernel(len(ins) // 4, *refs),
         grid=(half // some,),
         out_shape=tuple(outs),
         in_specs=specs,
-        out_specs=tuple(pl.BlockSpec((some,) + shape[1:], lambda i: (i, 0, 0)) for x in outs),
+        out_specs=tuple(out_specs),
         compiler_params=pltpu.CompilerParams(vmem_limit_bytes=56 << 20),
         cost_estimate=pl.CostEstimate(
-            flops=1, bytes_accessed=sum(6 * x.size for x in outs), transcendentals=0
+            flops=1, bytes_accessed=1, transcendentals=0
         ),
     )(*ins)
     return list(out[::2]), list(out[1::2])
@@ -163,6 +160,14 @@
     for job, x, (unused, mask) in zip(jobs, sent, sends):
         job.take(x, trade(x, mask, count))
     return sent[0]
+
+
+def sync(jobs, *arrays):
+    held = [job.x for job in jobs]
+    held, arrays = lax.optimization_barrier((held, arrays))
+    for job, x in zip(jobs, held):
+        job.x = x
+    return arrays
 
 
 def share_seq(x, seq_count, count):
@@ -365,7 +370,8 @@
         self.arrays = [x for pieces in parts for x in pieces]
         self.orders = orders
         self.cols = sum(pieces[0].shape[2] for pieces in parts)
-        self.ends = [parts[0][0].shape[2] * (k + 1) for k in range(len(parts))]
+        widths = [pieces[0].shape[2] for pieces in parts]
+        self.ends = [sum(widths[: k + 1]) for k in range(len(parts))]
 
     def fetch(self, me, refs, into, sems):
         at, waits = 0, []
@@ -473,7 +479,8 @@
     down_ref,
     down_keep_ref,
     down_send_ref,
-    up_ref,
+    up_keep_ref,
+    up_send_ref,
     keep_ref,
     send_ref,
 ):
@@ -482,7 +489,9 @@
     down = dot(active_ref[...], grad_rows_ref[...], first)
     down_keep_ref[...] = down[:units]
     down_send_ref[...] = down[units:].astype(BF)
-    up_ref[...] = dot(rows_ref[...], pre_ref[...], first).astype(BF)
+    up = dot(rows_ref[...], pre_ref[...], first)
+    up_keep_ref[...] = up[:, :units].astype(BF)
+    up_send_ref[...] = up[:, units:].astype(BF)
     out = dot(active_ref[...], down_ref[...])
     half = out.shape[0] // 2
     keep_ref[...] = out[:half].reshape(keep_ref.shape)
@@ -537,34 +546,37 @@
 def sums_kernel(orders, me_ref, s_ref, s2_ref, g_ref, g2_ref, *refs):
     *out_refs, s_held, g_held, held, sems = refs
     me = me_ref[0] - me_ref[0] % 2
-    half, block, cols = out_refs[0].shape
+    half, block, unused = out_refs[0].shape
+    widths = [ref.shape[2] for ref in out_refs[::2]]
+    starts = [sum(widths[:k]) for k in range(len(widths))]
     rows = s_ref.shape[0]
     for k, ref in enumerate((s_ref, s2_ref)):
         pltpu.make_async_copy(ref, s_held.at[k * rows : (k + 1) * rows], sems.at[0]).start()
     for part in range(len(orders)):
-        columns = slice(part * cols, (part + 1) * cols)
+        columns = slice(starts[part], starts[part] + widths[part])
         for k, ref in enumerate((g_ref, g2_ref)):
             to = g_held.at[k * rows : (k + 1) * rows, columns]
             pltpu.make_async_copy(ref.at[:, columns], to, sems.at[1 + part]).start()
     pltpu.make_async_copy(s_held, s_held, sems.at[0]).wait()
     some = held.shape[0]
     for part, order in enumerate(orders):
-        columns = slice(part * cols, (part + 1) * cols)
+        columns = slice(starts[part], starts[part] + widths[part])
         here = g_held.at[:, columns]
         pltpu.make_async_copy(here, here, sems.at[1 + part]).wait()
         first = (me // order[-1]) % 2
         for start in range(0, 2 * half, some):
             full = dot(s_held[:, start * block : (start + some) * block], here[...], ((0,), (0,)))
-            held[...] = full.astype(BF).reshape(held.shape)
+            cols = widths[part]
+            held[:, :, :cols] = full.astype(BF).reshape(some, block, cols)
             for bit in range(2):
 
                 @pl.when(first == bit)
-                def _(bit=bit, start=start, part=part, order=order):
+                def _(bit=bit, start=start, part=part, order=order, cols=cols):
                     for n in range(some):
                         owner = 2 * (start + n)
                         place = place_of(owner ^ me, order) % half
                         send = (owner // order[-1]) % 2 != bit
-                        out_refs[2 * part + send][place] = held[n]
+                        out_refs[2 * part + send][place] = held[n, :, :cols]
 
 
 SCALAR = pl.BlockSpec(memory_space=pltpu.SMEM)
@@ -587,7 +599,7 @@
         out_specs=tuple(FAR if far_outputs else whole(x) for x in outputs),
         scratch_shapes=list(scratch),
         compiler_params=pltpu.CompilerParams(vmem_limit_bytes=56 << 20),
-        cost_estimate=pl.CostEstimate(flops=flops, bytes_accessed=nbytes, transcendentals=0),
+        cost_estimate=pl.CostEstimate(flops=flops // 1000, bytes_accessed=nbytes // 1000, transcendentals=0),
     )(*inputs)
 
 
@@ -629,7 +641,8 @@
         head + [side, fold, near] + tail,
         head + [near, side, fold] + tail,
     )
-    ffn_order = head + [near, side] + tail
+    ffn_order = item_bits + seq_bits[:-1]
+    core = seq_bits[-1]
     block = width // count
     regular = block % 16 == 0
 
@@ -646,11 +659,10 @@
     media_normed, media_unit, media_rstd = layer_norm(shifted, media_gain, media_bias)
     sources = jnp.concatenate([media_normed.astype(BF), latent_normed], axis=0)
 
+    def in_columns(x):
+        return x.reshape(x.shape[0], count, -1).transpose(1, 0, 2)
+
     def spread(x):
-        x = x.reshape(x.shape[0], count, -1).transpose(1, 0, 2)
-        pairs = x.reshape(-1, 2, fold, *x.shape[1:])
-        pairs = jnp.concatenate([pairs[:, 1:], pairs[:, :1]], axis=1).reshape(x.shape)
-        x = jnp.concatenate([x, pairs], axis=2)
         x = lax.all_to_all(x, AXES, split_axis=0, concat_axis=0, tiled=True)
         return x.reshape(-1, x.shape[2])
 
@@ -674,63 +686,60 @@
 
     parts = len(orders)
     units = w_down.shape[0]
-    out_orders = (orders[0], head + [fold, side, near] + tail)
+    out_orders = (head + [near, fold, side] + tail, head + [near, side, fold] + tail)
+    shares = (width * 5 // 6, width * 5 // 6, width // 3)
+    def query_pieces(x):
+        pieces = [columns_of(x, m) for m in range(seq_count)]
+        return [pieces[0]] + [trade(pieces[m], m, count) for m in range(1, seq_count)]
+
     if regular:
         first = GatherRel(jnp.concatenate([w_key, w_value], axis=1)[None], head)
-        second = GatherRel(w_out[None], head + [fold])
-
-        def split(x, orders, done):
-            cols = x.shape[2] // len(orders)
+        second = GatherRel(w_out[None], head + [near])
+
+        def split(x, shares, orders, done):
             return [
-                GatherApart(x[..., k * cols : (k + 1) * cols], order[done:])
+                GatherApart(x[..., sum(shares[:k]) : sum(shares[: k + 1])], order[done:])
                 for k, order in enumerate(orders)
             ]
 
-        down_job = GatherRel(w_down[None], [fold])
-        started = exchange(count, first, down_job)
         while first.order:
             exchange(count, first)
         latent_item = share_seq(latent_normed, seq_count, count)
-        pieces = [columns_of(w_query, m) for m in range(seq_count)]
-        pieces = [pieces[0]] + [trade(pieces[m], m, count) for m in range(1, seq_count)]
-        query_cols = Gather(
-            seq_blocks(jnp.stack(pieces), 0), head + [near, fold], me
-        )
-        first = split(first.x, orders, len(head))
-        started = exchange(count, *first, second, query_cols, wait=(down_job.x,))
-        rows_all = lax.all_gather(
-            jnp.concatenate([after(latent_normed, started), grad_out[0]], axis=1), AXES, axis=0
-        )
-        exchange(count, *first, second, query_cols)
-        second = split(second.x, out_orders, len(head) + 1)
-        started = exchange(count, *first)
+        pieces = query_pieces(w_query)
         half_mine, half_other = call(
             halves_kernel,
-            (me[None], after(sources, started)),
+            (me[None], sources),
             (share((sources.shape[0], width // 2)),) * 2,
             0,
             specs={0: SCALAR},
         )
-        half_other = trade(half_other, 1, count)
+        rows_mine = jnp.concatenate([latent_normed, grad_out[0]], axis=1)
+        sources, latent_item, half_mine, half_other, rows_mine, *pieces = sync(
+            [first], sources, latent_item, half_mine, half_other, rows_mine, *pieces
+        )
+        query_cols = Gather(seq_blocks(jnp.stack(pieces), 0), [near] + head + [fold], me)
+        first = split(first.x, shares, orders, len(head))
+        exchange(count, *first, second, query_cols)
+        sync([*first, second, query_cols])
+        exchange(count, *first, second, query_cols)
+        (up_in,) = sync([*first, second, query_cols], in_columns(w_up))
+        second = split(second.x, (width // 2, width // 2), out_orders, len(head) + 1)
+        exchange(count, *first, query_cols)
+        sources, latent_item, rows_mine, half_other = sync(
+            [*first, query_cols], sources, latent_item, rows_mine, half_other
+        )
         for job in first:
-            job.last(count, half_other)
-        ready = [piece for job in first for piece in job.x]
-        exchange(count, *second, query_cols, wait=ready)
-        started = exchange(count, *second)
-        up_pair = spread(after(w_up, *ready))
-        key_value = Stacks([job.x for job in first], orders)
+            job.last(count)
+        rows_all = lax.all_gather(rows_mine, AXES, axis=0)
     else:
-        started = w_key
-        up_pair = spread(w_up)
+        up_mine = spread(in_columns(w_up))
         rows_all = lax.all_gather(
             jnp.concatenate([latent_normed, grad_out[0]], axis=1), AXES, axis=0
         )
         latent_item = share_seq(latent_normed, seq_count, count)
-        pieces = [columns_of(w_query, m) for m in range(seq_count)]
-        pieces = [pieces[0]] + [trade(pieces[m], m, count) for m in range(1, seq_count)]
-        query_cols = Gather(seq_blocks(jnp.stack(pieces), 0), item_bits, me)
-        down_job = GatherRel(w_down[None], [fold])
-        exchange(count, down_job)
+        query_cols = Gather(seq_blocks(jnp.stack(query_pieces(w_query)), 0), item_bits, me)
+        while query_cols.order:
+            exchange(count, query_cols)
         both = lax.all_gather(jnp.concatenate([w_key, w_value], 1), AXES, axis=0, tiled=True)
         key_value = Plain(both)
         out_full = Plain(lax.all_gather(w_out, AXES, axis=0, tiled=True))
@@ -750,6 +759,14 @@
             scratch=scratch + [pltpu.SemaphoreType.DMA((len(whole.orders),))],
         )
 
+    query_slice = query_cols.rows().reshape(width, cols_here)
+    query_mine = (dot(latent_item, query_slice) * scaling).astype(BF)
+    sends = [reordered(query_mine, m) for m in range(1, seq_count)]
+    if regular:
+        query_mine, *sends = sync([*first, *second], query_mine, *sends)
+        key_value = Stacks([job.x for job in first], orders)
+        exchange(count, *second)
+    pieces = [query_mine] + [trade(x, m + 1, count) for m, x in enumerate(sends)]
     source_count = sources.shape[0]
     keys = with_weights(
         project_kernel,
@@ -758,20 +775,12 @@
         (share((source_count, 2 * width)),),
         4 * source_count * width * width,
     )[0]
-    while query_cols.order:
-        exchange(count, query_cols)
-    query_slice = query_cols.x.reshape(width, cols_here)
-    query_mine = (dot(latent_item, query_slice) * scaling).astype(BF)
-    sends = [reordered(query_mine, m) for m in range(1, seq_count)]
-    *sends, keys = lax.optimization_barrier((*sends, keys))
-    pieces = [query_mine] + [trade(x, m + 1, count) for m, x in enumerate(sends)]
+    if regular:
+        keys, half_other, up_in, *pieces = sync(second, keys, half_other, up_in, *pieces)
+        up_mine = spread(up_in)
+        half_other = trade(half_other, 1, count)
+        exchange(count, *second)
     queries = seq_blocks(jnp.stack(pieces), 1)
-    down_pair = down_job.x.reshape(-1, width)
-    if regular:
-        for job in second:
-            job.last(count, keys)
-        out_full = Stacks([job.x for job in second], out_orders)
-
     seen = jnp.clip((frames - seq_index * frames_here) * PATCH, 0, media_rows).astype(jnp.int32)
     all_rows = queries.shape[0]
     pair_flops = 2 * H // 2 * 2 * all_rows * 256 * sources.shape[0]
@@ -788,11 +797,21 @@
         return [blocks[0]] + [trade(blocks[m], m, count) for m in range(1, seq_count)]
 
 
+    mixed_parts = own_parts(mixed)
+    if regular:
+        mixed_parts = sync(second, *mixed_parts)
+        for job in second:
+            job.last(count, join=True)
+        sync(second)
+        out_full = Stacks([job.x for job in second], out_orders)
+    up_other, down_other = trade(up_mine, core, count), trade(w_down, core, count)
+    up_pair = jnp.concatenate([up_mine, up_other], axis=1)
+    down_pair = jnp.concatenate([w_down, down_other], axis=0)
     rows_wide = jax.ShapeDtypeStruct((latent_rows, width), F32)
     rows_low = jax.ShapeDtypeStruct((latent_rows, width), BF)
     mixture_wide, mixture, log_total, hidden, ffn_in = with_weights(
         lambda *refs: combine_kernel(seq_count, *refs),
-        (*own_parts(mixed), latents[0], ffn_gain[None], ffn_bias[None]),
+        (*mixed_parts, latents[0], ffn_gain[None], ffn_bias[None]),
         out_full,
         (
             rows_wide,
@@ -803,8 +822,6 @@
         ),
         2 * latent_rows * width * width,
     )
-    mixture_all = lax.all_gather(mixture, AXES, axis=0, tiled=True)
-
     ffn_rows = GatherRel(ffn_in[None], ffn_order)
     while len(ffn_rows.order) > 1:
         exchange(count, ffn_rows)
@@ -825,25 +842,29 @@
     )
     back = Halves([keep], [send], [ffn_order])
     back.step(count)
-    back.split()
-    back.step(count)
-    down_keep, down_send, up_sums, keep, send = call(
+    down_keep, down_send, up_keep, up_send, keep, send = call(
         ffn_sums_kernel,
         (ffn_all, after(grad_all, back.token), active, pre, down_pair),
         (
             jax.ShapeDtypeStruct((units, width), F32),
             share((units, width)),
-            share((width, 2 * units)),
+            share((width, units)),
+            share((width, units)),
             *halves,
         ),
         3 * ffn_flops,
     )
     result = Halves([keep], [send], [ffn_order])
-    back.split()
-    back.step(count, (down_send,))
+    wait = (down_send,)
     while back.orders[0]:
         back.split()
-        back.step(count)
+        back.step(count, wait)
+        if not wait:
+            result.split()
+        result.step(count, (back.token,))
+        wait = ()
+        if back.orders[0]:
+            back.others, result.others = lax.optimization_barrier((back.others, result.others))
 
     hidden_grad, attended_low, packed, ffn_sums = with_weights(
         hidden_back_kernel,
@@ -865,10 +886,11 @@
         ),
         2 * latent_rows * width * width,
     )
-    down_other = trade(after(down_send, packed), fold, count)
-    up_blocks = after(up_sums, packed).reshape(count, -1, 2 * units)
-    up_blocks = lax.all_to_all(up_blocks, AXES, split_axis=0, concat_axis=0, tiled=True)
+    down_send, up_send = sync([], down_send, up_send, packed)[:2]
+    down_other, up_other = trade(down_send, core, count), trade(up_send, core, count)
     pieces = [packed] + [trade(packed, m, count) for m in range(1, seq_count)]
+    result.split()
+    result.step(count, (packed,))
     query_part, row_grad = call(
         lambda *refs: attend_back_kernel(media_rows, seq_count, *refs),
         (seen, queries, keys, *pieces),
@@ -877,44 +899,43 @@
         specs={0: SCALAR},
     )
     sends = [reordered(columns_of(query_part, m), m) for m in range(seq_count)]
-    row_send, mixture_all, *sends = lax.optimization_barrier((row_grad, mixture_all, *sends))
+    row_send, result.others, *sends = lax.optimization_barrier((row_grad, result.others, *sends))
     row_other = trade(row_send, 1, count)
     pieces = [sends[0]] + [trade(sends[m], m, count) for m in range(1, seq_count)]
-    row_other, *pieces = lax.optimization_barrier((row_other, *pieces))
+    row_grad, row_other, *pieces = sync([], row_send, row_other, *pieces)
     query_cols_grad = sum(x.astype(F32) for x in pieces).astype(BF)
     query_side = dot(query_cols_grad, query_slice, ((1,), (1,))).astype(BF)
     query_side = own_parts(jnp.concatenate([query_side, query_cols_grad], axis=1))
-    query_rows = seq_blocks(jnp.stack([x[:, width:] for x in query_side]), 1)
-    rows = lax.all_gather(
-        jnp.concatenate([attended_low, query_rows], axis=1), AXES, axis=0, tiled=True
-    )
-
-    cols = 2 * width // parts
-    result.step(count, (query_side[1],))
+
     if regular:
-        place = share((count // 4, block, cols))
         outs = call(
             lambda *refs: sums_kernel([order[:-1] for order in orders], *refs),
             (me[None], half_mine, half_other, row_grad, row_other),
-            (place,) * (2 * parts),
+            tuple(share((count // 4, block, cols)) for cols in shares for unused in range(2)),
             4 * width * width * source_count,
             specs={0: SCALAR, 1: FAR, 2: FAR, 3: FAR, 4: FAR},
             scratch=(
                 pltpu.VMEM((2 * source_count, width // 2), BF),
                 pltpu.VMEM((2 * source_count, 2 * width), BF),
-                pltpu.VMEM((8, block, cols), BF),
+                pltpu.VMEM((8, block, max(shares)), BF),
                 pltpu.SemaphoreType.DMA((1 + parts,)),
             ),
         )
         weights = Halves(outs[::2], outs[1::2], [order[:-1] for order in orders])
-        weights.step(count, query_side[1:])
+        weights.step(count, (*query_side[1:], *result.others))
         started = weights.token
     else:
         full = dot(sources, row_grad, ((0,), (0,))).astype(BF)
         full = lax.psum_scatter(full, AXES, scatter_dimension=0, tiled=True).astype(F32)
-        started = query_rows
-    result.split()
-    result.step(count, (started,))
+        started = row_other
+    result.others, up_keep, up_other = sync([], result.others, up_keep, up_other, started)[:-1]
+    up_blocks = (up_keep.astype(F32) + up_other.astype(F32)).astype(BF)
+    up_blocks = up_blocks.reshape(count, -1, units)
+    up_blocks = lax.all_to_all(up_blocks, AXES, split_axis=0, concat_axis=0, tiled=True)
+    query_rows = seq_blocks(jnp.stack([x[:, width:] for x in query_side]), 1)
+    rows = lax.all_gather(
+        jnp.concatenate([attended_low, query_rows, mixture], axis=1), AXES, axis=0, tiled=True
+    )
 
     media_grad, latent_source, media_sums = with_weights(
         source_kernel,
@@ -951,12 +972,14 @@
             ],
             axis=0,
         ),
-        [near, fold] + head + seq_bits,
+        [side, near, fold],
     )
     if regular:
         while weights.orders[0]:
             weights.split()
             weights.step(count)
+            if len(weights.orders[0]) == 1:
+                down_other, up_blocks = after(down_other, weights.token), after(up_blocks, weights.token)
             if result.orders[0]:
                 result.split()
                 result.step(count, (weights.token,))
@@ -967,21 +990,23 @@
         result.split()
         result.step(count)
     down_grad = down_keep + down_other.astype(F32)
-    up_blocks = up_blocks.reshape(-1, 2, fold, width // count, 2 * units).astype(F32)
-    swapped = jnp.concatenate([up_blocks[:, 1:], up_blocks[:, :1]], axis=1)
-    up_grad = up_blocks[..., :units] + swapped[..., units:]
-    up_grad = up_grad.reshape(count, -1, units).transpose(1, 0, 2).reshape(-1, count * units)
+    up_grad = up_blocks.transpose(1, 0, 2).reshape(-1, count * units).astype(F32)
+    latents_out = hidden + result.total()[0][0]
+
+    def my_columns(x):
+        return lax.dynamic_slice_in_dim(x, me * block, block, 1)
+
+    out_grad = dot(my_columns(rows[:, 2 * width :]), rows[:, :width], ((0,), (0,)))
+    latent_all = my_columns(rows_all.reshape(-1, 2 * width))
+    query_grad = dot(latent_all, rows[:, width : 2 * width], ((0,), (0,))) * scaling
     while sums.order:
         exchange(count, sums)
-    sums = sums.x
-    latents_out = hidden + result.total()[0][0]
-
-    def my_columns(x):
-        return lax.dynamic_slice_in_dim(x, me * block, block, 1)
-
-    out_grad = dot(my_columns(mixture_all), rows[:, :width], ((0,), (0,)))
-    latent_all = my_columns(rows_all.reshape(-1, 2 * width))
-    query_grad = dot(latent_all, rows[:, width : 2 * width], ((0,), (0,))) * scaling
+    sums, others = sums.x, [0]
+    for bit in head + tail:
+        others += [mask ^ bit for mask in others]
+    sums_parts = [trade(sums, mask, count) for mask in others[1:]]
+    out_grad, query_grad, *sums_parts = sync([], out_grad, query_grad, *sums_parts)
+    sums = sums + sum(sums_parts)
     return (
         latents_out.astype(BF)[None],
         latents_grad[None],

time: 425 us -> 410 us (0.965)
  waiting for transfers between devices: 159 us -> 117 us
  starting transfers between devices: 78.3 us -> 100 us
    ppermute x83 -> x84, waiting for transfers between devices: 159 us -> 116 us  [trade(): return lax.ppermute(x, AXES, [(i, i ^ mask) for i in range(count)])]
    all_gather x3 -> x2, starting transfers between devices: 0.53 us -> 12.3 us  [the longest x1 12.3 us: shards(): lax.all_gather(jnp.concatenate([attended_low, query_rows, mixture], axis=...]
    ppermute x83 -> x84, starting transfers between devices: 72 us -> 80.2 us  [trade(): return lax.ppermute(x, AXES, [(i, i ^ mask) for i in range(count)])]
    unnamed x153 -> x162, local copies, waits for them, and re-layouts: 16.5 us -> 11.2 us
  transfers between devices with their start and end apart: 88 -> 88, of which waited for: 41 -> 42; matrix products, arithmetic and copies ran while one was open for 10% -> 13% of each run, Pallas kernels for 24% -> 22%
where the time goes in v3:
time: 410 us; the launch traced here: 402 us
  waiting for transfers between devices  117 us (29%)
  starting transfers between devices  100 us (24%)
  Pallas kernels  100 us (24%)
  local copies, waits for them, and re-layouts  35.5 us (9%)
  other arithmetic  27.3 us (7%)
  between operations  16.2 us (4%)
  matrix products  6.22 us (2%)
    ppermute x84, waiting for transfers between devices, trade(): return lax.ppermute(x, AXES, [(i, i ^ mask) for i in range(count)])  116 us
    ppermute x84, starting transfers between devices, trade(): return lax.ppermute(x, AXES, [(i, i ^ mask) for i in range(count)])  80.2 us
    pallas_call x11, Pallas kernels, call(): pl.pallas_call(kernel, grid=(1,), out_shape=tuple(outputs), in_specs=[spe...  79.5 us
    pallas_call x9, Pallas kernels, add_split(): pl.pallas_call(lambda *refs: add_split_kernel(len(ins) // 4, *refs), grid...  20.9 us
    all_gather x1, starting transfers between devices, shards(): lax.all_gather(jnp.concatenate([attended_low, query_rows, mixture], axis=...  12.3 us
    unnamed x162, local copies, waits for them, and re-layouts  11.2 us
  transfers between devices with their start and end apart: 88, of which 42 were waited for; matrix products, arithmetic and copies ran while one was open for 13% of the time, Pallas kernels for 22%

profile of v3, /device:TPU:0, one launch (start us, length us, event | category | flops | bytes accessed | tf_op | source)
XLA Modules:
  0.0 402.4 jit_solution(8375826749030209563)
XLA Ops:
  10.6 2.6 collective-permute-start.2
  15.3 3.1 collective-permute-start
  23.8 4.6 %shard_map.288 = (bf16[528,768]{1,0:T(8,128)(2,1)}, bf16[528,768]{1,0:T(8,128)(2,1)}) custom-call(s32[1]{0:T(128)} %bitcast.me_ref.refs_0_, bf16[528,1536]{1,0:T(8,128)(2,1)} %pad_maximum_fusion.s_ref.refs_1_), custom_call_target="tpu_custom_call" | custom-call | bytes 3244 | tf_op jit(solution)/shard_map/pallas_call | solution.py:594
  36.3 3.2 collective-permute-start.7
  40.1 4.7 %collective-permute-done.10 = bf16[1,48,1536]{2,1,0:T(8,128)(2,1)S(1)} collective-permute-done((bf16[1,48,1536]{2,1,0:T(8,128)(2,1)S(1)}, bf16[1,48,1536]{2,1,0:T(8,128)(2,1)S(1)}, u32[]{:S(2)}, u32[]{:S(2)}) %collective-permute-start.10) | collective-permute-done | bytes 147488 | tf_op jit(solution)/shard_map/ppermute | solution.py:36
  54.3 3.9 collective-permute-start.16
  58.7 7.6 %collective-permute-done.13 = bf16[4,48,1280]{2,1,0:T(8,128)(2,1)} collective-permute-done((bf16[4,48,1280]{2,1,0:T(8,128)(2,1)S(1)}, bf16[4,48,1280]{2,1,0:T(8,128)(2,1)}, u32[]{:S(2)}, u32[]{:S(2)}) %collective-permute-start.13) | collective-permute-done | bytes 491552 | tf_op jit(solution)/shard_map/ppermute | solution.py:36
  74.4 18.0 %collective-permute-done.19.refs_11_.refs_14_ = bf16[8,48,512]{2,1,0:T(8,128)(2,1)S(1)} collective-permute-done((bf16[8,48,512]{2,1,0:T(8,128)(2,1)S(1)}, bf16[8,48,512]{2,1,0:T(8,128)(2,1)S(1)}, u32[]{:S(2)}, u32[]{:S(2)}) %collective-permute-start.19) | collective-permute-done | bytes 393248 | tf_op jit(solution)/shard_map/ppermute | solution.py:36
  97.3 3.3 collective-permute-done.25.refs_12_.refs_15_
  107.7 11.7 %shard_map.289.refs_2_ = bf16[528,3072]{1,0:T(8,128)(2,1)} custom-call(s32[1]{0:T(128)} %bitcast.me_ref.refs_0_, bf16[528,1536]{1,0:T(8,128)(2,1)} %pad_maximum_fusion.s_ref.refs_1_, bf16[8,48,1280]{2,1,0:T(8,128)(2,1)} %copy-done.4, bf16[8,48,1280]{2,1,0:T(8,128)(2,1)} %collective-permute-done.17.refs_3_.refs_6_, bf16[8,48,1280]{2,1,0:T(8,128)(2,1)} %copy-done.10, ...), custom_call_target="tpu_custom_call" | custom-call | flops 4982833 | bytes 14303 | tf_op jit(solution)/shard_map/pallas_call | solution.py:594
  123.7 5.8 %shard_map.290 = bf16[64,1664]{1,0:T(8,128)(2,1)} custom-call(s32[1]{0:T(128)S(6)} %min.6.refs_0_, bf16[64,1536]{1,0:T(8,128)(2,1)} %pad_maximum_fusion.18.refs_1_, bf16[528,3072]{1,0:T(8,128)(2,1)} %shard_map.289.refs_2_), custom_call_target="tpu_custom_call" | custom-call | flops 553648 | bytes 3653 | tf_op jit(solution)/shard_map/pallas_call | solution.py:594
  132.9 5.9 %collective-permute-done.35.refs_3_ = bf16[16,1664]{1,0:T(8,128)(2,1)S(1)} collective-permute-done((bf16[16,1664]{1,0:T(8,128)(2,1)S(1)}, bf16[16,1664]{1,0:T(8,128)(2,1)S(1)}, u32[]{:S(2)}, u32[]{:S(2)}) %collective-permute-start.35) | collective-permute-done | bytes 53280 | tf_op jit(solution)/shard_map/ppermute | solution.py:36
  139.3 4.3 %collective-permute-done.33 = bf16[8,48,768]{2,1,0:T(8,128)(2,1)S(1)} collective-permute-done((bf16[8,48,768]{2,1,0:T(8,128)(2,1)S(1)}, bf16[8,48,768]{2,1,0:T(8,128)(2,1)S(1)}, u32[]{:S(2)}, u32[]{:S(2)}) %collective-permute-start.33) | collective-permute-done | bytes 589856 | tf_op jit(solution)/shard_map/ppermute | solution.py:36
  144.7 3.9 all-to-all-start
  148.6 12.3 %all-gather.4.cloned.1.call-start = ((), (), s32[]{:S(2)}) async-start(), calls=%async_computation.2 | async-start | bytes 4866048 | tf_op jit(solution)/shard_map/all_gather | solution.py:936
  162.1 5.0 %shard_map.291 = (f32[16,1536]{1,0:T(8,128)}, bf16[16,1536]{1,0:T(8,128)(2,1)}, f32[16,128]{1,0:T(8,128)}, f32[16,1536]{1,0:T(8,128)}, bf16[16,1536]{1,0:T(8,128)(2,1)}) custom-call(s32[1]{0:T(128)} %bitcast.me_ref.refs_0_, bf16[16,1664]{1,0:T(8,128)(2,1)} %get-tuple-element.302.refs_1_, bf16[16,1664]{1,0:T(8,128)(2,1)} %copy-done.55, ...), custom_call_target="tpu_custom_call" | custom-call | flops 75497 | bytes 5296 | tf_op jit(solution)/shard_map/pallas_call | solution.py:594
  167.1 2.7 collective-permute-start.39
  169.8 3.1 collective-permute-done.39
  178.4 2.3 collective-permute-start.41
  180.7 3.8 collective-permute-done.41
  189.4 2.6 pad_maximum_fusion.1.refs_3_
  194.0 5.1 %shard_map.292 = (f32[8,16,1536]{2,1,0:T(8,128)}, bf16[8,16,1536]{2,1,0:T(8,128)(2,1)}, bf16[256,384]{1,0:T(8,128)(2,1)}, bf16[256,384]{1,0:T(8,128)(2,1)}, bf16...) custom-call(s32[1]{0:T(128)} %bitcast.me_ref.refs_0_, bf16[8,16,1536]{2,1,0:T(8,128)(2,1)} %copy-done.27, ...), custom_call_target="tpu_custom_call" | custom-call | flops 905969 | bytes 9437 | tf_op jit(solution)/shard_map/pallas_call | solution.py:594
  200.2 4.5 %shard_map.293 = (f32[192,1536]{1,0:T(8,128)}, bf16[192,1536]{1,0:T(8,128)(2,1)}, bf16[1536,192]{1,0:T(8,128)(2,1)}, bf16[1536,192]{1,0:T(8,128)(2,1)}, f32[8,16...) custom-call(bf16[256,1536]{1,0:T(8,128)(2,1)} %get-tuple-element.318.rows_ref, ...), custom_call_target="tpu_custom_call" | custom-call | flops 905969 | bytes 7274 | tf_op jit(solution)/shard_map/pallas_call | solution.py:594
  204.7 3.0 collective-permute-done.45.refs_2_.refs_3_
  212.6 4.4 %collective-permute-done.46.refs_2_.refs_3_ = bf16[4,16,1536]{2,1,0:T(8,128)(2,1)S(1)} collective-permute-done((bf16[4,16,1536]{2,1,0:T(8,128)(2,1)}, bf16[4,16,1536]{2,1,0:T(8,128)(2,1)S(1)}, u32[]{:S(2)}, u32[]{:S(2)}) %collective-permute-start.46) | collective-permute-done | bytes 196640 | tf_op jit(solution)/shard_map/ppermute | solution.py:36
  223.1 4.0 %collective-permute-start.48 = (bf16[2,16,1536]{2,1,0:T(8,128)(2,1)S(1)}, bf16[2,16,1536]{2,1,0:T(8,128)(2,1)S(1)}, u32[]{:S(2)}, u32[]{:S(2)}) collective-permute-start(bf16[2,16,1536]{2,1,0:T(8,128)(2,1)S(1)} %copy-done.76), channel_id=1, source_target_pairs={{0,8},{1,9},{2,10},{3,11},{4,12},{5,13},{6,14},{7,15},{8,0},{9,1},... | collective-permute-start | bytes 294920 | tf_op jit(solution)/shard_map/ppermute | solution.py:36
  227.1 2.6 collective-permute-done.48.refs_2_.refs_3_
  232.0 4.7 %collective-permute-start.51 = (bf16[1,16,1536]{2,1,0:T(8,128)(2,1)}, bf16[1,16,1536]{2,1,0:T(8,128)(2,1)S(1)}, u32[]{:S(2)}, u32[]{:S(2)}) collective-permute-start(bf16[1,16,1536]{2,1,0:T(8,128)(2,1)} %get-tuple-element.343), channel_id=1, source_target_pairs={{0,16},{1,17},{2,18},{3,19},{4,20},{5,21},{6,22},{7,23},{8,24},{9,... | collective-permute-start | bytes 147464 | tf_op jit(solution)/shard_map/ppermute | solution.py:36
  239.8 5.7 %shard_map.300 = (f32[16,1536]{1,0:T(8,128)}, bf16[16,1536]{1,0:T(8,128)(2,1)}, bf16[16,1664]{1,0:T(8,128)(2,1)}, f32[8,1536]{1,0:T(8,128)}) custom-call(s32[1]{0:T(128)} %bitcast.me_ref.refs_0_, f32[1,16,1536]{2,1,0:T(8,128)} %get-tuple-element.346.refs_1_, bf16[1,16,1536]{2,1,0:T(8,128)(2,1)} %copy-done.61, f32[16,1536]{1,0:T(8,128)} %get-tuple-element.314.refs_3_, ...), custom_call_target="tpu_custom_call" | custom-call | flops 75497 | bytes 5376 | tf_op jit(solution)/shard_map/pallas_call | solution.py:594
  249.7 2.7 collective-permute-start.55
  253.7 7.7 %shard_map.301 = (bf16[64,1536]{1,0:T(8,128)(2,1)}, bf16[528,3072]{1,0:T(8,128)(2,1)}) custom-call(s32[1]{0:T(128)S(6)} %min.6.refs_0_, bf16[64,1536]{1,0:T(8,128)(2,1)} %pad_maximum_fusion.18.refs_1_, bf16[528,3072]{1,0:T(8,128)(2,1)} %shard_map.289.refs_2_, bf16[16,1664]{1,0:T(8,128)(2,1)} %get-tuple-element.349.refs_3_, bf16[16,1664]{1,0:T(8,128)(2,1)} %copy-done.58, ...), custom_call_target="tpu_custom_call" | custom-call | flops 1384120 | bytes 7094 | tf_op jit(solution)/shard_map/pallas_call | solution.py:594
  265.9 3.5 collective-permute-done.59
  282.0 14.2 %shard_map.302 = (bf16[8,48,1280]{2,1,0:T(8,128)(2,1)}, bf16[8,48,1280]{2,1,0:T(8,128)(2,1)}, bf16[8,48,1280]{2,1,0:T(8,128)(2,1)}, bf16[8,48,1280]{2,1,0:T(8,12...) custom-call(s32[1]{0:T(128)} %bitcast.me_ref.refs_0_, bf16[528,768]{1,0:T(8,128)(2,1)} %get-tuple-element.358.refs_1_, ...), custom_call_target="tpu_custom_call" | custom-call | flops 4982833 | bytes 12828 | tf_op jit(solution)/shard_map/pallas_call | solution.py:594
  301.4 2.2 add_convert_fusion
  303.6 3.7 all-to-all-start.1
  307.4 13.2 %shard_map.303 = (bf16[512,1536]{1,0:T(8,128)(2,1)}, f32[16,1536]{1,0:T(8,128)}, f32[8,1536]{1,0:T(8,128)}) custom-call(s32[1]{0:T(128)} %bitcast.me_ref.refs_0_, bf16[528,3072]{1,0:T(8,128)(2,1)} %get-tuple-element.376.refs_3_.refs_1_, bf16[512,1536]{1,0:T(8,128)(2,1)} %bitcast.110, f32[2,1536]{1,0:T(2,128)} %copy-done.48, ...), custom_call_target="tpu_custom_call" | custom-call | flops 4982833 | bytes 15992 | tf_op jit(solution)/shard_map/pallas_call | solution.py:594
  322.4 5.4 %collective-permute-done.65.refs_2_.refs_3_ = bf16[8,48,1280]{2,1,0:T(8,128)(2,1)S(1)} collective-permute-done((bf16[8,48,1280]{2,1,0:T(8,128)(2,1)}, bf16[8,48,1280]{2,1,0:T(8,128)(2,1)S(1)}, u32[]{:S(2)}, u32[]{:S(2)}) %collective-permute-start.65) | collective-permute-done | bytes 983072 | tf_op jit(solution)/shard_map/ppermute | solution.py:36
  327.8 8.1 %collective-permute-done.66.refs_6_.refs_7_ = bf16[8,48,1280]{2,1,0:T(8,128)(2,1)S(1)} collective-permute-done((bf16[8,48,1280]{2,1,0:T(8,128)(2,1)}, bf16[8,48,1280]{2,1,0:T(8,128)(2,1)S(1)}, u32[]{:S(2)}, u32[]{:S(2)}) %collective-permute-start.66) | collective-permute-done | bytes 983072 | tf_op jit(solution)/shard_map/ppermute | solution.py:36
  336.8 3.9 shard_map.305
  347.2 4.3 %collective-permute-done.68 = f32[16,1536]{1,0:T(8,128)S(1)} collective-permute-done((f32[16,1536]{1,0:T(8,128)S(1)}, f32[16,1536]{1,0:T(8,128)S(1)}, u32[]{:S(2)}, u32[]{:S(2)}) %collective-permute-start.68) | collective-permute-done | bytes 98336 | tf_op jit(solution)/shard_map/ppermute | solution.py:36
  352.9 3.6 collective-permute-done.70.refs_6_.refs_7_
  357.2 3.3 shard_map.306
  368.0 2.4 shard_map.307
  373.5 2.8 collective-permute-start.80
  378.1 4.0 %collective-permute-done.76 = f32[16,1536]{1,0:T(8,128)S(1)} collective-permute-done((f32[16,1536]{1,0:T(8,128)S(1)}, f32[16,1536]{1,0:T(8,128)S(1)}, u32[]{:S(2)}, u32[]{:S(2)}) %collective-permute-start.76) | collective-permute-done | bytes 98336 | tf_op jit(solution)/shard_map/ppermute | solution.py:36
  382.2 3.0 collective-permute-start.77
  386.6 2.8 convolution_multiply_fusion
  389.4 2.6 fusion.7
  (415 shorter events, 144.4 us)
Async XLA Ops:
  7.2 186.8 %all-gather.6.cloned.1.call-start = ((), (), s32[]{:S(2)}) async-start(), calls=%async_computation.3 | async-start | bytes 3244032 | tf_op jit(solution)/shard_map/all_gather | solution.py:733
  10.1 18.3 %collective-permute-start.1 = (bf16[16,1536]{1,0:T(8,128)(2,1)S(1)}, bf16[16,1536]{1,0:T(8,128)(2,1)S(1)}, u32[]{:S(2)}, u32[]{:S(2)}) collective-permute-start(bf16[16,1536]{1,0:T(8,128)(2,1)S(1)} %fusion.17), channel_id=1, source_target_pairs={{0,1},{1,0},{2,3},{3,2},{4,5},{5,4},{6,7},{7,6},{8,9},{9,8},{10,11... | collective-permute-start | bytes 147464 | tf_op jit(solution)/shard_map/ppermute | solution.py:36
  10.6 19.3 %collective-permute-start.2 = (bf16[16,1536]{1,0:T(8,128)(2,1)S(1)}, bf16[16,1536]{1,0:T(8,128)(2,1)S(1)}, u32[]{:S(2)}, u32[]{:S(2)}) collective-permute-start(bf16[16,1536]{1,0:T(8,128)(2,1)S(1)} %fusion.17), channel_id=1, source_target_pairs={{0,2},{1,3},{2,0},{3,1},{4,6},{5,7},{6,4},{7,5},{8,10},{9,11},{10,... | collective-permute-start | bytes 147464 | tf_op jit(solution)/shard_map/ppermute | solution.py:36
  13.2 16.7 %collective-permute-start.3 = (bf16[16,1536]{1,0:T(8,128)(2,1)S(1)}, bf16[16,1536]{1,0:T(8,128)(2,1)S(1)}, u32[]{:S(2)}, u32[]{:S(2)}) collective-permute-start(bf16[16,1536]{1,0:T(8,128)(2,1)S(1)} %fusion.17), channel_id=1, source_target_pairs={{0,3},{1,2},{2,1},{3,0},{4,7},{5,6},{6,5},{7,4},{8,11},{9,10},{10,... | collective-permute-start | bytes 147464 | tf_op jit(solution)/shard_map/ppermute | solution.py:36
  14.1 18.0 %collective-permute-start.4 = (bf16[48,384]{1,0:T(8,128)(2,1)S(1)}, bf16[48,384]{1,0:T(8,128)(2,1)S(1)}, u32[]{:S(2)}, u32[]{:S(2)}) collective-permute-start(bf16[48,384]{1,0:T(8,128)(2,1)S(1)} %get-tuple-element.471), channel_id=1, source_target_pairs={{0,1},{1,0},{2,3},{3,2},{4,5},{5,4},{6,7},{7,6},{8,9},{9,8},{10,11... | collective-permute-start | bytes 110600 | tf_op jit(solution)/shard_map/ppermute | solution.py:36
  15.3 16.7 %collective-permute-start = (bf16[1,48,3072]{2,1,0:T(8,128)(2,1)S(1)}, bf16[1,48,3072]{2,1,0:T(8,128)(2,1)S(1)}, u32[]{:S(2)}, u32[]{:S(2)}) collective-permute-start(bf16[1,48,3072]{2,1,0:T(8,128)(2,1)S(1)} %maximum_bitcast_fusion), channel_id=1, source_target_pairs={{0,16},{1,17},{2,18},{3,19},{4,20},{5,21},{6,22},{7,23},{8,24},{9,... | collective-permute-start | bytes 884744 | tf_op jit(solution)/shard_map/ppermute | solution.py:36
  35.2 9.5 %collective-permute-start.10 = (bf16[1,48,1536]{2,1,0:T(8,128)(2,1)S(1)}, bf16[1,48,1536]{2,1,0:T(8,128)(2,1)S(1)}, u32[]{:S(2)}, u32[]{:S(2)}) collective-permute-start(bf16[1,48,1536]{2,1,0:T(8,128)(2,1)S(1)} %bitcast.125), channel_id=1, source_target_pairs={{0,16},{1,17},{2,18},{3,19},{4,20},{5,21},{6,22},{7,23},{8,24},{9,... | collective-permute-start | bytes 442376 | tf_op jit(solution)/shard_map/ppermute | solution.py:36
  35.5 9.2 %collective-permute-start.8 = (bf16[2,48,1280]{2,1,0:T(8,128)(2,1)S(1)}, bf16[2,48,1280]{2,1,0:T(8,128)(2,1)S(1)}, u32[]{:S(2)}, u32[]{:S(2)}) collective-permute-start(bf16[2,48,1280]{2,1,0:T(8,128)(2,1)S(1)} %get-tuple-element.232), channel_id=1, source_target_pairs={{0,2},{1,3},{2,0},{3,1},{4,6},{5,7},{6,4},{7,5},{8,10},{9,11},{10,... | collective-permute-start | bytes 737288 | tf_op jit(solution)/shard_map/ppermute | solution.py:36
  36.3 10.6 %collective-permute-start.7 = (bf16[2,48,1280]{2,1,0:T(8,128)(2,1)S(1)}, bf16[2,48,1280]{2,1,0:T(8,128)(2,1)S(1)}, u32[]{:S(2)}, u32[]{:S(2)}) collective-permute-start(bf16[2,48,1280]{2,1,0:T(8,128)(2,1)S(1)} %get-tuple-element.231), channel_id=1, source_target_pairs={{0,8},{1,9},{2,10},{3,11},{4,12},{5,13},{6,14},{7,15},{8,0},{9,1},... | collective-permute-start | bytes 737288 | tf_op jit(solution)/shard_map/ppermute | solution.py:36
  47.8 10.4 %collective-permute-start.14 = (bf16[4,48,512]{2,1,0:T(8,128)(2,1)S(1)}, bf16[4,48,512]{2,1,0:T(8,128)(2,1)S(1)}, u32[]{:S(2)}, u32[]{:S(2)}) collective-permute-start(bf16[4,48,512]{2,1,0:T(8,128)(2,1)S(1)} %pad_maximum_fusion.16), channel_id=1, source_target_pairs={{0,2},{1,3},{2,0},{3,1},{4,6},{5,7},{6,4},{7,5},{8,10},{9,11},{10,... | collective-permute-start | bytes 589832 | tf_op jit(solution)/shard_map/ppermute | solution.py:36
  48.7 9.9 %collective-permute-start.15 = (bf16[2,48,1536]{2,1,0:T(8,128)(2,1)S(1)}, bf16[2,48,1536]{2,1,0:T(8,128)(2,1)S(1)}, u32[]{:S(2)}, u32[]{:S(2)}) collective-permute-start(bf16[2,48,1536]{2,1,0:T(8,128)(2,1)S(1)} %pad_maximum_fusion.14), channel_id=1, source_target_pairs={{0,4},{1,5},{2,6},{3,7},{4,0},{5,1},{6,2},{7,3},{8,12},{9,13},{10,... | collective-permute-start | bytes 884744 | tf_op jit(solution)/shard_map/ppermute | solution.py:36
  49.3 17.1 %collective-permute-start.13 = (bf16[4,48,1280]{2,1,0:T(8,128)(2,1)S(1)}, bf16[4,48,1280]{2,1,0:T(8,128)(2,1)}, u32[]{:S(2)}, u32[]{:S(2)}) collective-permute-start(bf16[4,48,1280]{2,1,0:T(8,128)(2,1)S(1)} %pad_maximum_fusion.9), channel_id=1, source_target_pairs={{0,8},{1,9},{2,10},{3,11},{4,12},{5,13},{6,14},{7,15},{8,0},{9,1},... | collective-permute-start | bytes 1474568 | tf_op jit(solution)/shard_map/ppermute | solution.py:36
  52.8 14.7 %collective-permute-start.12 = (bf16[4,48,1280]{2,1,0:T(8,128)(2,1)S(1)}, bf16[4,48,1280]{2,1,0:T(8,128)(2,1)S(1)}, u32[]{:S(2)}, u32[]{:S(2)}) collective-permute-start(bf16[4,48,1280]{2,1,0:T(8,128)(2,1)S(1)} %pad_maximum_fusion.8), channel_id=1, source_target_pairs={{0,4},{1,5},{2,6},{3,7},{4,0},{5,1},{6,2},{7,3},{8,12},{9,13},{10,... | collective-permute-start | bytes 1474568 | tf_op jit(solution)/shard_map/ppermute | solution.py:36
  54.3 15.5 %collective-permute-start.16 = (bf16[2,192,384]{2,1,0:T(8,128)(2,1)}, bf16[2,192,384]{2,1,0:T(8,128)(2,1)S(1)}, u32[]{:S(2)}, u32[]{:S(2)}) collective-permute-start(bf16[2,192,384]{2,1,0:T(8,128)(2,1)} %maximum_select_fusion.2), channel_id=1, source_target_pairs={{0,16},{1,17},{2,18},{3,19},{4,20},{5,21},{6,22},{7,23},{8,24},{9,... | collective-permute-start | bytes 884744 | tf_op jit(solution)/shard_map/ppermute | solution.py:36
  71.0 21.4 %collective-permute-start.17 = (bf16[8,48,1280]{2,1,0:T(8,128)(2,1)S(1)}, bf16[8,48,1280]{2,1,0:T(8,128)(2,1)}, u32[]{:S(2)}, u32[]{:S(2)}) collective-permute-start(bf16[8,48,1280]{2,1,0:T(8,128)(2,1)S(1)} %pad_maximum_fusion.2.refs_2_.refs_5_), channel_id=1, source_target_pairs={{0,2},{1,3},{2,0},{3,1},{4,6},{5,7},{6,4},{7,5},{8,10},{9,11},{10,... | collective-permute-start | bytes 2949128 | tf_op jit(solution)/shard_map/ppermute | solution.py:36
  72.1 21.1 %collective-permute-start.18 = (bf16[8,48,1280]{2,1,0:T(8,128)(2,1)S(1)}, bf16[8,48,1280]{2,1,0:T(8,128)(2,1)}, u32[]{:S(2)}, u32[]{:S(2)}) collective-permute-start(bf16[8,48,1280]{2,1,0:T(8,128)(2,1)S(1)} %pad_maximum_fusion.3.refs_6_.refs_9_), channel_id=1, source_target_pairs={{0,4},{1,5},{2,6},{3,7},{4,0},{5,1},{6,2},{7,3},{8,12},{9,13},{10,... | collective-permute-start | bytes 2949128 | tf_op jit(solution)/shard_map/ppermute | solution.py:36
  72.4 20.0 %collective-permute-start.20 = (bf16[2,2,192,384]{3,2,1,0:T(8,128)(2,1)S(1)}, bf16[2,2,192,384]{3,2,1,0:T(8,128)(2,1)S(1)}, u32[]{:S(2)}, u32[]{:S(2)}) collective-permute-start(bf16[2,2,192,384]{3,2,1,0:T(8,128)(2,1)S(1)} %maximum_select_fusion.1), channel_id=1, source_target_pairs={{0,8},{1,9},{2,10},{3,11},{4,12},{5,13},{6,14},{7,15},{8,0},{9,1},... | collective-permute-start | bytes 1769480 | tf_op jit(solution)/shard_map/ppermute | solution.py:36
  73.3 19.1 %collective-permute-start.19 = (bf16[8,48,512]{2,1,0:T(8,128)(2,1)S(1)}, bf16[8,48,512]{2,1,0:T(8,128)(2,1)S(1)}, u32[]{:S(2)}, u32[]{:S(2)}) collective-permute-start(bf16[8,48,512]{2,1,0:T(8,128)(2,1)S(1)} %pad_maximum_fusion.10.refs_10_.refs_13_), channel_id=1, source_target_pairs={{0,8},{1,9},{2,10},{3,11},{4,12},{5,13},{6,14},{7,15},{8,0},{9,1},... | collective-permute-start | bytes 1179656 | tf_op jit(solution)/shard_map/ppermute | solution.py:36
  93.3 8.9 %collective-permute-start.21 = (bf16[8,48,1280]{2,1,0:T(8,128)(2,1)S(1)}, bf16[8,48,1280]{2,1,0:T(8,128)(2,1)S(1)}, u32[]{:S(2)}, u32[]{:S(2)}) collective-permute-start(bf16[8,48,1280]{2,1,0:T(8,128)(2,1)S(1)} %pad_maximum_fusion.2.refs_2_.refs_5_), channel_id=1, source_target_pairs={{0,1},{1,0},{2,3},{3,2},{4,5},{5,4},{6,7},{7,6},{8,9},{9,8},{10,11... | collective-permute-start | bytes 2949128 | tf_op jit(solution)/shard_map/ppermute | solution.py:36
  93.4 8.8 %collective-permute-start.22 = (bf16[8,48,1280]{2,1,0:T(8,128)(2,1)}, bf16[8,48,1280]{2,1,0:T(8,128)(2,1)S(1)}, u32[]{:S(2)}, u32[]{:S(2)}) collective-permute-start(bf16[8,48,1280]{2,1,0:T(8,128)(2,1)} %collective-permute-done.17.refs_3_.refs_6_), channel_id=1, source_target_pairs={{0,1},{1,0},{2,3},{3,2},{4,5},{5,4},{6,7},{7,6},{8,9},{9,8},{10,11... | collective-permute-start | bytes 2949128 | tf_op jit(solution)/shard_map/ppermute | solution.py:36
  102.3 17.0 %collective-permute-start.28 = (bf16[4,48,768]{2,1,0:T(8,128)(2,1)}, bf16[4,48,768]{2,1,0:T(8,128)(2,1)S(1)}, u32[]{:S(2)}, u32[]{:S(2)}) collective-permute-start(bf16[4,48,768]{2,1,0:T(8,128)(2,1)} %get-tuple-element.273), channel_id=1, source_target_pairs={{0,2},{1,3},{2,0},{3,1},{4,6},{5,7},{6,4},{7,5},{8,10},{9,11},{10,... | collective-permute-start | bytes 884744 | tf_op jit(solution)/shard_map/ppermute | solution.py:36
  103.9 16.6 %collective-permute-start.27 = (bf16[4,48,768]{2,1,0:T(8,128)(2,1)}, bf16[4,48,768]{2,1,0:T(8,128)(2,1)S(1)}, u32[]{:S(2)}, u32[]{:S(2)}) collective-permute-start(bf16[4,48,768]{2,1,0:T(8,128)(2,1)} %get-tuple-element.272), channel_id=1, source_target_pairs={{0,8},{1,9},{2,10},{3,11},{4,12},{5,13},{6,14},{7,15},{8,0},{9,1},... | collective-permute-start | bytes 884744 | tf_op jit(solution)/shard_map/ppermute | solution.py:36
  105.7 15.8 %collective-permute-start.29 = (bf16[64,384]{1,0:T(8,128)(2,1)}, bf16[64,384]{1,0:T(8,128)(2,1)S(1)}, u32[]{:S(2)}, u32[]{:S(2)}) collective-permute-start(bf16[64,384]{1,0:T(8,128)(2,1)} %get-tuple-element.290), channel_id=1, source_target_pairs={{0,1},{1,0},{2,3},{3,2},{4,5},{5,4},{6,7},{7,6},{8,9},{9,8},{10,11... | collective-permute-start | bytes 147464 | tf_op jit(solution)/shard_map/ppermute | solution.py:36
  105.8 15.7 %collective-permute-start.30 = (bf16[64,384]{1,0:T(8,128)(2,1)}, bf16[64,384]{1,0:T(8,128)(2,1)S(1)}, u32[]{:S(2)}, u32[]{:S(2)}) collective-permute-start(bf16[64,384]{1,0:T(8,128)(2,1)} %get-tuple-element.291), channel_id=1, source_target_pairs={{0,2},{1,3},{2,0},{3,1},{4,6},{5,7},{6,4},{7,5},{8,10},{9,11},{10,... | collective-permute-start | bytes 147464 | tf_op jit(solution)/shard_map/ppermute | solution.py:36
  107.0 14.5 %collective-permute-start.31 = (bf16[64,384]{1,0:T(8,128)(2,1)}, bf16[64,384]{1,0:T(8,128)(2,1)S(1)}, u32[]{:S(2)}, u32[]{:S(2)}) collective-permute-start(bf16[64,384]{1,0:T(8,128)(2,1)} %get-tuple-element.292), channel_id=1, source_target_pairs={{0,3},{1,2},{2,1},{3,0},{4,7},{5,6},{6,5},{7,4},{8,11},{9,10},{10,... | collective-permute-start | bytes 147464 | tf_op jit(solution)/shard_map/ppermute | solution.py:36
  121.5 17.8 %collective-permute-start.32 = (bf16[8,48,768]{2,1,0:T(8,128)(2,1)S(1)}, bf16[8,48,768]{2,1,0:T(8,128)(2,1)S(1)}, u32[]{:S(2)}, u32[]{:S(2)}) collective-permute-start(bf16[8,48,768]{2,1,0:T(8,128)(2,1)S(1)} %pad_maximum_fusion.6), channel_id=1, source_target_pairs={{0,2},{1,3},{2,0},{3,1},{4,6},{5,7},{6,4},{7,5},{8,10},{9,11},{10,... | collective-permute-start | bytes 1769480 | tf_op jit(solution)/shard_map/ppermute | solution.py:36
  122.7 20.9 %collective-permute-start.33 = (bf16[8,48,768]{2,1,0:T(8,128)(2,1)S(1)}, bf16[8,48,768]{2,1,0:T(8,128)(2,1)S(1)}, u32[]{:S(2)}, u32[]{:S(2)}) collective-permute-start(bf16[8,48,768]{2,1,0:T(8,128)(2,1)S(1)} %pad_maximum_fusion.7), channel_id=1, source_target_pairs={{0,8},{1,9},{2,10},{3,11},{4,12},{5,13},{6,14},{7,15},{8,0},{9,1},... | collective-permute-start | bytes 1769480 | tf_op jit(solution)/shard_map/ppermute | solution.py:36
  143.7 18.4 %collective-permute-start.38 = (bf16[16,48,768]{2,1,0:T(8,128)(2,1)S(1)}, bf16[16,48,768]{2,1,0:T(8,128)(2,1)}, u32[]{:S(2)}, u32[]{:S(2)}) collective-permute-start(bf16[16,48,768]{2,1,0:T(8,128)(2,1)S(1)} %constant_dynamic-update-slice_fusion.2.refs_10_), channel_id=1, source_target_pairs={{0,1},{1,0},{2,3},{3,2},{4,5},{5,4},{6,7},{7,6},{8,9},{9,8},{10,11... | collective-permute-start | bytes 3538952 | tf_op jit(solution)/shard_map/ppermute | solution.py:36
  143.9 18.2 %collective-permute-start.37 = (bf16[16,48,768]{2,1,0:T(8,128)(2,1)S(1)}, bf16[16,48,768]{2,1,0:T(8,128)(2,1)}, u32[]{:S(2)}, u32[]{:S(2)}) collective-permute-start(bf16[16,48,768]{2,1,0:T(8,128)(2,1)S(1)} %constant_dynamic-update-slice_fusion.refs_8_), channel_id=1, source_target_pairs={{0,1},{1,0},{2,3},{3,2},{4,5},{5,4},{6,7},{7,6},{8,9},{9,8},{10,11... | collective-permute-start | bytes 3538952 | tf_op jit(solution)/shard_map/ppermute | solution.py:36
  144.7 30.3 %all-to-all-start = ((bf16[32,48,192]{2,1,0:T(8,128)(2,1)}), bf16[32,48,192]{2,1,0:T(8,128)(2,1)}, u32[]{:S(2)}, u32[]{:S(2)}) async-start(bf16[32,48,192]{2,1,0:T(8,128)(2,1)} %bitcast.114), calls=%async_computation | async-start | bytes 1572864 | tf_op jit(solution)/shard_map/all_to_all | solution.py:666
  148.6 238.0 %all-gather.4.cloned.1.call-start = ((), (), s32[]{:S(2)}) async-start(), calls=%async_computation.2 | async-start | bytes 4866048 | tf_op jit(solution)/shard_map/all_gather | solution.py:936
  174.9 11.5 %collective-permute-start.44 = (bf16[192,1536]{1,0:T(8,128)(2,1)S(1)}, bf16[192,1536]{1,0:T(8,128)(2,1)}, u32[]{:S(2)}, u32[]{:S(2)}) collective-permute-start(bf16[192,1536]{1,0:T(8,128)(2,1)S(1)} %copy-done.39), channel_id=1, source_target_pairs={{0,1},{1,0},{2,3},{3,2},{4,5},{5,4},{6,7},{7,6},{8,9},{9,8},{10,11... | collective-permute-start | bytes 1769480 | tf_op jit(solution)/shard_map/ppermute | solution.py:36
  177.2 10.4 %collective-permute-start.43 = (bf16[1536,192]{0,1:T(8,128)(2,1)}, bf16[1536,192]{0,1:T(8,128)(2,1)}, u32[]{:S(2)}, u32[]{:S(2)}) collective-permute-start(bf16[1536,192]{0,1:T(8,128)(2,1)} %copy.38), channel_id=1, source_target_pairs={{0,1},{1,0},{2,3},{3,2},{4,5},{5,4},{6,7},{7,6},{8,9},{9,8},{10,11... | collective-permute-start | bytes 1769480 | tf_op jit(solution)/shard_map/ppermute | solution.py:36
  184.6 9.4 %collective-permute-start.42 = (bf16[8,16,1536]{2,1,0:T(8,128)(2,1)S(1)}, bf16[8,16,1536]{2,1,0:T(8,128)(2,1)}, u32[]{:S(2)}, u32[]{:S(2)}) collective-permute-start(bf16[8,16,1536]{2,1,0:T(8,128)(2,1)S(1)} %pad_maximum_fusion.11.refs_1_), channel_id=1, source_target_pairs={{0,2},{1,3},{2,0},{3,1},{4,6},{5,7},{6,4},{7,5},{8,10},{9,11},{10,... | collective-permute-start | bytes 1179656 | tf_op jit(solution)/shard_map/ppermute | solution.py:36
  238.5 8.9 %collective-permute-start.50 = (bf16[2,16,1536]{2,1,0:T(8,128)(2,1)}, bf16[2,16,1536]{2,1,0:T(8,128)(2,1)S(1)}, u32[]{:S(2)}, u32[]{:S(2)}) collective-permute-start(bf16[2,16,1536]{2,1,0:T(8,128)(2,1)} %get-tuple-element.344), channel_id=1, source_target_pairs={{0,8},{1,9},{2,10},{3,11},{4,12},{5,13},{6,14},{7,15},{8,0},{9,1},... | collective-permute-start | bytes 294920 | tf_op jit(solution)/shard_map/ppermute | solution.py:36
  249.7 14.1 %collective-permute-start.55 = (bf16[1,16,1536]{2,1,0:T(8,128)(2,1)}, bf16[1,16,1536]{2,1,0:T(8,128)(2,1)S(1)}, u32[]{:S(2)}, u32[]{:S(2)}) collective-permute-start(bf16[1,16,1536]{2,1,0:T(8,128)(2,1)} %get-tuple-element.352), channel_id=1, source_target_pairs={{0,16},{1,17},{2,18},{3,19},{4,20},{5,21},{6,22},{7,23},{8,24},{9,... | collective-permute-start | bytes 147464 | tf_op jit(solution)/shard_map/ppermute | solution.py:36
  278.9 21.2 %collective-permute-start.56 = (bf16[1536,192]{0,1:T(8,128)(2,1)S(1)}, bf16[1536,192]{0,1:T(8,128)(2,1)}, u32[]{:S(2)}, u32[]{:S(2)}) collective-permute-start(bf16[1536,192]{0,1:T(8,128)(2,1)S(1)} %copy.40), channel_id=1, source_target_pairs={{0,1},{1,0},{2,3},{3,2},{4,5},{5,4},{6,7},{7,6},{8,9},{9,8},{10,11... | collective-permute-start | bytes 1769480 | tf_op jit(solution)/shard_map/ppermute | solution.py:36
  296.3 31.6 %collective-permute-start.65 = (bf16[8,48,1280]{2,1,0:T(8,128)(2,1)}, bf16[8,48,1280]{2,1,0:T(8,128)(2,1)S(1)}, u32[]{:S(2)}, u32[]{:S(2)}) collective-permute-start(bf16[8,48,1280]{2,1,0:T(8,128)(2,1)} %get-tuple-element.374), channel_id=1, source_target_pairs={{0,2},{1,3},{2,0},{3,1},{4,6},{5,7},{6,4},{7,5},{8,10},{9,11},{10,... | collective-permute-start | bytes 2949128 | tf_op jit(solution)/shard_map/ppermute | solution.py:36
  297.6 38.3 %collective-permute-start.66 = (bf16[8,48,1280]{2,1,0:T(8,128)(2,1)}, bf16[8,48,1280]{2,1,0:T(8,128)(2,1)S(1)}, u32[]{:S(2)}, u32[]{:S(2)}) collective-permute-start(bf16[8,48,1280]{2,1,0:T(8,128)(2,1)} %get-tuple-element.386), channel_id=1, source_target_pairs={{0,4},{1,5},{2,6},{3,7},{4,0},{5,1},{6,2},{7,3},{8,12},{9,13},{10,... | collective-permute-start | bytes 2949128 | tf_op jit(solution)/shard_map/ppermute | solution.py:36
  299.3 61.6 %collective-permute-start.83 = (bf16[192,1536]{1,0:T(8,128)(2,1)}, bf16[192,1536]{1,0:T(8,128)(2,1)}, u32[]{:S(2)}, u32[]{:S(2)}) collective-permute-start(bf16[192,1536]{1,0:T(8,128)(2,1)} %get-tuple-element.430), channel_id=1, source_target_pairs={{0,1},{1,0},{2,3},{3,2},{4,5},{5,4},{6,7},{7,6},{8,9},{9,8},{10,11... | collective-permute-start | bytes 1769480 | tf_op jit(solution)/shard_map/ppermute | solution.py:36
  300.1 22.3 %collective-permute-start.67 = (bf16[8,48,512]{2,1,0:T(8,128)(2,1)}, bf16[8,48,512]{2,1,0:T(8,128)(2,1)S(1)}, u32[]{:S(2)}, u32[]{:S(2)}) collective-permute-start(bf16[8,48,512]{2,1,0:T(8,128)(2,1)} %get-tuple-element.388), channel_id=1, source_target_pairs={{0,8},{1,9},{2,10},{3,11},{4,12},{5,13},{6,14},{7,15},{8,0},{9,1},... | collective-permute-start | bytes 1179656 | tf_op jit(solution)/shard_map/ppermute | solution.py:36
  303.6 61.7 %all-to-all-start.1 = ((bf16[32,48,192]{2,1,0:T(8,128)(2,1)}), bf16[32,48,192]{2,1,0:T(8,128)(2,1)S(1)}, u32[]{:S(2)}, u32[]{:S(2)}) async-start(bf16[32,48,192]{2,1,0:T(8,128)(2,1)} %bitcast.51), calls=%async_computation.1 | async-start | bytes 1572864 | tf_op jit(solution)/shard_map/all_to_all | solution.py:934
  340.8 12.1 %collective-permute-start.69 = (bf16[4,48,1280]{2,1,0:T(8,128)(2,1)}, bf16[4,48,1280]{2,1,0:T(8,128)(2,1)S(1)}, u32[]{:S(2)}, u32[]{:S(2)}) collective-permute-start(bf16[4,48,1280]{2,1,0:T(8,128)(2,1)} %get-tuple-element.392), channel_id=1, source_target_pairs={{0,4},{1,5},{2,6},{3,7},{4,0},{5,1},{6,2},{7,3},{8,12},{9,13},{10,... | collective-permute-start | bytes 1474568 | tf_op jit(solution)/shard_map/ppermute | solution.py:36
  341.5 14.9 %collective-permute-start.70 = (bf16[4,48,1280]{2,1,0:T(8,128)(2,1)}, bf16[4,48,1280]{2,1,0:T(8,128)(2,1)S(1)}, u32[]{:S(2)}, u32[]{:S(2)}) collective-permute-start(bf16[4,48,1280]{2,1,0:T(8,128)(2,1)} %get-tuple-element.396), channel_id=1, source_target_pairs={{0,8},{1,9},{2,10},{3,11},{4,12},{5,13},{6,14},{7,15},{8,0},{9,1},... | collective-permute-start | bytes 1474568 | tf_op jit(solution)/shard_map/ppermute | solution.py:36
  362.2 11.3 %collective-permute-start.72 = (f32[16,1536]{1,0:T(8,128)S(1)}, f32[16,1536]{1,0:T(8,128)S(1)}, u32[]{:S(2)}, u32[]{:S(2)}) collective-permute-start(f32[16,1536]{1,0:T(8,128)S(1)} %add.181), channel_id=1, source_target_pairs={{0,4},{1,5},{2,6},{3,7},{4,0},{5,1},{6,2},{7,3},{8,12},{9,13},{10,... | collective-permute-start | bytes 294920 | tf_op jit(solution)/shard_map/ppermute | solution.py:36
  373.5 11.8 %collective-permute-start.80 = (bf16[1,48,1280]{2,1,0:T(8,128)(2,1)S(1)}, bf16[1,48,1280]{2,1,0:T(8,128)(2,1)S(1)}, u32[]{:S(2)}, u32[]{:S(2)}) collective-permute-start(bf16[1,48,1280]{2,1,0:T(8,128)(2,1)S(1)} %copy-done.75), channel_id=1, source_target_pairs={{0,16},{1,17},{2,18},{3,19},{4,20},{5,21},{6,22},{7,23},{8,24},{9,... | collective-permute-start | bytes 368648 | tf_op jit(solution)/shard_map/ppermute | solution.py:36
  376.3 9.4 %collective-permute-start.81 = (bf16[1,48,1280]{2,1,0:T(8,128)(2,1)S(1)}, bf16[1,48,1280]{2,1,0:T(8,128)(2,1)S(1)}, u32[]{:S(2)}, u32[]{:S(2)}) collective-permute-start(bf16[1,48,1280]{2,1,0:T(8,128)(2,1)S(1)} %copy-done.74), channel_id=1, source_target_pairs={{0,16},{1,17},{2,18},{3,19},{4,20},{5,21},{6,22},{7,23},{8,24},{9,... | collective-permute-start | bytes 368648 | tf_op jit(solution)/shard_map/ppermute | solution.py:36
  382.2 9.8 %collective-permute-start.77 = (f32[16,1536]{1,0:T(8,128)S(1)}, f32[16,1536]{1,0:T(8,128)S(1)}, u32[]{:S(2)}, u32[]{:S(2)}) collective-permute-start(f32[16,1536]{1,0:T(8,128)S(1)} %add.183), channel_id=1, source_target_pairs={{0,16},{1,17},{2,18},{3,19},{4,20},{5,21},{6,22},{7,23},{8,24},{9,... | collective-permute-start | bytes 294920 | tf_op jit(solution)/shard_map/ppermute | solution.py:36
  (118 other events, 829.2 us)
Sparse Core Ops, SparseCore 0:
  93.4 60.7 all-gather.5
  278.7 75.9 all-gather.3
